TPU v7x, 256 devices: a whole 4x4x8 slice. The times are simulated.
256 devices in a mesh: lat: 16 (over z, x_lo), lon: 16 (over x_hi, y, core).
Axes of the slice: x: 4 (x_hi: 2, x_lo: 2; x = x_hi * 2 + x_lo), y: 4, z: 8, core: 2. Of those that a mesh axis runs over, the one named last changes fastest.
Arguments:
- tokens: bfloat16 [2, 384, 384, 512], P(None, 'lat', 'lon'), may hold values from -6 to 6
- norm_gain: float32 [512], replicated, may hold values from 0.25 to 1.75
- qkv_weight: bfloat16 [512, 1536], replicated, may hold values from -0.25 to 0.25
- out_weight: bfloat16 [512, 512], replicated, may hold values from -0.25 to 0.25
- bias_table: float32 [759, 8], replicated, may hold values from -4 to 320
- bias_index: int32 [144, 144], replicated, may hold values from 0 to 758
- cotangent: bfloat16 [2, 384, 384, 512], P(None, 'lat', 'lon'), may hold values from -6 to 6
Outputs:
- grad_tokens: bfloat16 [2, 384, 384, 512], P(None, 'lat', 'lon')
- grad_qkv: float32 [512, 1536], replicated
- grad_out: float32 [512, 512], replicated
- grad_bias: float32 [759, 8], replicated
- grad_gain: float32 [512], replicated
All inputs are finite; a program needn't handle non-finite values.
Results may differ from a plain program's by a relative error of at most 0.015.
Values may be sent and summed in bfloat16 or wider, within the bound.
No kernel may reach another device: no remote copies, remote signals or barrier semaphores. Data moves between devices by JAX's collectives and lax.ppermute only.
A program may use at most 128 MiB of HBM per device.

v0:
```python
import jax
import jax.numpy as jnp
from jax import lax
from jax.experimental import pallas as pl
from jax.experimental.pallas import tpu as pltpu
from jax.sharding import PartitionSpec as P

WH = 6
WW = 12
SH = 3
SW = 6
F32 = jnp.float32
BF16 = jnp.bfloat16
MIB = 1024 * 1024

LAST, CORE, X, Y = range(4)

NT = (((1,), (1,)), ((), ()))


def dot(a, b):
    return jnp.dot(a, b, preferred_element_type=F32)


def dot_nt(a, b):
    return lax.dot_general(a, b, NT, preferred_element_type=F32)


class Geometry:
    def __init__(self, depth, rows, cols):
        self.depth, self.rows, self.cols = depth, rows, cols
        self.cells = depth * rows * cols
        self.win = depth * WH * WW
        self.nwin = self.cells // self.win
        self.wins_lon = cols // WW
        self.wins_lat = rows // WH
        self.n_rows = depth * SH * (cols - SW)
        self.n_cols = depth * (rows - SH) * SW
        self.n_corner = depth * SH * SW

    def local(self, z, r, c):
        return (z * self.rows + r) * self.cols + c

    def rim_row(self, z, r):
        return (z * SH + r) * (self.cols - SW)

    def rim_col(self, z, r):
        return (z * (self.rows - SH) + r) * SW

    def corner(self, z, r):
        return (z * SH + r) * SW

    def cell(self, z, r, c):
        window = (r // WH) * self.wins_lon + c // WW
        return window * self.win + (z * WH + r % WH) * WW + c % WW


def pad16(n):
    return (n + 15) // 16 * 16


def forward_pieces(geo, z, r):
    own = geo.cols - SW
    if r < geo.rows - SH:
        first = ("local", geo.local(z, r + SH, SW), 0, own)
        second = ("cols", geo.rim_col(z, r), own, SW)
    else:
        first = ("rows", geo.rim_row(z, r - geo.rows + SH), 0, own)
        second = ("corner", geo.corner(z, r - geo.rows + SH), own, SW)
    return (first, second)


def window_cuts(start, length):
    at = start
    while at < start + length:
        stop = min(start + length, (at // WW + 1) * WW)
        yield at, stop - at
        at = stop


def pack_kernel(geo, tok_ref, cot_ref, rows_ref, cols_ref, corner_ref, top, left, wide, slim, buf, sems):
    n_rows, n_cols, n_corner = geo.n_rows, geo.n_cols, geo.n_corner
    base_cols = pad16(2 * n_rows)
    base_corner = base_cols + pad16(2 * n_cols)
    own = geo.cols - SW
    copies = []
    for which, ref in enumerate((tok_ref, cot_ref)):
        for part, (src, dst) in enumerate(
            (
                (ref.at[:, 0:SH], top.at[which]),
                (ref.at[:, SH : geo.rows, 0:16], left.at[which]),
            )
        ):
            copy = pltpu.make_async_copy(src, dst, sems.at[which, part])
            copy.start()
            copies.append(copy)
    buf[base_cols - 16 : base_cols] = jnp.zeros((16, buf.shape[1]), F32)
    buf[base_corner - 16 : base_corner] = jnp.zeros((16, buf.shape[1]), F32)
    buf[-16:] = jnp.zeros((16, buf.shape[1]), F32)
    for copy in copies:
        copy.wait()
    wide[...] = top[...].astype(F32)
    slim[...] = left[...].astype(F32)
    for which in range(2):
        for z in range(geo.depth):
            for r in range(SH):
                at = which * n_rows + geo.rim_row(z, r)
                buf[at : at + own] = wide[which, z, r, SW:]
                at = base_corner + which * n_corner + geo.corner(z, r)
                buf[at : at + SW] = wide[which, z, r, 0:SW]
            for r in range(geo.rows - SH):
                at = base_cols + which * n_cols + geo.rim_col(z, r)
                buf[at : at + SW] = slim[which, z, r, 0:SW]
    rows_ref[...] = buf[0:base_cols].astype(BF16)
    cols_ref[...] = buf[base_cols:base_corner].astype(BF16)
    corner_ref[...] = buf[base_corner : base_corner + pad16(2 * n_corner)].astype(BF16)


BANDS = 8
SPAN = 96


def band_of(index):
    band = (index * 683) >> 16
    return band, index - band * SPAN


def lookup_kernel(heads, raw_ref, table_ref, bias_ref, idx_ref, split):
    win = idx_ref.shape[0]
    rows = heads * BANDS
    entries = table_ref.shape[1]
    idx_ref[...] = raw_ref[...].T
    split[...] = jnp.zeros_like(split)
    rest = table_ref[...]
    for part in range(3):
        low = rest.astype(BF16).astype(F32)
        for band in range(BANDS):
            at = part * rows + band * heads
            stop = min(entries, (band + 1) * SPAN)
            split[at : at + heads, 0 : stop - band * SPAN] = low[:, band * SPAN : stop]
        rest = rest - low
    table = split[...].astype(BF16)
    iota = lax.broadcasted_iota(jnp.int32, (SPAN, win), 0)

    def step(block, carry):
        start = pl.multiple_of(block * 8, 8)
        band, place = band_of(idx_ref[pl.ds(start, 8), :])
        for j in range(8):
            onehot = jnp.where(iota == place[j : j + 1, :], 1.0, 0.0).astype(BF16)
            found = dot(table, onehot)
            found = (found[:rows] + found[rows : 2 * rows]) + found[2 * rows :]
            mine = jnp.broadcast_to(band[j : j + 1, :], (heads, win))
            total = jnp.zeros((heads, win), F32)
            for b in range(BANDS):
                total = jnp.where(mine == b, found[b * heads : (b + 1) * heads], total)
            for h in range(heads):
                bias_ref[h, pl.ds(start + j, 1), :] = total[h : h + 1]
        return carry

    lax.fori_loop(0, win // 8, step, 0)


def table_kernel(heads, idx_ref, sum_ref, gsum_ref, gain_ref, out_ref, acc, line):
    win = idx_ref.shape[0]
    rows = heads * BANDS
    iota = lax.broadcasted_iota(jnp.int32, (SPAN, win), 0)
    bands = lax.broadcasted_iota(jnp.int32, (BANDS, win), 0)
    acc[...] = jnp.zeros_like(acc)

    def step(block, carry):
        start = pl.multiple_of(block * 8, 8)
        band, place = band_of(idx_ref[pl.ds(start, 8), :])
        tops, rests = [], []
        for h in range(heads):
            slab = sum_ref[h, pl.ds(start, 8), :]
            top = slab.astype(BF16).astype(F32)
            tops.append(top)
            rests.append(slab - top)
        total = None
        for j in range(8):
            onehot = jnp.where(iota == place[j : j + 1, :], 1.0, 0.0).astype(BF16)
            keep = jnp.where(bands == band[j : j + 1, :], 1.0, 0.0)
            spread = [p[h][j : j + 1, :] * keep for p in (tops, rests) for h in range(heads)]
            term = dot_nt(jnp.concatenate(spread, axis=0).astype(BF16), onehot)
            total = term if total is None else total + term
        acc[...] += total[:rows] + total[rows:]
        return carry

    lax.fori_loop(0, win // 8, step, 0)
    for h in range(heads):
        for b in range(BANDS):
            line[h : h + 1, b * SPAN : (b + 1) * SPAN] = acc[h * BANDS + b : h * BANDS + b + 1, :]
    width = out_ref.shape[1]
    more = BANDS * SPAN - width
    gain = jnp.sum(gsum_ref[...].T, axis=0, keepdims=True) / gain_ref[...]
    out_ref[0:heads, :] = line[:, :width]
    out_ref[heads:, 0:more] = line[:, width:]
    out_ref[heads:, more:] = jnp.zeros((16 - heads, width - more), F32)
    out_ref[heads : heads + 1, more:] = gain[:, : width - more]
    out_ref[heads + 1 : heads + 2, more:] = gain[:, width - more :]


def main_kernel(
    geo, heads, info_ref, tok_ref, cot_ref, rows_ref, cols_ref, corner_ref, gain_ref, wqkv_hbm,
    wout_hbm, bias_ref,
    send_ref, keep_ref, bsum_ref, dproj, ftok, inv, cotb, gsum_ref,
    loc, rim_rows, rim_cols, rim_corner, fcot, normed, proj, gatt, att_t, dq_t,
    bias2, normed_t, gout, grads, wqkv_ref, wout_ref, sems,
):
    copies = [
        pltpu.make_async_copy(wqkv_hbm, wqkv_ref, sems.at[0]),
        pltpu.make_async_copy(wout_hbm, wout_ref, sems.at[1]),
    ]
    for copy in copies:
        copy.start()
    width = ftok.shape[1]
    win = geo.win
    head_size = width // heads
    scale = head_size ** (-0.5)

    for which, (ref, dst) in enumerate(((tok_ref, ftok), (cot_ref, fcot))):
        loc[...] = ref[...].astype(F32)
        if which == 0:
            rim_rows[...] = rows_ref[...].astype(F32)
            rim_cols[...] = cols_ref[...].astype(F32)
            rim_corner[...] = corner_ref[...].astype(F32)
        sources = {
            "local": (loc, 0),
            "rows": (rim_rows, which * geo.n_rows),
            "cols": (rim_cols, which * geo.n_cols),
            "corner": (rim_corner, which * geo.n_corner),
        }
        for z in range(geo.depth):
            for r in range(geo.rows):
                for name, first, column, length in forward_pieces(geo, z, r):
                    src, base = sources[name]
                    for at, count in window_cuts(column, length):
                        begin = base + first + at - column
                        cell = geo.cell(z, r, at)
                        dst[cell : cell + count] = src[begin : begin + count]

    gain = gain_ref[...]

    spot = lax.broadcasted_iota(jnp.int32, (win, win), 0)
    other = lax.broadcasted_iota(jnp.int32, (win, win), 1)
    half = WH * WW
    polar_a = jnp.where(spot >= half, spot - half, spot) >= (WH - SH) * WW
    polar_b = jnp.where(other >= half, other - half, other) >= (WH - SH) * WW
    flag_a = jnp.where(polar_a, 1.0, 0.0)
    flag_b = jnp.where(polar_b, 1.0, 0.0)
    mask = jnp.where(flag_a == flag_b, 0.0, -1e30)
    for h in range(heads):
        plain = bias_ref[h]
        bias2[0, h] = plain
        bias2[1, h] = plain + mask
        bsum_ref[h] = jnp.zeros((win, win), F32)
    gout[...] = jnp.zeros_like(gout)

    def norm_step(w, carry):
        at = pl.ds(pl.multiple_of(w * win, 16), win)
        x = ftok[at, :]
        centred = x - jnp.mean(x, axis=-1, keepdims=True)
        istd = lax.rsqrt(jnp.mean(centred * centred, axis=-1, keepdims=True) + 1e-05)
        unit = centred * istd
        ftok[at, :] = unit
        inv[at, :] = jnp.broadcast_to(istd, (win, 128))
        normed[at, :] = (unit * gain).astype(BF16)
        cotb[at, :] = fcot[at, :].astype(BF16)
        return carry

    lax.fori_loop(0, geo.nwin, norm_step, 0)
    for copy in copies:
        copy.wait()

    def proj_step(w, carry):
        at = pl.ds(pl.multiple_of(w * (2 * win), 16), 2 * win)
        x = normed[at, :]
        for part in range(3):
            cols = slice(part * width, (part + 1) * width)
            proj[at, cols] = dot(x, wqkv_ref[:, cols]).astype(BF16)
        gatt[at, :] = dot_nt(cotb[at, :], wout_ref[...]).astype(BF16)
        return carry

    lax.fori_loop(0, geo.nwin // 2, proj_step, 0)

    lane = lax.broadcasted_iota(jnp.int32, (win, 128), 1)
    lower = lane < head_size
    polar_from = geo.nwin - geo.wins_lon

    def attend(w, carry):
        at = pl.ds(pl.multiple_of(w * win, 16), win)
        sel = jnp.where(w >= polar_from, info_ref[LAST], 0)
        k_t = proj[at, width : 2 * width].T
        v_t = proj[at, 2 * width :].T
        for pair in range(heads // 2):
            cols = slice(pair * 128, (pair + 1) * 128)
            q = proj[at, cols] * BF16(scale)
            k = proj[at, width + pair * 128 : width + (pair + 1) * 128]
            v = proj[at, 2 * width + pair * 128 : 2 * width + (pair + 1) * 128]
            g = gatt[at, cols]
            dv = None
            dk = None
            for side in range(2):
                h = 2 * pair + side
                keep = lower if side == 0 else jnp.logical_not(lower)
                qm = jnp.where(keep, q, BF16(0))
                gm = jnp.where(keep, g, BF16(0))
                scores = dot_nt(k, qm) + bias2[sel, h]
                top = jnp.max(scores, axis=0, keepdims=True)
                grown = jnp.exp(scores - top)
                probs = grown * (1.0 / jnp.sum(grown, axis=0, keepdims=True))
                probs_low = probs.astype(BF16)
                gprobs = dot_nt(v, gm)
                weighted = jnp.sum(probs * gprobs, axis=0, keepdims=True)
                gscores = probs * (gprobs - weighted)
                bsum_ref[h] += gscores
                scores_low = gscores.astype(BF16)
                feats = slice(h * head_size, (h + 1) * head_size)
                att_t[feats, :] = dot(v_t[feats], probs_low).astype(BF16)
                dq_t[feats, :] = (dot(k_t[feats], scores_low) * scale).astype(BF16)
                dv_term = dot(probs_low, gm)
                dk_term = dot(scores_low, qm)
                dv = dv_term if dv is None else dv + dv_term
                dk = dk_term if dk is None else dk + dk_term
            dproj[at, width + pair * 128 : width + (pair + 1) * 128] = dk.astype(BF16)
            dproj[at, 2 * width + pair * 128 : 2 * width + (pair + 1) * 128] = dv.astype(BF16)
        dproj[at, 0:width] = dq_t[...].T
        gout[...] += dot(att_t[...], cotb[at, :])
        return carry

    lax.fori_loop(0, geo.nwin, attend, 0)

    grads[1, width:, :] = gout[...].astype(BF16)
    for block in range(geo.cells // 128):
        rows = slice(block * 128, (block + 1) * 128)
        normed_t[:, rows] = normed[rows, :].T

    gsum = jnp.zeros((width, 128), F32)
    for part in range(3):
        half, first = part // 2, part % 2 * width
        for sub in range(2):
            cols = slice(part * width + sub * 256, part * width + (sub + 1) * 256)
            term = dot(normed_t[...], dproj[:, cols])
            grads[half, first : first + width, sub * 256 : (sub + 1) * 256] = term.astype(BF16)
            term = term * wqkv_ref[:, cols].astype(F32)
            gsum = gsum + (term[:, :128] + term[:, 128:])
    gsum_ref[...] = gsum
    keep_ref[...] = grads[info_ref[CORE]]
    send_ref[...] = grads[1 - info_ref[CORE]]


def back_kernel(geo, first, count, dproj, unit_ref, inv, cotb, gain_ref, wqkv_ref, gtok_ref):
    win = geo.win
    gain = gain_ref[...]

    def back_step(w, carry):
        at = pl.ds(pl.multiple_of((first + w) * win, 16), win)
        gn = dot_nt(dproj[at, :], wqkv_ref[...]).astype(BF16).astype(F32)
        unit = unit_ref[at, :]
        hat = gn * gain
        centre = jnp.mean(hat, axis=-1, keepdims=True)
        slope = jnp.mean(hat * unit, axis=-1, keepdims=True)
        istd = inv[at, 0:1]
        cot = cotb[at, :].astype(F32)
        to = pl.ds(pl.multiple_of(w * win, 16), win)
        gtok_ref[to, :] = (cot + istd * (hat - centre - unit * slope)).astype(BF16)
        return carry

    lax.fori_loop(0, count, back_step, 0)


def unpack_send_kernel(geo, low_ref, high_ref, rows_ref, cols_ref, corner_ref, fg, buf):
    base_cols = pad16(geo.n_rows)
    base_corner = base_cols + pad16(geo.n_cols)
    half = low_ref.shape[0]
    fg[0:half] = low_ref[...].astype(F32)
    fg[half:] = high_ref[...].astype(F32)
    buf[...] = jnp.zeros_like(buf)
    bases = {"rows": 0, "cols": base_cols, "corner": base_corner}
    for z in range(geo.depth):
        for r in range(geo.rows):
            for name, first, column, length in forward_pieces(geo, z, r):
                if name == "local":
                    continue
                for at, count in window_cuts(column, length):
                    to = bases[name] + first + at - column
                    cell = geo.cell(z, r, at)
                    buf[to : to + count] = fg[cell : cell + count]
    rows_ref[...] = buf[0:base_cols].astype(BF16)
    cols_ref[...] = buf[base_cols:base_corner].astype(BF16)
    corner_ref[...] = buf[base_corner : base_corner + pad16(geo.n_corner)].astype(BF16)


def assemble_kernel(geo, low_ref, high_ref, rows_ref, cols_ref, corner_ref, out_ref, fg, rr, rc, rk, grid):
    half = low_ref.shape[0]
    fg[0:half] = low_ref[...].astype(F32)
    fg[half:] = high_ref[...].astype(F32)
    rr[...] = rows_ref[...].astype(F32)
    rc[...] = cols_ref[...].astype(F32)
    rk[...] = corner_ref[...].astype(F32)
    own = geo.cols - SW
    for z in range(geo.depth):
        for r in range(geo.rows):
            for name, first, column, length in forward_pieces(geo, z, r):
                if name != "local":
                    continue
                for at, count in window_cuts(column, length):
                    to = first + at - column
                    cell = geo.cell(z, r, at)
                    grid[to : to + count] = fg[cell : cell + count]
        for r in range(SH):
            to = geo.local(z, r, SW)
            grid[to : to + own] = rr[geo.rim_row(z, r) : geo.rim_row(z, r) + own]
            to = geo.local(z, r, 0)
            grid[to : to + SW] = rk[geo.corner(z, r) : geo.corner(z, r) + SW]
        for r in range(geo.rows - SH):
            to = geo.local(z, r + SH, 0)
            grid[to : to + SW] = rc[geo.rim_col(z, r) : geo.rim_col(z, r) + SW]
    out_ref[...] = grid[...].astype(BF16)


def call(kernel, out_shapes, scratch, n_in, limit, smem_first=False, cost=None):
    specs = [pl.BlockSpec(memory_space=pltpu.VMEM)] * n_in
    if smem_first:
        specs[0] = pl.BlockSpec(memory_space=pltpu.SMEM)
    return pl.pallas_call(
        kernel,
        out_shape=out_shapes,
        in_specs=specs,
        out_specs=jax.tree.map(lambda s: pl.BlockSpec(memory_space=pltpu.VMEM), out_shapes),
        scratch_shapes=scratch,
        compiler_params=pltpu.CompilerParams(vmem_limit_bytes=limit),
        cost_estimate=cost,
    )


def shape(dims, dtype):
    return jax.ShapeDtypeStruct(dims, dtype)


def moved(value, lat_step, lon_step):
    lats, lons = lax.axis_size("lat"), lax.axis_size("lon")
    pairs = []
    for a in range(lats):
        for o in range(lons):
            target = ((a - lat_step) % lats) * lons + (o - lon_step) % lons
            pairs.append((a * lons + o, target))
    return lax.ppermute(value, ("lat", "lon"), pairs)


class Chips:
    def __init__(self):
        self.lats, self.lons = lax.axis_size("lat"), lax.axis_size("lon")
        self.nz, self.nx, self.ny = self.lats // 2, 4, self.lons // 4

    def split(self, device):
        lat, lon = device // self.lons, device % self.lons
        x = lon // (2 * self.ny) * 2 + lat % 2
        return lat // 2, x, lon // 2 % self.ny, lon % 2

    def join(self, z, x, y, core):
        return (z * 2 + x % 2) * self.lons + (x // 2 * self.ny + y) * 2 + core

    def send(self, value, change):
        pairs = []
        for device in range(self.lats * self.lons):
            z, x, y, core = change(*self.split(device))
            pairs.append((device, self.join(z, x, y, core)))
        return lax.ppermute(value, ("lat", "lon"), pairs)

    def core(self, value):
        return self.send(value, lambda z, x, y, c: (z, x, y, 1 - c))

    def x(self, value, step):
        return self.send(value, lambda z, x, y, c: (z, (x + step) % self.nx, y, c))

    def y(self, value, step):
        return self.send(value, lambda z, x, y, c: (z, x, (y + step) % self.ny, c))

    def z(self, value, bit):
        return self.send(value, lambda z, x, y, c: (z ^ (2 * bit - 1), x, y, c))


def pair_sum_kernel(ny, nx, info_ref, keep_ref, recv_ref, *outs):
    rows = keep_ref.shape[0] // 2
    for base, count, place, refs in ((0, ny, Y, outs[:ny]), (rows, nx, X, outs[ny:])):
        piece = rows // count
        for k, ref in enumerate(refs):
            part = (info_ref[place] + k) & (count - 1)
            at = pl.ds(pl.multiple_of(base + part * piece, 16), piece)
            ref[...] = (keep_ref[at, :].astype(F32) + recv_ref[at, :].astype(F32)).astype(BF16)


def total_of(refs):
    total = refs[0][...].astype(F32)
    for ref in refs[1:]:
        total += ref[...].astype(F32)
    return total


def cross_sum_kernel(ny, nx, info_ref, *refs):
    ins_a, ins_b = refs[:ny], refs[ny : ny + nx]
    outs_a, outs_b = refs[ny + nx : ny + 2 * nx], refs[ny + 2 * nx : 2 * ny + 2 * nx]
    hold = refs[-1]
    for ins, outs, count, place in ((ins_a, outs_a, nx, X), (ins_b, outs_b, ny, Y)):
        hold[...] = total_of(ins)
        piece = hold.shape[0] // count
        for k, ref in enumerate(outs):
            part = (info_ref[place] + k) & (count - 1)
            at = pl.ds(pl.multiple_of(part * piece, 16), piece)
            ref[...] = hold[at, :].astype(BF16)


SMALL = 16


def put_small(ref, base, total):
    top = total.astype(BF16)
    ref[base : base + SMALL] = top
    ref[base + SMALL : base + 2 * SMALL] = (total - top.astype(F32)).astype(BF16)


def small_of(refs, base):
    total = None
    for ref in refs:
        for part in range(2):
            at = base + part * SMALL
            term = ref[at : at + SMALL].astype(F32)
            total = term if total is None else total + term
    return total


def join_sum_kernel(ny, nx, *refs):
    piece = refs[0].shape[0]
    small_ref, out_ref = refs[-2:]
    out_ref[0:piece] = total_of(refs[:nx]).astype(BF16)
    out_ref[piece : 2 * piece] = total_of(refs[nx : nx + ny]).astype(BF16)
    put_small(out_ref, 2 * piece, small_ref[...])


def z_sum_kernel(mine_ref, got_ref, *outs):
    rows = mine_ref.shape[0] - 2 * SMALL
    total = (mine_ref[0:rows].astype(F32) + got_ref[0:rows].astype(F32)).astype(BF16)
    last = small_of((mine_ref, got_ref), rows)
    if len(outs) == 1:
        outs[0][0:rows] = total
    else:
        outs[0][...] = total[: rows // 2]
        outs[1][0 : rows // 2] = total[rows // 2 :]
    put_small(outs[-1], outs[-1].shape[0] - 2 * SMALL, last)


def gather_kernel(ny, nx, info_ref, *refs):
    a_ref, b_ref = refs[-2:]
    ins_a, ins_b = refs[:nx], refs[nx : nx + ny]
    piece = ins_a[0].shape[0]
    for ins, out, count, place in ((ins_a, a_ref, nx, X), (ins_b, b_ref, ny, Y)):
        for k, ref in enumerate(ins):
            part = (info_ref[place] + (count - k)) & (count - 1)
            out[pl.ds(pl.multiple_of(part * piece, 16), piece), :] = ref[0:piece]
    put_small(b_ref, ny * piece, small_of(ins_b, piece))


def merge_kernel(count, place, with_small, info_ref, *refs):
    ins, outs = refs[:count], refs[count:]
    out_ref = outs[0]
    width = out_ref.shape[1]
    piece = out_ref.shape[0] // count
    for k, ref in enumerate(ins):
        part = (info_ref[place] + (count - k)) & (count - 1)
        out_ref[pl.ds(pl.multiple_of(part * piece, 16), piece), :] = ref[0:piece]
    if with_small:
        line_ref, gain_ref = outs[1:]
        total = small_of(ins, piece)
        more = line_ref.shape[1] - width
        line_ref[:, 0:width] = total[0:8]
        line_ref[:, width:] = total[8:, 0:more]
        gain_ref[:, 0 : width - more] = total[8:9, more:]
        gain_ref[:, width - more :] = total[9:10, more:]


def place_kernel(mine, info_ref, a_ref, b_ref, *refs):
    gqkv_ref, gout_ref, hold, sems = refs[-4:]
    width = gout_ref.shape[1]
    core = info_ref[CORE]
    half = core if mine else 1 - core
    steps = 4
    rows = width // steps

    def write(targets):
        copies = []
        for which, ref in enumerate((a_ref, b_ref)):
            for step in range(steps):
                at = slice(step * rows, (step + 1) * rows)
                hold[which, at] = ref[at].astype(F32)
                copy = pltpu.make_async_copy(
                    hold.at[which, at], targets[which].at[at], sems.at[which, step]
                )
                copy.start()
                copies.append(copy)
        for copy in copies:
            copy.wait()

    @pl.when(half == 0)
    def _():
        write((gqkv_ref.at[:, 0:width], gqkv_ref.at[:, width : 2 * width]))

    @pl.when(half == 1)
    def _():
        write((gqkv_ref.at[:, 2 * width :], gout_ref))


def per_device(tokens, norm_gain, qkv_weight, out_weight, bias_table, bias_index, cotangent):
    depth, rows_lat, cols_lon, width = tokens.shape
    entries, heads = bias_table.shape
    geo = Geometry(depth, rows_lat, cols_lon)
    win, cells = geo.win, geo.cells
    tok = tokens.reshape(cells, width)
    cot = cotangent.reshape(cells, width)

    n_rows, n_cols, n_corner = pad16(2 * geo.n_rows), pad16(2 * geo.n_cols), pad16(2 * geo.n_corner)
    rim = pl.pallas_call(
        lambda *refs: pack_kernel(geo, *refs),
        out_shape=[shape((n, width), BF16) for n in (n_rows, n_cols, n_corner)],
        in_specs=[pl.BlockSpec(memory_space=pl.ANY)] * 2,
        out_specs=[pl.BlockSpec(memory_space=pltpu.VMEM)] * 3,
        scratch_shapes=[
            pltpu.VMEM((2, depth, SH, cols_lon, width), BF16),
            pltpu.VMEM((2, depth, rows_lat - SH, 16, width), BF16),
            pltpu.VMEM((2, depth, SH, cols_lon, width), F32),
            pltpu.VMEM((2, depth, rows_lat - SH, 16, width), F32),
            pltpu.VMEM((n_rows + n_cols + n_corner, width), F32),
            pltpu.SemaphoreType.DMA((2, 2)),
        ],
        compiler_params=pltpu.CompilerParams(vmem_limit_bytes=60 * MIB),
    )(tokens, cotangent)
    rim = (moved(rim[0], 1, 0), moved(rim[1], 0, 1), moved(rim[2], 1, 1))

    bias, index_t = call(
        lambda *refs: lookup_kernel(heads, *refs),
        [shape((heads, win, win), F32), shape((win, win), jnp.int32)],
        [pltpu.VMEM((3 * heads * BANDS, SPAN), F32)],
        2,
        8 * MIB,
        cost=pl.CostEstimate(flops=4 * 10**9, bytes_accessed=10**6, transcendentals=0),
    )(bias_index, bias_table.T)

    chips = Chips()
    ny, nx = chips.ny, chips.nx
    lat, lon = lax.axis_index("lat"), lax.axis_index("lon")
    is_last = (lat == chips.lats - 1).astype(jnp.int32)
    info = jnp.stack([is_last, lon % 2, lon // (2 * ny) * 2 + lat % 2, lon // 2 % ny])
    half_rows = 2 * width
    big = 36 * MIB
    small_limit = 10 * MIB

    vmem, smem = pl.BlockSpec(memory_space=pltpu.VMEM), pl.BlockSpec(memory_space=pltpu.SMEM)
    hbm = pl.BlockSpec(memory_space=pl.ANY)
    send, keep, bias_sum, grad_proj, unit, inv, cot_win, gain_sum = pl.pallas_call(
        lambda *refs: main_kernel(geo, heads, *refs),
        in_specs=[smem] + [vmem] * 6 + [hbm, hbm, vmem],
        out_specs=[vmem] * 8,
        compiler_params=pltpu.CompilerParams(vmem_limit_bytes=big),
        out_shape=[
            shape((half_rows, width), BF16),
            shape((half_rows, width), BF16),
            shape((heads, win, win), F32),
            shape((cells, 3 * width), BF16),
            shape((cells, width), F32),
            shape((cells, 128), F32),
            shape((cells, width), BF16),
            shape((width, 128), F32),
        ],
        scratch_shapes=[
            pltpu.VMEM((cells, width), F32),
            pltpu.VMEM((n_rows, width), F32),
            pltpu.VMEM((n_cols, width), F32),
            pltpu.VMEM((n_corner, width), F32),
            pltpu.VMEM((cells, width), F32),
            pltpu.VMEM((cells, width), BF16),
            pltpu.VMEM((cells, 3 * width), BF16),
            pltpu.VMEM((cells, width), BF16),
            pltpu.VMEM((width, win), BF16),
            pltpu.VMEM((width, win), BF16),
            pltpu.VMEM((2, heads, win, win), F32),
            pltpu.VMEM((width, cells), BF16),
            pltpu.VMEM((width, width), F32),
            pltpu.VMEM((2, half_rows, width), BF16),
            pltpu.VMEM((width, 3 * width), BF16),
            pltpu.VMEM((width, width), BF16),
            pltpu.SemaphoreType.DMA((2,)),
        ],
    )(info, tok, cot, *rim, norm_gain.reshape(1, width), qkv_weight, out_weight, bias)

    got = chips.core(send)
    piece = half_rows // 2 // ny
    outs = call(
        lambda *refs: pair_sum_kernel(ny, nx, *refs),
        [shape((piece, width), BF16)] * (ny + nx),
        [],
        3,
        small_limit,
        smem_first=True,
    )(info, keep, got)

    outs, bias_sum = lax.optimization_barrier((outs, bias_sum))
    got_a = [outs[0]] + [chips.y(outs[k], k) for k in range(1, ny)]
    got_b = [outs[ny]] + [chips.x(outs[ny + k], k) for k in range(1, nx)]
    gain_row = norm_gain.reshape(1, width)
    small = call(
        lambda *refs: table_kernel(heads, *refs),
        shape((SMALL, width), F32),
        [pltpu.VMEM((heads * BANDS, SPAN), F32), pltpu.VMEM((heads, BANDS * SPAN), F32)],
        4,
        small_limit,
        cost=pl.CostEstimate(flops=3 * 10**9, bytes_accessed=10**6, transcendentals=0),
    )(index_t, bias_sum, gain_sum, gain_row)
    outs = call(
        lambda *refs: cross_sum_kernel(ny, nx, *refs),
        [shape((piece // nx, width), BF16)] * nx + [shape((piece // ny, width), BF16)] * ny,
        [pltpu.VMEM((piece, width), F32)],
        1 + ny + nx,
        small_limit,
        smem_first=True,
    )(info, *got_a, *got_b)

    got_a = [outs[0]] + [chips.x(outs[k], k) for k in range(1, nx)]
    got_b = [outs[nx]] + [chips.y(outs[nx + k], k) for k in range(1, ny)]
    small = small + chips.core(small)
    part = piece // nx
    mine = call(
        lambda *refs: join_sum_kernel(ny, nx, *refs),
        shape((2 * part + 2 * SMALL, width), BF16),
        [],
        ny + nx + 1,
        small_limit,
    )(*got_a, *got_b, small)

    def layer_norm_back(first, count, proj):
        return call(
            lambda *refs: back_kernel(geo, first, count, *refs),
            shape((count * win, width), BF16),
            [],
            6,
            small_limit,
            cost=pl.CostEstimate(flops=3 * 10**9, bytes_accessed=10**7, transcendentals=0),
        )(proj, unit, inv, cot_win, gain_row, qkv_weight)

    half_wins = geo.nwin // 2
    mine, grad_proj = lax.optimization_barrier((mine, grad_proj))
    got = chips.z(mine, 1)
    low = layer_norm_back(0, half_wins, grad_proj)
    mine = call(z_sum_kernel, shape(mine.shape, BF16), [], 2, small_limit)(mine, got)
    mine, grad_proj = lax.optimization_barrier((mine, grad_proj))
    got = chips.z(mine, 2)
    high = layer_norm_back(half_wins, geo.nwin - half_wins, grad_proj)
    b_rows, b_cols, b_corner = pad16(geo.n_rows), pad16(geo.n_cols), pad16(geo.n_corner)
    back = call(
        lambda *refs: unpack_send_kernel(geo, *refs),
        [shape((n, width), BF16) for n in (b_rows, b_cols, b_corner)],
        [
            pltpu.VMEM((cells, width), F32),
            pltpu.VMEM((b_rows + b_cols + b_corner, width), F32),
        ],
        2,
        small_limit,
    )(low, high)
    mine = call(z_sum_kernel, shape(mine.shape, BF16), [], 2, small_limit)(mine, got)
    mine, back = lax.optimization_barrier((mine, back))
    got = chips.z(mine, 4)
    back = (moved(back[0], -1, 0), moved(back[1], 0, -1), moved(back[2], -1, -1))
    own_a, own_b = call(
        z_sum_kernel,
        [shape((part, width), BF16), shape((part + 2 * SMALL, width), BF16)],
        [],
        2,
        small_limit,
    )(mine, got)

    got_a = [own_a] + [chips.x(own_a, k) for k in range(1, nx)]
    got_b = [own_b] + [chips.y(own_b, k) for k in range(1, ny)]
    own_a, own_b = call(
        lambda *refs: gather_kernel(ny, nx, *refs),
        [shape((piece, width), BF16), shape((piece + 2 * SMALL, width), BF16)],
        [],
        1 + ny + nx,
        small_limit,
        smem_first=True,
    )(info, *got_a, *got_b)
    own_a, own_b, back, low = lax.optimization_barrier((own_a, own_b, back, low))
    got_a = [own_a] + [chips.y(own_a, k) for k in range(1, ny)]
    got_b = [own_b] + [chips.x(own_b, k) for k in range(1, nx)]
    grad_tokens = call(
        lambda *refs: assemble_kernel(geo, *refs),
        shape((cells, width), BF16),
        [
            pltpu.VMEM((cells, width), F32),
            pltpu.VMEM((b_rows, width), F32),
            pltpu.VMEM((b_cols, width), F32),
            pltpu.VMEM((b_corner, width), F32),
            pltpu.VMEM((cells, width), F32),
        ],
        5,
        small_limit,
    )(low, high, *back)
    mine_a = call(
        lambda *refs: merge_kernel(ny, Y, False, *refs),
        [shape((width, width), BF16)],
        [],
        1 + ny,
        small_limit,
        smem_first=True,
    )(info, *got_a)[0]
    their_a = chips.core(mine_a)
    mine_b, line, grad_gain = call(
        lambda *refs: merge_kernel(nx, X, True, *refs),
        [
            shape((width, width), BF16),
            shape((heads, BANDS * SPAN), F32),
            shape((1, width), F32),
        ],
        [],
        1 + nx,
        small_limit,
        smem_first=True,
    )(info, *got_b)
    their_b = chips.core(mine_b)

    def write(mine, a, b, written):
        return pl.pallas_call(
            lambda *refs: place_kernel(mine, *refs),
            out_shape=[shape((width, 3 * width), F32), shape((width, width), F32)],
            in_specs=[smem, vmem, vmem] + [hbm] * len(written),
            out_specs=[hbm, hbm],
            input_output_aliases={3 + i: i for i in range(len(written))},
            scratch_shapes=[
                pltpu.VMEM((2, width, width), F32),
                pltpu.SemaphoreType.DMA((2, 4)),
            ],
            compiler_params=pltpu.CompilerParams(vmem_limit_bytes=small_limit),
        )(info, a, b, *written)

    written = write(True, mine_a, mine_b, ())
    grad_qkv, grad_out = write(False, their_a, their_b, tuple(written))
    grad_bias = line.T[:entries]
    return (grad_tokens.reshape(tokens.shape), grad_qkv, grad_out, grad_bias, grad_gain.reshape(width))


def solution(mesh):
    in_specs = (P(None, "lat", "lon", None), P(), P(), P(), P(), P(), P(None, "lat", "lon", None))
    out_specs = (P(None, "lat", "lon", None), P(), P(), P(), P())
    return jax.shard_map(
        per_device, mesh=mesh, in_specs=in_specs, out_specs=out_specs, check_vma=False
    )
```

profile of v0, /device:TPU:1, one launch (start us, length us, event | category | flops | bytes accessed | tf_op | source)
XLA Modules:
  0.0 153.0 jit_solution(4106901482244271565)
XLA Ops:
  0.7 2.7 %shard_map.110 = (bf16[224,512]{1,0:T(8,128)(2,1)}, bf16[512,512]{1,0:T(8,128)(2,1)}, bf16[80,512]{1,0:T(8,128)(2,1)}) custom-call(bf16[2,24,24,512]{3,2,1,0:T(8,128)(2,1)} %refs_0_.2, bf16[2,24,24,512]{3,2,1,0:T(8,128)(2,1)} %refs_1_.1), custom_call_target="tpu_custom_call" | custom-call | tf_op jit(solution)/shard_map/pallas_call | solution.py:622
  3.3 3.3 %collective-permute-start.1 = (bf16[512,512]{1,0:T(8,128)(2,1)}, bf16[512,512]{1,0:T(8,128)(2,1)}, u32[]{:S(2)}, u32[]{:S(2)}) collective-permute-start(bf16[512,512]{1,0:T(8,128)(2,1)} %get-tuple-element.72), channel_id=1, source_target_pairs={{0,15},{1,0},{2,1},{3,2},{4,3},{5,4},{6,5},{7,6},{8,7},{9,8},{10,9... | collective-permute-start | bytes 1572872 | tf_op jit(solution)/shard_map/ppermute | solution.py:448
  6.6 8.7 %collective-permute-start.2 = (bf16[80,512]{1,0:T(8,128)(2,1)}, bf16[80,512]{1,0:T(8,128)(2,1)}, u32[]{:S(2)}, u32[]{:S(2)}) collective-permute-start(bf16[80,512]{1,0:T(8,128)(2,1)} %get-tuple-element.73), channel_id=1, source_target_pairs={{0,255},{1,240},{2,241},{3,242},{4,243},{5,244},{6,245},{7,246},{8... | collective-permute-start | bytes 245768 | tf_op jit(solution)/shard_map/ppermute | solution.py:448
  15.3 1.2 collective-permute-start
  16.5 6.7 %shard_map.111 = (f32[8,144,144]{2,1,0:T(8,128)S(1)}, s32[144,144]{1,0:T(8,128)S(1)}) custom-call(s32[144,144]{1,0:T(8,128)S(1)} %copy-done.5, f32[8,759]{1,0:T(8,128)S(1)} %bitcast.18), custom_call_target="tpu_custom_call" | custom-call | flops 4000000000 | bytes 1000000 | tf_op jit(solution)/shard_map/pallas_call | solution.py:639
  24.0 1.4 copy-done.2
  25.4 1.0 copy-done.3
  26.5 32.8 %shard_map.112 = (bf16[1024,512]{1,0:T(8,128)(2,1)S(1)}, bf16[1024,512]{1,0:T(8,128)(2,1)S(1)}, f32[8,144,144]{2,1,0:T(8,128)S(1)}, bf16[1152,1536]{1,0:T(8,128)...) custom-call(s32[4]{0:T(128)S(1)} %pad_add_fusion.refs_0_, ...), custom_call_target="tpu_custom_call" | custom-call | tf_op jit(solution)/shard_map/pallas_call | solution.py:659
  59.4 2.6 %collective-permute-done.3.refs_2_ = bf16[1024,512]{1,0:T(8,128)(2,1)S(1)} collective-permute-done((bf16[1024,512]{1,0:T(8,128)(2,1)S(1)}, bf16[1024,512]{1,0:T(8,128)(2,1)S(1)}, u32[]{:S(2)}, u32[]{:S(2)}) %collective-permute-start.3) | collective-permute-done | bytes 1048608 | tf_op jit(solution)/shard_map/ppermute | solution.py:469
  62.0 0.8 shard_map.113
  62.9 2.5 %collective-permute-start.5 = (bf16[128,512]{1,0:T(8,128)(2,1)S(1)}, bf16[128,512]{1,0:T(8,128)(2,1)S(1)}, u32[]{:S(2)}, u32[]{:S(2)}) collective-permute-start(bf16[128,512]{1,0:T(8,128)(2,1)S(1)} %get-tuple-element.88), channel_id=1, source_target_pairs={{0,4},{1,5},{2,6},{3,7},{4,0},{5,1},{6,2},{7,3},{8,12},{9,13},{10,... | collective-permute-start | bytes 393224 | tf_op jit(solution)/shard_map/ppermute | solution.py:469
  66.0 2.1 %collective-permute-start.8 = (bf16[128,512]{1,0:T(8,128)(2,1)S(1)}, bf16[128,512]{1,0:T(8,128)(2,1)S(1)}, u32[]{:S(2)}, u32[]{:S(2)}) collective-permute-start(bf16[128,512]{1,0:T(8,128)(2,1)S(1)} %get-tuple-element.92), channel_id=1, source_target_pairs={{0,8},{1,9},{2,10},{3,11},{4,12},{5,13},{6,14},{7,15},{8,0},{9,1},... | collective-permute-start | bytes 393224 | tf_op jit(solution)/shard_map/ppermute | solution.py:469
  68.1 1.1 collective-permute-done.4.refs_2_
  69.2 3.5 %collective-permute-start.9 = (bf16[128,512]{1,0:T(8,128)(2,1)S(1)}, bf16[128,512]{1,0:T(8,128)(2,1)S(1)}, u32[]{:S(2)}, u32[]{:S(2)}) collective-permute-start(bf16[128,512]{1,0:T(8,128)(2,1)S(1)} %get-tuple-element.93), channel_id=1, source_target_pairs={{0,24},{1,25},{2,26},{3,27},{4,28},{5,29},{6,30},{7,31},{8,16},{9,... | collective-permute-start | bytes 393224 | tf_op jit(solution)/shard_map/ppermute | solution.py:469
  72.8 6.0 %shard_map.115 = f32[16,512]{1,0:T(8,128)S(1)} custom-call(s32[144,144]{1,0:T(8,128)S(1)} %copy-done.8, f32[8,144,144]{2,1,0:T(8,128)S(1)} %get-tuple-element.103.refs_1_, f32[512,128]{1,0:T(8,128)S(1)} %get-tuple-element.104.refs_2_, f32[1,512]{1,0:T(1,128)S(1)} %bitcast.15), custom_call_target="tpu_custom_call" | custom-call | flops 3000000000 | bytes 1000000 | tf_op jit(solution)/shard_map/pallas_call | solution.py:710
  78.8 1.3 collective-permute-start.16
  80.1 0.7 shard_map.114
  80.8 0.7 collective-permute-start.10
  81.5 0.8 collective-permute-start.11
  82.4 2.0 %collective-permute-start.12 = (bf16[32,512]{1,0:T(8,128)(2,1)S(1)}, bf16[32,512]{1,0:T(8,128)(2,1)S(1)}, u32[]{:S(2)}, u32[]{:S(2)}) collective-permute-start(bf16[32,512]{1,0:T(8,128)(2,1)S(1)} %get-tuple-element.97), channel_id=1, source_target_pairs={{0,24},{1,25},{2,26},{3,27},{4,28},{5,29},{6,30},{7,31},{8,16},{9,... | collective-permute-start | bytes 98312 | tf_op jit(solution)/shard_map/ppermute | solution.py:469
  84.9 2.2 %collective-permute-start.15 = (bf16[32,512]{1,0:T(8,128)(2,1)S(1)}, bf16[32,512]{1,0:T(8,128)(2,1)S(1)}, u32[]{:S(2)}, u32[]{:S(2)}) collective-permute-start(bf16[32,512]{1,0:T(8,128)(2,1)S(1)} %get-tuple-element.101), channel_id=1, source_target_pairs={{0,6},{1,7},{2,0},{3,1},{4,2},{5,3},{6,4},{7,5},{8,14},{9,15},{10,... | collective-permute-start | bytes 98312 | tf_op jit(solution)/shard_map/ppermute | solution.py:469
  87.1 1.2 collective-permute-done.13.refs_5_
  88.7 0.9 collective-permute-done.15.refs_7_
  89.7 3.1 %shard_map.119.refs_0_ = bf16[576,512]{1,0:T(8,128)(2,1)S(1)} custom-call(bf16[1152,1536]{1,0:T(8,128)(2,1)S(1)} %get-tuple-element.112.refs_0_, f32[1152,512]{1,0:T(8,128)S(1)} %get-tuple-element.109.refs_1_, f32[1152,128]{1,0:T(8,128)S(1)} %get-tuple-element.110.refs_2_, bf16[1152,512]{1,0:T(8,128)(2,1)S(1)} %get-tuple-element.111.refs_3_, ...), custom_call_target="tpu_custom_call" | custom-call | flops 3000000000 | bytes 10000000 | tf_op jit(solution)/shard_map/pallas_call | solution.py:740
  93.2 2.6 %collective-permute-start.18 = (bf16[96,512]{1,0:T(8,128)(2,1)S(1)}, bf16[96,512]{1,0:T(8,128)(2,1)S(1)}, u32[]{:S(2)}, u32[]{:S(2)}) collective-permute-start(bf16[96,512]{1,0:T(8,128)(2,1)S(1)} %shard_map.117.mine_ref), channel_id=1, source_target_pairs={{0,96},{1,97},{2,98},{3,99},{4,100},{5,101},{6,102},{7,103},{8,104... | collective-permute-start | bytes 294920 | tf_op jit(solution)/shard_map/ppermute | solution.py:469
  95.7 3.1 %shard_map.120.refs_1_ = bf16[576,512]{1,0:T(8,128)(2,1)S(1)} custom-call(bf16[1152,1536]{1,0:T(8,128)(2,1)S(1)} %get-tuple-element.112.refs_0_, f32[1152,512]{1,0:T(8,128)S(1)} %get-tuple-element.109.refs_1_, f32[1152,128]{1,0:T(8,128)S(1)} %get-tuple-element.110.refs_2_, bf16[1152,512]{1,0:T(8,128)(2,1)S(1)} %get-tuple-element.111.refs_3_, ...), custom_call_target="tpu_custom_call" | custom-call | flops 3000000000 | bytes 10000000 | tf_op jit(solution)/shard_map/pallas_call | solution.py:740
  99.2 5.0 %collective-permute-start.27 = (bf16[256,512]{1,0:T(8,128)(2,1)S(1)}, bf16[256,512]{1,0:T(8,128)(2,1)S(1)}, u32[]{:S(2)}, u32[]{:S(2)}) collective-permute-start(bf16[256,512]{1,0:T(8,128)(2,1)S(1)} %get-tuple-element.122), channel_id=1, source_target_pairs={{0,1},{1,2},{2,3},{3,4},{4,5},{5,6},{6,7},{7,8},{8,9},{9,10},{10,1... | collective-permute-start | bytes 786440 | tf_op jit(solution)/shard_map/ppermute | solution.py:448
  104.2 3.7 %collective-permute-start.19 = (bf16[96,512]{1,0:T(8,128)(2,1)S(1)}, bf16[96,512]{1,0:T(8,128)(2,1)S(1)}, u32[]{:S(2)}, u32[]{:S(2)}) collective-permute-start(bf16[96,512]{1,0:T(8,128)(2,1)S(1)} %shard_map.118.mine_ref), channel_id=1, source_target_pairs={{0,224},{1,225},{2,226},{3,227},{4,228},{5,229},{6,230},{7,231},{8... | collective-permute-start | bytes 294920 | tf_op jit(solution)/shard_map/ppermute | solution.py:469
  107.9 3.6 %collective-permute-done.19.got_ref = bf16[96,512]{1,0:T(8,128)(2,1)S(1)} collective-permute-done((bf16[96,512]{1,0:T(8,128)(2,1)S(1)}, bf16[96,512]{1,0:T(8,128)(2,1)S(1)}, u32[]{:S(2)}, u32[]{:S(2)}) %collective-permute-start.19) | collective-permute-done | bytes 98336 | tf_op jit(solution)/shard_map/ppermute | solution.py:469
  112.0 2.3 %collective-permute-start.25 = (bf16[64,512]{1,0:T(8,128)(2,1)S(1)}, bf16[64,512]{1,0:T(8,128)(2,1)S(1)}, u32[]{:S(2)}, u32[]{:S(2)}) collective-permute-start(bf16[64,512]{1,0:T(8,128)(2,1)S(1)} %get-tuple-element.118.refs_5_), channel_id=1, source_target_pairs={{0,6},{1,7},{2,0},{3,1},{4,2},{5,3},{6,4},{7,5},{8,14},{9,15},{10,... | collective-permute-start | bytes 196616 | tf_op jit(solution)/shard_map/ppermute | solution.py:469
  114.3 1.2 collective-permute-start.26
  115.4 2.1 %collective-permute-start.21 = (bf16[32,512]{1,0:T(8,128)(2,1)S(1)}, bf16[32,512]{1,0:T(8,128)(2,1)S(1)}, u32[]{:S(2)}, u32[]{:S(2)}) collective-permute-start(bf16[32,512]{1,0:T(8,128)(2,1)S(1)} %get-tuple-element.117.refs_1_), channel_id=1, source_target_pairs={{0,8},{1,9},{2,10},{3,11},{4,12},{5,13},{6,14},{7,15},{8,0},{9,1},... | collective-permute-start | bytes 98312 | tf_op jit(solution)/shard_map/ppermute | solution.py:469
  117.6 3.0 %collective-permute-done.21.refs_3_ = bf16[32,512]{1,0:T(8,128)(2,1)S(1)} collective-permute-done((bf16[32,512]{1,0:T(8,128)(2,1)S(1)}, bf16[32,512]{1,0:T(8,128)(2,1)S(1)}, u32[]{:S(2)}, u32[]{:S(2)}) %collective-permute-start.21) | collective-permute-done | bytes 32800 | tf_op jit(solution)/shard_map/ppermute | solution.py:469
  120.5 1.3 collective-permute-done.20.refs_2_
  121.8 3.0 %collective-permute-start.28 = (bf16[48,512]{1,0:T(8,128)(2,1)S(1)}, bf16[48,512]{1,0:T(8,128)(2,1)S(1)}, u32[]{:S(2)}, u32[]{:S(2)}) collective-permute-start(bf16[48,512]{1,0:T(8,128)(2,1)S(1)} %get-tuple-element.123), channel_id=1, source_target_pairs={{0,17},{1,18},{2,19},{3,20},{4,21},{5,22},{6,23},{7,24},{8,25},{9,... | collective-permute-start | bytes 147464 | tf_op jit(solution)/shard_map/ppermute | solution.py:448
  125.1 1.0 collective-permute-done.23.refs_6_
  126.7 2.1 %collective-permute-done.28.refs_4_ = bf16[48,512]{1,0:T(8,128)(2,1)S(1)} collective-permute-done((bf16[48,512]{1,0:T(8,128)(2,1)S(1)}, bf16[48,512]{1,0:T(8,128)(2,1)S(1)}, u32[]{:S(2)}, u32[]{:S(2)}) %collective-permute-start.28) | collective-permute-done | bytes 49184 | tf_op jit(solution)/shard_map/ppermute | solution.py:448
  128.9 2.5 %collective-permute-start.31 = (bf16[128,512]{1,0:T(8,128)(2,1)S(1)}, bf16[128,512]{1,0:T(8,128)(2,1)S(1)}, u32[]{:S(2)}, u32[]{:S(2)}) collective-permute-start(bf16[128,512]{1,0:T(8,128)(2,1)S(1)} %get-tuple-element.128.refs_1_), channel_id=1, source_target_pairs={{0,6},{1,7},{2,0},{3,1},{4,2},{5,3},{6,4},{7,5},{8,14},{9,15},{10,... | collective-permute-start | bytes 393224 | tf_op jit(solution)/shard_map/ppermute | solution.py:469
  131.3 2.2 %collective-permute-start.34 = (bf16[160,512]{1,0:T(8,128)(2,1)S(1)}, bf16[160,512]{1,0:T(8,128)(2,1)S(1)}, u32[]{:S(2)}, u32[]{:S(2)}) collective-permute-start(bf16[160,512]{1,0:T(8,128)(2,1)S(1)} %get-tuple-element.129.refs_1_), channel_id=1, source_target_pairs={{0,8},{1,9},{2,10},{3,11},{4,12},{5,13},{6,14},{7,15},{8,0},{9,1},... | collective-permute-start | bytes 491528 | tf_op jit(solution)/shard_map/ppermute | solution.py:469
  133.6 0.9 collective-permute-start.33
  134.4 1.3 collective-permute-start.30
  135.7 4.3 %collective-permute-done.30.refs_3_ = bf16[128,512]{1,0:T(8,128)(2,1)S(1)} collective-permute-done((bf16[128,512]{1,0:T(8,128)(2,1)S(1)}, bf16[128,512]{1,0:T(8,128)(2,1)S(1)}, u32[]{:S(2)}, u32[]{:S(2)}) %collective-permute-start.30) | collective-permute-done | bytes 131104 | tf_op jit(solution)/shard_map/ppermute | solution.py:469
  140.0 1.8 %collective-permute-done.29.refs_2_ = bf16[128,512]{1,0:T(8,128)(2,1)S(1)} collective-permute-done((bf16[128,512]{1,0:T(8,128)(2,1)S(1)}, bf16[128,512]{1,0:T(8,128)(2,1)S(1)}, u32[]{:S(2)}, u32[]{:S(2)}) %collective-permute-start.29) | collective-permute-done | bytes 131104 | tf_op jit(solution)/shard_map/ppermute | solution.py:469
  142.4 3.6 %collective-permute-start.32 = (bf16[512,512]{1,0:T(8,128)(2,1)S(1)}, bf16[512,512]{1,0:T(8,128)(2,1)S(1)}, u32[]{:S(2)}, u32[]{:S(2)}) collective-permute-start(bf16[512,512]{1,0:T(8,128)(2,1)S(1)} %shard_map.125.refs_1_), channel_id=1, source_target_pairs={{0,1},{1,0},{2,3},{3,2},{4,5},{5,4},{6,7},{7,6},{8,9},{9,8},{10,11... | collective-permute-start | bytes 1572872 | tf_op jit(solution)/shard_map/ppermute | solution.py:469
  146.0 1.2 shard_map.126
  147.3 1.7 %shard_map.124 = bf16[1152,512]{1,0:T(8,128)(2,1)} custom-call(bf16[576,512]{1,0:T(8,128)(2,1)S(1)} %shard_map.119.refs_0_, bf16[576,512]{1,0:T(8,128)(2,1)S(1)} %shard_map.120.refs_1_, bf16[112,512]{1,0:T(8,128)(2,1)S(1)} %collective-permute-done.26.refs_2_, bf16[256,512]{1,0:T(8,128)(2,1)S(1)} %collective-permute-done.27.refs_3_, ...), custom_call_target="tpu_custom_call" | custom-call | tf_op jit(solution)/shard_map/pallas_call | solution.py:793
  148.9 1.9 %shard_map.127 = (f32[512,1536]{1,0:T(8,128)}, f32[512,512]{1,0:T(8,128)}) custom-call(s32[4]{0:T(128)S(1)} %pad_add_fusion.refs_0_, bf16[512,512]{1,0:T(8,128)(2,1)S(1)} %shard_map.125.refs_1_, bf16[512,512]{1,0:T(8,128)(2,1)S(1)} %get-tuple-element.130.refs_2_), custom_call_target="tpu_custom_call" | custom-call | tf_op jit(solution)/shard_map/pallas_call | solution.py:830
  150.9 1.9 %shard_map.128 = (f32[512,1536]{1,0:T(8,128)}, f32[512,512]{1,0:T(8,128)}) custom-call(s32[4]{0:T(128)S(1)} %pad_add_fusion.refs_0_, bf16[512,512]{1,0:T(8,128)(2,1)S(1)} %collective-permute-done.32.refs_1_, bf16[512,512]{1,0:T(8,128)(2,1)S(1)} %collective-permute-done.36.refs_2_, ...), custom_call_target="tpu_custom_call", output_to_operand_aliasing={{0}: (3, {}), {1}: (4, {})} | custom-call | tf_op jit(solution)/shard_map/pallas_call | solution.py:830
  (65 shorter events, 5.3 us)
Async XLA Ops:
  0.6 15.8 %copy-start.5 = (s32[144,144]{1,0:T(8,128)S(1)}, s32[144,144]{1,0:T(8,128)}, u32[]{:S(2)}) copy-start(s32[144,144]{1,0:T(8,128)} %refs_0_.3) | copy-start | bytes 248836
  0.6 15.8 %copy-start.6 = (f32[759,8]{0,1:T(8,128)S(1)}, f32[759,8]{0,1:T(8,128)}, u32[]{:S(2)}) copy-start(f32[759,8]{0,1:T(8,128)} %param.11) | copy-start | bytes 72868
  3.3 20.7 %collective-permute-start.1 = (bf16[512,512]{1,0:T(8,128)(2,1)}, bf16[512,512]{1,0:T(8,128)(2,1)}, u32[]{:S(2)}, u32[]{:S(2)}) collective-permute-start(bf16[512,512]{1,0:T(8,128)(2,1)} %get-tuple-element.72), channel_id=1, source_target_pairs={{0,15},{1,0},{2,1},{3,2},{4,3},{5,4},{6,5},{7,6},{8,7},{9,8},{10,9... | collective-permute-start | bytes 1572872 | tf_op jit(solution)/shard_map/ppermute | solution.py:448
  6.6 17.3 %collective-permute-start.2 = (bf16[80,512]{1,0:T(8,128)(2,1)}, bf16[80,512]{1,0:T(8,128)(2,1)}, u32[]{:S(2)}, u32[]{:S(2)}) collective-permute-start(bf16[80,512]{1,0:T(8,128)(2,1)} %get-tuple-element.73), channel_id=1, source_target_pairs={{0,255},{1,240},{2,241},{3,242},{4,243},{5,244},{6,245},{7,246},{8... | collective-permute-start | bytes 245768 | tf_op jit(solution)/shard_map/ppermute | solution.py:448
  15.3 8.7 %collective-permute-start = (bf16[224,512]{1,0:T(8,128)(2,1)}, bf16[224,512]{1,0:T(8,128)(2,1)}, u32[]{:S(2)}, u32[]{:S(2)}) collective-permute-start(bf16[224,512]{1,0:T(8,128)(2,1)} %get-tuple-element.71), channel_id=1, source_target_pairs={{0,240},{1,241},{2,242},{3,243},{4,244},{5,245},{6,246},{7,247},{8... | collective-permute-start | bytes 688136 | tf_op jit(solution)/shard_map/ppermute | solution.py:448
  16.5 7.5 %copy-start = (bf16[2,24,24,512]{3,2,1,0:T(8,128)(2,1)S(1)}, bf16[2,24,24,512]{3,2,1,0:T(8,128)(2,1)}, u32[]{:S(2)}) copy-start(bf16[2,24,24,512]{3,2,1,0:T(8,128)(2,1)} %refs_0_.2) | copy-start | bytes 3538948
  16.5 7.5 %copy-start.1 = (bf16[2,24,24,512]{3,2,1,0:T(8,128)(2,1)S(1)}, bf16[2,24,24,512]{3,2,1,0:T(8,128)(2,1)}, u32[]{:S(2)}) copy-start(bf16[2,24,24,512]{3,2,1,0:T(8,128)(2,1)} %refs_1_.1) | copy-start | bytes 3538948
  16.5 7.5 %copy-start.4 = (f32[512]{0:T(512)S(1)}, f32[512]{0:T(512)}, u32[]{:S(2)}) copy-start(f32[512]{0:T(512)} %param.8) | copy-start | bytes 6148
  23.2 0.7 copy-start.7
  24.0 1.4 copy-start.2
  25.4 1.0 copy-start.3
  59.3 13.5 %copy-start.8 = (s32[144,144]{1,0:T(8,128)S(1)}, s32[144,144]{1,0:T(8,128)}, u32[]{:S(2)}) copy-start(s32[144,144]{1,0:T(8,128)} %copy-done.7) | copy-start | bytes 248836
  59.3 2.7 %collective-permute-start.3 = (bf16[1024,512]{1,0:T(8,128)(2,1)S(1)}, bf16[1024,512]{1,0:T(8,128)(2,1)S(1)}, u32[]{:S(2)}, u32[]{:S(2)}) collective-permute-start(bf16[1024,512]{1,0:T(8,128)(2,1)S(1)} %get-tuple-element.76), channel_id=1, source_target_pairs={{0,1},{1,0},{2,3},{3,2},{4,5},{5,4},{6,7},{7,6},{8,9},{9,8},{10,11... | collective-permute-start | bytes 3145736 | tf_op jit(solution)/shard_map/ppermute | solution.py:469
  62.8 6.4 %collective-permute-start.4 = (bf16[128,512]{1,0:T(8,128)(2,1)S(1)}, bf16[128,512]{1,0:T(8,128)(2,1)S(1)}, u32[]{:S(2)}, u32[]{:S(2)}) collective-permute-start(bf16[128,512]{1,0:T(8,128)(2,1)S(1)} %get-tuple-element.87), channel_id=1, source_target_pairs={{0,2},{1,3},{2,4},{3,5},{4,6},{5,7},{6,0},{7,1},{8,10},{9,11},{10,... | collective-permute-start | bytes 393224 | tf_op jit(solution)/shard_map/ppermute | solution.py:469
  62.9 15.8 %collective-permute-start.5 = (bf16[128,512]{1,0:T(8,128)(2,1)S(1)}, bf16[128,512]{1,0:T(8,128)(2,1)S(1)}, u32[]{:S(2)}, u32[]{:S(2)}) collective-permute-start(bf16[128,512]{1,0:T(8,128)(2,1)S(1)} %get-tuple-element.88), channel_id=1, source_target_pairs={{0,4},{1,5},{2,6},{3,7},{4,0},{5,1},{6,2},{7,3},{8,12},{9,13},{10,... | collective-permute-start | bytes 393224 | tf_op jit(solution)/shard_map/ppermute | solution.py:469
  65.4 14.6 %collective-permute-start.6 = (bf16[128,512]{1,0:T(8,128)(2,1)S(1)}, bf16[128,512]{1,0:T(8,128)(2,1)S(1)}, u32[]{:S(2)}, u32[]{:S(2)}) collective-permute-start(bf16[128,512]{1,0:T(8,128)(2,1)S(1)} %get-tuple-element.89), channel_id=1, source_target_pairs={{0,6},{1,7},{2,0},{3,1},{4,2},{5,3},{6,4},{7,5},{8,14},{9,15},{10,... | collective-permute-start | bytes 393224 | tf_op jit(solution)/shard_map/ppermute | solution.py:469
  65.6 14.5 %collective-permute-start.7 = (bf16[128,512]{1,0:T(8,128)(2,1)S(1)}, bf16[128,512]{1,0:T(8,128)(2,1)S(1)}, u32[]{:S(2)}, u32[]{:S(2)}) collective-permute-start(bf16[128,512]{1,0:T(8,128)(2,1)S(1)} %get-tuple-element.91), channel_id=1, source_target_pairs={{0,16},{1,17},{2,18},{3,19},{4,20},{5,21},{6,22},{7,23},{8,24},{9,... | collective-permute-start | bytes 393224 | tf_op jit(solution)/shard_map/ppermute | solution.py:469
  66.0 14.1 %collective-permute-start.8 = (bf16[128,512]{1,0:T(8,128)(2,1)S(1)}, bf16[128,512]{1,0:T(8,128)(2,1)S(1)}, u32[]{:S(2)}, u32[]{:S(2)}) collective-permute-start(bf16[128,512]{1,0:T(8,128)(2,1)S(1)} %get-tuple-element.92), channel_id=1, source_target_pairs={{0,8},{1,9},{2,10},{3,11},{4,12},{5,13},{6,14},{7,15},{8,0},{9,1},... | collective-permute-start | bytes 393224 | tf_op jit(solution)/shard_map/ppermute | solution.py:469
  69.2 10.8 %collective-permute-start.9 = (bf16[128,512]{1,0:T(8,128)(2,1)S(1)}, bf16[128,512]{1,0:T(8,128)(2,1)S(1)}, u32[]{:S(2)}, u32[]{:S(2)}) collective-permute-start(bf16[128,512]{1,0:T(8,128)(2,1)S(1)} %get-tuple-element.93), channel_id=1, source_target_pairs={{0,24},{1,25},{2,26},{3,27},{4,28},{5,29},{6,30},{7,31},{8,16},{9,... | collective-permute-start | bytes 393224 | tf_op jit(solution)/shard_map/ppermute | solution.py:469
  78.8 5.6 %collective-permute-start.16 = (f32[16,512]{1,0:T(8,128)S(1)}, f32[16,512]{1,0:T(8,128)S(1)}, u32[]{:S(2)}, u32[]{:S(2)}) collective-permute-start(f32[16,512]{1,0:T(8,128)S(1)} %shard_map.115), channel_id=1, source_target_pairs={{0,1},{1,0},{2,3},{3,2},{4,5},{5,4},{6,7},{7,6},{8,9},{9,8},{10,11... | collective-permute-start | bytes 98312 | tf_op jit(solution)/shard_map/ppermute | solution.py:469
  80.8 4.1 %collective-permute-start.10 = (bf16[32,512]{1,0:T(8,128)(2,1)S(1)}, bf16[32,512]{1,0:T(8,128)(2,1)S(1)}, u32[]{:S(2)}, u32[]{:S(2)}) collective-permute-start(bf16[32,512]{1,0:T(8,128)(2,1)S(1)} %get-tuple-element.95), channel_id=1, source_target_pairs={{0,16},{1,17},{2,18},{3,19},{4,20},{5,21},{6,22},{7,23},{8,24},{9,... | collective-permute-start | bytes 98312 | tf_op jit(solution)/shard_map/ppermute | solution.py:469
  81.5 5.6 %collective-permute-start.11 = (bf16[32,512]{1,0:T(8,128)(2,1)S(1)}, bf16[32,512]{1,0:T(8,128)(2,1)S(1)}, u32[]{:S(2)}, u32[]{:S(2)}) collective-permute-start(bf16[32,512]{1,0:T(8,128)(2,1)S(1)} %get-tuple-element.96), channel_id=1, source_target_pairs={{0,8},{1,9},{2,10},{3,11},{4,12},{5,13},{6,14},{7,15},{8,0},{9,1},... | collective-permute-start | bytes 98312 | tf_op jit(solution)/shard_map/ppermute | solution.py:469
  82.4 4.8 %collective-permute-start.12 = (bf16[32,512]{1,0:T(8,128)(2,1)S(1)}, bf16[32,512]{1,0:T(8,128)(2,1)S(1)}, u32[]{:S(2)}, u32[]{:S(2)}) collective-permute-start(bf16[32,512]{1,0:T(8,128)(2,1)S(1)} %get-tuple-element.97), channel_id=1, source_target_pairs={{0,24},{1,25},{2,26},{3,27},{4,28},{5,29},{6,30},{7,31},{8,16},{9,... | collective-permute-start | bytes 98312 | tf_op jit(solution)/shard_map/ppermute | solution.py:469
  84.3 4.0 %collective-permute-start.13 = (bf16[32,512]{1,0:T(8,128)(2,1)S(1)}, bf16[32,512]{1,0:T(8,128)(2,1)S(1)}, u32[]{:S(2)}, u32[]{:S(2)}) collective-permute-start(bf16[32,512]{1,0:T(8,128)(2,1)S(1)} %get-tuple-element.99), channel_id=1, source_target_pairs={{0,2},{1,3},{2,4},{3,5},{4,6},{5,7},{6,0},{7,1},{8,10},{9,11},{10,... | collective-permute-start | bytes 98312 | tf_op jit(solution)/shard_map/ppermute | solution.py:469
  84.3 4.3 %collective-permute-start.14 = (bf16[32,512]{1,0:T(8,128)(2,1)S(1)}, bf16[32,512]{1,0:T(8,128)(2,1)S(1)}, u32[]{:S(2)}, u32[]{:S(2)}) collective-permute-start(bf16[32,512]{1,0:T(8,128)(2,1)S(1)} %get-tuple-element.100), channel_id=1, source_target_pairs={{0,4},{1,5},{2,6},{3,7},{4,0},{5,1},{6,2},{7,3},{8,12},{9,13},{10,... | collective-permute-start | bytes 98312 | tf_op jit(solution)/shard_map/ppermute | solution.py:469
  84.9 4.7 %collective-permute-start.15 = (bf16[32,512]{1,0:T(8,128)(2,1)S(1)}, bf16[32,512]{1,0:T(8,128)(2,1)S(1)}, u32[]{:S(2)}, u32[]{:S(2)}) collective-permute-start(bf16[32,512]{1,0:T(8,128)(2,1)S(1)} %get-tuple-element.101), channel_id=1, source_target_pairs={{0,6},{1,7},{2,0},{3,1},{4,2},{5,3},{6,4},{7,5},{8,14},{9,15},{10,... | collective-permute-start | bytes 98312 | tf_op jit(solution)/shard_map/ppermute | solution.py:469
  89.6 3.6 %collective-permute-start.17 = (bf16[96,512]{1,0:T(8,128)(2,1)S(1)}, bf16[96,512]{1,0:T(8,128)(2,1)S(1)}, u32[]{:S(2)}, u32[]{:S(2)}) collective-permute-start(bf16[96,512]{1,0:T(8,128)(2,1)S(1)} %shard_map.116.mine_ref), channel_id=1, source_target_pairs={{0,32},{1,33},{2,34},{3,35},{4,36},{5,37},{6,38},{7,39},{8,40},{9,... | collective-permute-start | bytes 294920 | tf_op jit(solution)/shard_map/ppermute | solution.py:469
  93.2 6.0 %collective-permute-start.18 = (bf16[96,512]{1,0:T(8,128)(2,1)S(1)}, bf16[96,512]{1,0:T(8,128)(2,1)S(1)}, u32[]{:S(2)}, u32[]{:S(2)}) collective-permute-start(bf16[96,512]{1,0:T(8,128)(2,1)S(1)} %shard_map.117.mine_ref), channel_id=1, source_target_pairs={{0,96},{1,97},{2,98},{3,99},{4,100},{5,101},{6,102},{7,103},{8,104... | collective-permute-start | bytes 294920 | tf_op jit(solution)/shard_map/ppermute | solution.py:469
  99.2 29.7 %collective-permute-start.27 = (bf16[256,512]{1,0:T(8,128)(2,1)S(1)}, bf16[256,512]{1,0:T(8,128)(2,1)S(1)}, u32[]{:S(2)}, u32[]{:S(2)}) collective-permute-start(bf16[256,512]{1,0:T(8,128)(2,1)S(1)} %get-tuple-element.122), channel_id=1, source_target_pairs={{0,1},{1,2},{2,3},{3,4},{4,5},{5,6},{6,7},{7,8},{8,9},{9,10},{10,1... | collective-permute-start | bytes 786440 | tf_op jit(solution)/shard_map/ppermute | solution.py:448
  104.2 7.3 %collective-permute-start.19 = (bf16[96,512]{1,0:T(8,128)(2,1)S(1)}, bf16[96,512]{1,0:T(8,128)(2,1)S(1)}, u32[]{:S(2)}, u32[]{:S(2)}) collective-permute-start(bf16[96,512]{1,0:T(8,128)(2,1)S(1)} %shard_map.118.mine_ref), channel_id=1, source_target_pairs={{0,224},{1,225},{2,226},{3,227},{4,228},{5,229},{6,230},{7,231},{8... | collective-permute-start | bytes 294920 | tf_op jit(solution)/shard_map/ppermute | solution.py:469
  111.6 6.0 %collective-permute-start.22 = (bf16[32,512]{1,0:T(8,128)(2,1)S(1)}, bf16[32,512]{1,0:T(8,128)(2,1)S(1)}, u32[]{:S(2)}, u32[]{:S(2)}) collective-permute-start(bf16[32,512]{1,0:T(8,128)(2,1)S(1)} %get-tuple-element.117.refs_1_), channel_id=1, source_target_pairs={{0,24},{1,25},{2,26},{3,27},{4,28},{5,29},{6,30},{7,31},{8,16},{9,... | collective-permute-start | bytes 98312 | tf_op jit(solution)/shard_map/ppermute | solution.py:469
  112.0 9.8 %collective-permute-start.25 = (bf16[64,512]{1,0:T(8,128)(2,1)S(1)}, bf16[64,512]{1,0:T(8,128)(2,1)S(1)}, u32[]{:S(2)}, u32[]{:S(2)}) collective-permute-start(bf16[64,512]{1,0:T(8,128)(2,1)S(1)} %get-tuple-element.118.refs_5_), channel_id=1, source_target_pairs={{0,6},{1,7},{2,0},{3,1},{4,2},{5,3},{6,4},{7,5},{8,14},{9,15},{10,... | collective-permute-start | bytes 196616 | tf_op jit(solution)/shard_map/ppermute | solution.py:469
  114.3 14.6 %collective-permute-start.26 = (bf16[112,512]{1,0:T(8,128)(2,1)S(1)}, bf16[112,512]{1,0:T(8,128)(2,1)S(1)}, u32[]{:S(2)}, u32[]{:S(2)}) collective-permute-start(bf16[112,512]{1,0:T(8,128)(2,1)S(1)} %get-tuple-element.121), channel_id=1, source_target_pairs={{0,16},{1,17},{2,18},{3,19},{4,20},{5,21},{6,22},{7,23},{8,24},{9,... | collective-permute-start | bytes 344072 | tf_op jit(solution)/shard_map/ppermute | solution.py:448
  115.4 5.1 %collective-permute-start.21 = (bf16[32,512]{1,0:T(8,128)(2,1)S(1)}, bf16[32,512]{1,0:T(8,128)(2,1)S(1)}, u32[]{:S(2)}, u32[]{:S(2)}) collective-permute-start(bf16[32,512]{1,0:T(8,128)(2,1)S(1)} %get-tuple-element.117.refs_1_), channel_id=1, source_target_pairs={{0,8},{1,9},{2,10},{3,11},{4,12},{5,13},{6,14},{7,15},{8,0},{9,1},... | collective-permute-start | bytes 98312 | tf_op jit(solution)/shard_map/ppermute | solution.py:469
  117.5 4.3 %collective-permute-start.20 = (bf16[32,512]{1,0:T(8,128)(2,1)S(1)}, bf16[32,512]{1,0:T(8,128)(2,1)S(1)}, u32[]{:S(2)}, u32[]{:S(2)}) collective-permute-start(bf16[32,512]{1,0:T(8,128)(2,1)S(1)} %get-tuple-element.117.refs_1_), channel_id=1, source_target_pairs={{0,16},{1,17},{2,18},{3,19},{4,20},{5,21},{6,22},{7,23},{8,24},{9,... | collective-permute-start | bytes 98312 | tf_op jit(solution)/shard_map/ppermute | solution.py:469
  120.5 4.6 %collective-permute-start.24 = (bf16[64,512]{1,0:T(8,128)(2,1)S(1)}, bf16[64,512]{1,0:T(8,128)(2,1)S(1)}, u32[]{:S(2)}, u32[]{:S(2)}) collective-permute-start(bf16[64,512]{1,0:T(8,128)(2,1)S(1)} %get-tuple-element.118.refs_5_), channel_id=1, source_target_pairs={{0,4},{1,5},{2,6},{3,7},{4,0},{5,1},{6,2},{7,3},{8,12},{9,13},{10,... | collective-permute-start | bytes 196616 | tf_op jit(solution)/shard_map/ppermute | solution.py:469
  121.8 4.3 %collective-permute-start.23 = (bf16[64,512]{1,0:T(8,128)(2,1)S(1)}, bf16[64,512]{1,0:T(8,128)(2,1)S(1)}, u32[]{:S(2)}, u32[]{:S(2)}) collective-permute-start(bf16[64,512]{1,0:T(8,128)(2,1)S(1)} %get-tuple-element.118.refs_5_), channel_id=1, source_target_pairs={{0,2},{1,3},{2,4},{3,5},{4,6},{5,7},{6,0},{7,1},{8,10},{9,11},{10,... | collective-permute-start | bytes 196616 | tf_op jit(solution)/shard_map/ppermute | solution.py:469
  121.8 7.0 %collective-permute-start.28 = (bf16[48,512]{1,0:T(8,128)(2,1)S(1)}, bf16[48,512]{1,0:T(8,128)(2,1)S(1)}, u32[]{:S(2)}, u32[]{:S(2)}) collective-permute-start(bf16[48,512]{1,0:T(8,128)(2,1)S(1)} %get-tuple-element.123), channel_id=1, source_target_pairs={{0,17},{1,18},{2,19},{3,20},{4,21},{5,22},{6,23},{7,24},{8,25},{9,... | collective-permute-start | bytes 147464 | tf_op jit(solution)/shard_map/ppermute | solution.py:448
  128.9 6.8 %collective-permute-start.31 = (bf16[128,512]{1,0:T(8,128)(2,1)S(1)}, bf16[128,512]{1,0:T(8,128)(2,1)S(1)}, u32[]{:S(2)}, u32[]{:S(2)}) collective-permute-start(bf16[128,512]{1,0:T(8,128)(2,1)S(1)} %get-tuple-element.128.refs_1_), channel_id=1, source_target_pairs={{0,6},{1,7},{2,0},{3,1},{4,2},{5,3},{6,4},{7,5},{8,14},{9,15},{10,... | collective-permute-start | bytes 393224 | tf_op jit(solution)/shard_map/ppermute | solution.py:469
  131.3 14.7 %collective-permute-start.35 = (bf16[160,512]{1,0:T(8,128)(2,1)S(1)}, bf16[160,512]{1,0:T(8,128)(2,1)S(1)}, u32[]{:S(2)}, u32[]{:S(2)}) collective-permute-start(bf16[160,512]{1,0:T(8,128)(2,1)S(1)} %get-tuple-element.129.refs_1_), channel_id=1, source_target_pairs={{0,24},{1,25},{2,26},{3,27},{4,28},{5,29},{6,30},{7,31},{8,16},{9,... | collective-permute-start | bytes 491528 | tf_op jit(solution)/shard_map/ppermute | solution.py:469
  131.3 14.7 %collective-permute-start.34 = (bf16[160,512]{1,0:T(8,128)(2,1)S(1)}, bf16[160,512]{1,0:T(8,128)(2,1)S(1)}, u32[]{:S(2)}, u32[]{:S(2)}) collective-permute-start(bf16[160,512]{1,0:T(8,128)(2,1)S(1)} %get-tuple-element.129.refs_1_), channel_id=1, source_target_pairs={{0,8},{1,9},{2,10},{3,11},{4,12},{5,13},{6,14},{7,15},{8,0},{9,1},... | collective-permute-start | bytes 491528 | tf_op jit(solution)/shard_map/ppermute | solution.py:469
  133.6 12.5 %collective-permute-start.33 = (bf16[160,512]{1,0:T(8,128)(2,1)S(1)}, bf16[160,512]{1,0:T(8,128)(2,1)S(1)}, u32[]{:S(2)}, u32[]{:S(2)}) collective-permute-start(bf16[160,512]{1,0:T(8,128)(2,1)S(1)} %get-tuple-element.129.refs_1_), channel_id=1, source_target_pairs={{0,16},{1,17},{2,18},{3,19},{4,20},{5,21},{6,22},{7,23},{8,24},{9,... | collective-permute-start | bytes 491528 | tf_op jit(solution)/shard_map/ppermute | solution.py:469
  134.4 5.6 %collective-permute-start.30 = (bf16[128,512]{1,0:T(8,128)(2,1)S(1)}, bf16[128,512]{1,0:T(8,128)(2,1)S(1)}, u32[]{:S(2)}, u32[]{:S(2)}) collective-permute-start(bf16[128,512]{1,0:T(8,128)(2,1)S(1)} %get-tuple-element.128.refs_1_), channel_id=1, source_target_pairs={{0,4},{1,5},{2,6},{3,7},{4,0},{5,1},{6,2},{7,3},{8,12},{9,13},{10,... | collective-permute-start | bytes 393224 | tf_op jit(solution)/shard_map/ppermute | solution.py:469
  135.7 6.1 %collective-permute-start.29 = (bf16[128,512]{1,0:T(8,128)(2,1)S(1)}, bf16[128,512]{1,0:T(8,128)(2,1)S(1)}, u32[]{:S(2)}, u32[]{:S(2)}) collective-permute-start(bf16[128,512]{1,0:T(8,128)(2,1)S(1)} %get-tuple-element.128.refs_1_), channel_id=1, source_target_pairs={{0,2},{1,3},{2,4},{3,5},{4,6},{5,7},{6,0},{7,1},{8,10},{9,11},{10,... | collective-permute-start | bytes 393224 | tf_op jit(solution)/shard_map/ppermute | solution.py:469
  142.4 8.5 %collective-permute-start.32 = (bf16[512,512]{1,0:T(8,128)(2,1)S(1)}, bf16[512,512]{1,0:T(8,128)(2,1)S(1)}, u32[]{:S(2)}, u32[]{:S(2)}) collective-permute-start(bf16[512,512]{1,0:T(8,128)(2,1)S(1)} %shard_map.125.refs_1_), channel_id=1, source_target_pairs={{0,1},{1,0},{2,3},{3,2},{4,5},{5,4},{6,7},{7,6},{8,9},{9,8},{10,11... | collective-permute-start | bytes 1572872 | tf_op jit(solution)/shard_map/ppermute | solution.py:469
  147.2 3.7 %collective-permute-start.36 = (bf16[512,512]{1,0:T(8,128)(2,1)S(1)}, bf16[512,512]{1,0:T(8,128)(2,1)S(1)}, u32[]{:S(2)}, u32[]{:S(2)}) collective-permute-start(bf16[512,512]{1,0:T(8,128)(2,1)S(1)} %get-tuple-element.130.refs_2_), channel_id=1, source_target_pairs={{0,1},{1,0},{2,3},{3,2},{4,5},{5,4},{6,7},{7,6},{8,9},{9,8},{10,11... | collective-permute-start | bytes 1572872 | tf_op jit(solution)/shard_map/ppermute | solution.py:469
where the time goes:
time: 153 us
  Pallas kernels  64.3 us (42%)
  starting transfers between devices  60.4 us (39%)
  waiting for transfers between devices  24.1 us (16%)
  local copies, waits for them, and re-layouts  3.13 us (2%)
    ppermute x31, starting transfers between devices, send(): return lax.ppermute(value, ('lat', 'lon'), pairs)  38.1 us
    pallas_call x1, Pallas kernels, per_device(): pl.pallas_call(lambda *refs: main_kernel(geo, heads, *refs), in_specs=[sm...  32.8 us
    ppermute x6, starting transfers between devices, moved(): return lax.ppermute(value, ('lat', 'lon'), pairs)  22.3 us
    ppermute x31, waiting for transfers between devices, send(): return lax.ppermute(value, ('lat', 'lon'), pairs)  21.9 us
    pallas_call x1, Pallas kernels, per_device(): call(lambda *refs: lookup_kernel(heads, *refs), [shape((heads, win, win),...  6.73 us
    pallas_call x2, Pallas kernels, layer_norm_back(): call(lambda *refs: back_kernel(geo, first, count, *refs), shape((count *...  6.2 us
    pallas_call x1, Pallas kernels, per_device(): call(lambda *refs: table_kernel(heads, *refs), shape((SMALL, width), F32)...  6 us
    pallas_call x2, Pallas kernels, write(): pl.pallas_call(lambda *refs: place_kernel(mine, *refs), out_shape=[shape(...  3.88 us
  transfers between devices with their start and end apart: 37, of which 15 were waited for; matrix products, arithmetic and copies ran while one was open for 0% of the time, Pallas kernels for 17%

commit v1 on v0

--- a/solution.py
+++ b/solution.py
@@ -88,7 +88,8 @@
         for part, (src, dst) in enumerate(
             (
                 (ref.at[:, 0:SH], top.at[which]),
-                (ref.at[:, SH : geo.rows, 0:16], left.at[which]),
+                (ref.at[0, SH : geo.rows, 0:16], left.at[which, 0]),
+                (ref.at[1, SH : geo.rows, 0:16], left.at[which, 1]),
             )
         ):
             copy = pltpu.make_async_copy(src, dst, sems.at[which, part])
@@ -160,15 +161,14 @@
     lax.fori_loop(0, win // 8, step, 0)
 
 
-def table_kernel(heads, idx_ref, sum_ref, gsum_ref, gain_ref, out_ref, acc, line):
+def table_sums(heads, first, count, idx_ref, sum_ref, acc):
     win = idx_ref.shape[0]
     rows = heads * BANDS
     iota = lax.broadcasted_iota(jnp.int32, (SPAN, win), 0)
     bands = lax.broadcasted_iota(jnp.int32, (BANDS, win), 0)
-    acc[...] = jnp.zeros_like(acc)
 
     def step(block, carry):
-        start = pl.multiple_of(block * 8, 8)
+        start = pl.multiple_of(first + block * 8, 8)
         band, place = band_of(idx_ref[pl.ds(start, 8), :])
         tops, rests = [], []
         for h in range(heads):
@@ -186,7 +186,17 @@
         acc[...] += total[:rows] + total[rows:]
         return carry
 
-    lax.fori_loop(0, win // 8, step, 0)
+    lax.fori_loop(0, count // 8, step, 0)
+
+
+def first_table_kernel(heads, count, idx_ref, sum_ref, out_ref):
+    out_ref[...] = jnp.zeros_like(out_ref)
+    table_sums(heads, 0, count, idx_ref, sum_ref, out_ref)
+
+
+def table_kernel(heads, first, idx_ref, sum_ref, part_ref, gsum_ref, gain_ref, out_ref, acc, line):
+    acc[...] = part_ref[...]
+    table_sums(heads, first, idx_ref.shape[0] - first, idx_ref, sum_ref, acc)
     for h in range(heads):
         for b in range(BANDS):
             line[h : h + 1, b * SPAN : (b + 1) * SPAN] = acc[h * BANDS + b : h * BANDS + b + 1, :]
@@ -562,24 +572,17 @@
 
 
 def merge_kernel(count, place, with_small, info_ref, *refs):
-    ins, outs = refs[:count], refs[count:]
-    out_ref = outs[0]
+    ins, out_ref = refs[:count], refs[count]
     width = out_ref.shape[1]
-    piece = out_ref.shape[0] // count
+    piece = width // count
     for k, ref in enumerate(ins):
         part = (info_ref[place] + (count - k)) & (count - 1)
         out_ref[pl.ds(pl.multiple_of(part * piece, 16), piece), :] = ref[0:piece]
     if with_small:
-        line_ref, gain_ref = outs[1:]
-        total = small_of(ins, piece)
-        more = line_ref.shape[1] - width
-        line_ref[:, 0:width] = total[0:8]
-        line_ref[:, width:] = total[8:, 0:more]
-        gain_ref[:, 0 : width - more] = total[8:9, more:]
-        gain_ref[:, width - more :] = total[9:10, more:]
-
-
-def place_kernel(mine, info_ref, a_ref, b_ref, *refs):
+        put_small(out_ref, width, small_of(ins, piece))
+
+
+def place_kernel(which, mine, info_ref, value_ref, *refs):
     gqkv_ref, gout_ref, hold, sems = refs[-4:]
     width = gout_ref.shape[1]
     core = info_ref[CORE]
@@ -587,27 +590,34 @@
     steps = 4
     rows = width // steps
 
-    def write(targets):
+    def write(target):
         copies = []
-        for which, ref in enumerate((a_ref, b_ref)):
-            for step in range(steps):
-                at = slice(step * rows, (step + 1) * rows)
-                hold[which, at] = ref[at].astype(F32)
-                copy = pltpu.make_async_copy(
-                    hold.at[which, at], targets[which].at[at], sems.at[which, step]
-                )
-                copy.start()
-                copies.append(copy)
+        for step in range(steps):
+            at = slice(step * rows, (step + 1) * rows)
+            hold[at] = value_ref[at].astype(F32)
+            copy = pltpu.make_async_copy(hold.at[at], target.at[at], sems.at[step])
+            copy.start()
+            copies.append(copy)
         for copy in copies:
             copy.wait()
 
     @pl.when(half == 0)
     def _():
-        write((gqkv_ref.at[:, 0:width], gqkv_ref.at[:, width : 2 * width]))
+        write(gqkv_ref.at[:, which * width : (which + 1) * width])
 
     @pl.when(half == 1)
     def _():
-        write((gqkv_ref.at[:, 2 * width :], gout_ref))
+        write(gqkv_ref.at[:, 2 * width :] if which == 0 else gout_ref)
+
+
+def last_small_kernel(mine_ref, got_ref, line_ref, gain_ref):
+    width = mine_ref.shape[1]
+    total = small_of((mine_ref, got_ref), width)
+    more = line_ref.shape[1] - width
+    line_ref[:, 0:width] = total[0:8]
+    line_ref[:, width:] = total[8:, 0:more]
+    gain_ref[:, 0 : width - more] = total[8:9, more:]
+    gain_ref[:, width - more :] = total[9:10, more:]
 
 
 def per_device(tokens, norm_gain, qkv_weight, out_weight, bias_table, bias_index, cotangent):
@@ -622,7 +632,7 @@
     rim = pl.pallas_call(
         lambda *refs: pack_kernel(geo, *refs),
         out_shape=[shape((n, width), BF16) for n in (n_rows, n_cols, n_corner)],
-        in_specs=[pl.BlockSpec(memory_space=pl.ANY)] * 2,
+        in_specs=[pl.BlockSpec(memory_space=pltpu.HBM)] * 2,
         out_specs=[pl.BlockSpec(memory_space=pltpu.VMEM)] * 3,
         scratch_shapes=[
             pltpu.VMEM((2, depth, SH, cols_lon, width), BF16),
@@ -630,7 +640,7 @@
             pltpu.VMEM((2, depth, SH, cols_lon, width), F32),
             pltpu.VMEM((2, depth, rows_lat - SH, 16, width), F32),
             pltpu.VMEM((n_rows + n_cols + n_corner, width), F32),
-            pltpu.SemaphoreType.DMA((2, 2)),
+            pltpu.SemaphoreType.DMA((2, 3)),
         ],
         compiler_params=pltpu.CompilerParams(vmem_limit_bytes=60 * MIB),
     )(tokens, cotangent)
@@ -655,7 +665,7 @@
     small_limit = 10 * MIB
 
     vmem, smem = pl.BlockSpec(memory_space=pltpu.VMEM), pl.BlockSpec(memory_space=pltpu.SMEM)
-    hbm = pl.BlockSpec(memory_space=pl.ANY)
+    hbm = pl.BlockSpec(memory_space=pltpu.HBM)
     send, keep, bias_sum, grad_proj, unit, inv, cot_win, gain_sum = pl.pallas_call(
         lambda *refs: main_kernel(geo, heads, *refs),
         in_specs=[smem] + [vmem] * 6 + [hbm, hbm, vmem],
@@ -693,6 +703,15 @@
     )(info, tok, cot, *rim, norm_gain.reshape(1, width), qkv_weight, out_weight, bias)
 
     got = chips.core(send)
+    first = win // 16 * 8
+    folded = call(
+        lambda *refs: first_table_kernel(heads, first, *refs),
+        shape((heads * BANDS, SPAN), F32),
+        [],
+        2,
+        small_limit,
+        cost=pl.CostEstimate(flops=2 * 10**9, bytes_accessed=10**6, transcendentals=0),
+    )(index_t, bias_sum)
     piece = half_rows // 2 // ny
     outs = call(
         lambda *refs: pair_sum_kernel(ny, nx, *refs),
@@ -701,20 +720,11 @@
         3,
         small_limit,
         smem_first=True,
-    )(info, keep, got)
-
-    outs, bias_sum = lax.optimization_barrier((outs, bias_sum))
+    )(info, *lax.optimization_barrier((keep, got, folded))[:2])
+
     got_a = [outs[0]] + [chips.y(outs[k], k) for k in range(1, ny)]
     got_b = [outs[ny]] + [chips.x(outs[ny + k], k) for k in range(1, nx)]
     gain_row = norm_gain.reshape(1, width)
-    small = call(
-        lambda *refs: table_kernel(heads, *refs),
-        shape((SMALL, width), F32),
-        [pltpu.VMEM((heads * BANDS, SPAN), F32), pltpu.VMEM((heads, BANDS * SPAN), F32)],
-        4,
-        small_limit,
-        cost=pl.CostEstimate(flops=3 * 10**9, bytes_accessed=10**6, transcendentals=0),
-    )(index_t, bias_sum, gain_sum, gain_row)
     outs = call(
         lambda *refs: cross_sum_kernel(ny, nx, *refs),
         [shape((piece // nx, width), BF16)] * nx + [shape((piece // ny, width), BF16)] * ny,
@@ -724,9 +734,17 @@
         smem_first=True,
     )(info, *got_a, *got_b)
 
+    outs, bias_sum = lax.optimization_barrier((outs, bias_sum))
     got_a = [outs[0]] + [chips.x(outs[k], k) for k in range(1, nx)]
     got_b = [outs[nx]] + [chips.y(outs[nx + k], k) for k in range(1, ny)]
-    small = small + chips.core(small)
+    small = call(
+        lambda *refs: table_kernel(heads, first, *refs),
+        shape((SMALL, width), F32),
+        [pltpu.VMEM((heads * BANDS, SPAN), F32), pltpu.VMEM((heads, BANDS * SPAN), F32)],
+        5,
+        small_limit,
+        cost=pl.CostEstimate(flops=2 * 10**9, bytes_accessed=10**6, transcendentals=0),
+    )(index_t, bias_sum, folded, gain_sum, gain_row)
     part = piece // nx
     mine = call(
         lambda *refs: join_sum_kernel(ny, nx, *refs),
@@ -747,13 +765,16 @@
         )(proj, unit, inv, cot_win, gain_row, qkv_weight)
 
     half_wins = geo.nwin // 2
-    mine, grad_proj = lax.optimization_barrier((mine, grad_proj))
+    mine, grad_proj, qkv_weight = lax.optimization_barrier((mine, grad_proj, qkv_weight))
     got = chips.z(mine, 1)
     low = layer_norm_back(0, half_wins, grad_proj)
     mine = call(z_sum_kernel, shape(mine.shape, BF16), [], 2, small_limit)(mine, got)
     mine, grad_proj = lax.optimization_barrier((mine, grad_proj))
     got = chips.z(mine, 2)
     high = layer_norm_back(half_wins, geo.nwin - half_wins, grad_proj)
+    mine = call(z_sum_kernel, shape(mine.shape, BF16), [], 2, small_limit)(mine, got)
+    mine, low, high = lax.optimization_barrier((mine, low, high))
+    got = chips.z(mine, 4)
     b_rows, b_cols, b_corner = pad16(geo.n_rows), pad16(geo.n_cols), pad16(geo.n_corner)
     back = call(
         lambda *refs: unpack_send_kernel(geo, *refs),
@@ -765,10 +786,8 @@
         2,
         small_limit,
     )(low, high)
-    mine = call(z_sum_kernel, shape(mine.shape, BF16), [], 2, small_limit)(mine, got)
-    mine, back = lax.optimization_barrier((mine, back))
-    got = chips.z(mine, 4)
     back = (moved(back[0], -1, 0), moved(back[1], 0, -1), moved(back[2], -1, -1))
+    got, back = lax.optimization_barrier((got, back))
     own_a, own_b = call(
         z_sum_kernel,
         [shape((part, width), BF16), shape((part + 2 * SMALL, width), BF16)],
@@ -803,45 +822,49 @@
         5,
         small_limit,
     )(low, high, *back)
+    own_a, grad_tokens = lax.optimization_barrier((own_a, grad_tokens))
+    got_a[0] = own_a
     mine_a = call(
         lambda *refs: merge_kernel(ny, Y, False, *refs),
-        [shape((width, width), BF16)],
+        shape((width, width), BF16),
         [],
         1 + ny,
         small_limit,
         smem_first=True,
-    )(info, *got_a)[0]
+    )(info, *got_a)
     their_a = chips.core(mine_a)
-    mine_b, line, grad_gain = call(
+
+    def write(which, mine, value, written):
+        return pl.pallas_call(
+            lambda *refs: place_kernel(which, mine, *refs),
+            out_shape=[shape((width, 3 * width), F32), shape((width, width), F32)],
+            in_specs=[smem, vmem] + [hbm] * len(written),
+            out_specs=[hbm, hbm],
+            input_output_aliases={2 + i: i for i in range(len(written))},
+            scratch_shapes=[pltpu.VMEM((width, width), F32), pltpu.SemaphoreType.DMA((4,))],
+            compiler_params=pltpu.CompilerParams(vmem_limit_bytes=small_limit),
+        )(info, value, *written)
+
+    written = write(0, True, mine_a, ())
+    mine_b = call(
         lambda *refs: merge_kernel(nx, X, True, *refs),
-        [
-            shape((width, width), BF16),
-            shape((heads, BANDS * SPAN), F32),
-            shape((1, width), F32),
-        ],
+        shape((width + 2 * SMALL, width), BF16),
         [],
         1 + nx,
         small_limit,
         smem_first=True,
     )(info, *got_b)
     their_b = chips.core(mine_b)
-
-    def write(mine, a, b, written):
-        return pl.pallas_call(
-            lambda *refs: place_kernel(mine, *refs),
-            out_shape=[shape((width, 3 * width), F32), shape((width, width), F32)],
-            in_specs=[smem, vmem, vmem] + [hbm] * len(written),
-            out_specs=[hbm, hbm],
-            input_output_aliases={3 + i: i for i in range(len(written))},
-            scratch_shapes=[
-                pltpu.VMEM((2, width, width), F32),
-                pltpu.SemaphoreType.DMA((2, 4)),
-            ],
-            compiler_params=pltpu.CompilerParams(vmem_limit_bytes=small_limit),
-        )(info, a, b, *written)
-
-    written = write(True, mine_a, mine_b, ())
-    grad_qkv, grad_out = write(False, their_a, their_b, tuple(written))
+    written = write(1, True, mine_b, tuple(written))
+    written = write(0, False, their_a, tuple(written))
+    line, grad_gain = call(
+        last_small_kernel,
+        [shape((heads, BANDS * SPAN), F32), shape((1, width), F32)],
+        [],
+        2,
+        small_limit,
+    )(mine_b, their_b)
+    grad_qkv, grad_out = write(1, False, their_b, tuple(written))
     grad_bias = line.T[:entries]
     return (grad_tokens.reshape(tokens.shape), grad_qkv, grad_out, grad_bias, grad_gain.reshape(width))
 

time: 153 us -> 151 us (0.987)
  waiting for transfers between devices: 24.1 us -> 17.5 us
  Pallas kernels: 64.3 us -> 66.6 us
    ppermute x31 -> x30, waiting for transfers between devices: 21.9 us -> 9.33 us  [send(): return lax.ppermute(value, ('lat', 'lon'), pairs)]
    ppermute x6, waiting for transfers between devices: 2.14 us -> 8.22 us  [moved(): return lax.ppermute(value, ('lat', 'lon'), pairs)]
    ppermute x31 -> x30, starting transfers between devices: 38.1 us -> 43 us  [send(): return lax.ppermute(value, ('lat', 'lon'), pairs)]
    ppermute x6, starting transfers between devices: 22.3 us -> 18.7 us  [moved(): return lax.ppermute(value, ('lat', 'lon'), pairs)]
    pallas_call x5 -> x9, Pallas kernels: 11.7 us -> 14 us  [the longest x4 6.25 us: write(): pl.pallas_call(lambda *refs: place_kernel(which, mine, *refs), out_shape=...]
  transfers between devices with their start and end apart: 37 -> 36, of which waited for: 15 -> 8; matrix products, arithmetic and copies ran while one was open for 0% -> 0% of each run, Pallas kernels for 17% -> 18%
where the time goes in v1:
time: 151 us; the launch traced here: 150 us
  Pallas kernels  66.6 us (44%)
  starting transfers between devices  61.7 us (41%)
  waiting for transfers between devices  17.5 us (12%)
  local copies, waits for them, and re-layouts  3.13 us (2%)
    ppermute x30, starting transfers between devices, send(): return lax.ppermute(value, ('lat', 'lon'), pairs)  43 us
    pallas_call x1, Pallas kernels, per_device(): pl.pallas_call(lambda *refs: main_kernel(geo, heads, *refs), in_specs=[sm...  32.8 us
    ppermute x6, starting transfers between devices, moved(): return lax.ppermute(value, ('lat', 'lon'), pairs)  18.7 us
    ppermute x30, waiting for transfers between devices, send(): return lax.ppermute(value, ('lat', 'lon'), pairs)  9.33 us
    ppermute x6, waiting for transfers between devices, moved(): return lax.ppermute(value, ('lat', 'lon'), pairs)  8.22 us
    pallas_call x1, Pallas kernels, per_device(): call(lambda *refs: lookup_kernel(heads, *refs), [shape((heads, win, win),...  6.72 us
    pallas_call x4, Pallas kernels, write(): pl.pallas_call(lambda *refs: place_kernel(which, mine, *refs), out_shape=...  6.25 us
    pallas_call x2, Pallas kernels, layer_norm_back(): call(lambda *refs: back_kernel(geo, first, count, *refs), shape((count *...  6.19 us
  transfers between devices with their start and end apart: 36, of which 8 were waited for; matrix products, arithmetic and copies ran while one was open for 0% of the time, Pallas kernels for 18%

profile of v1, /device:TPU:1, one launch (start us, length us, event | category | flops | bytes accessed | tf_op | source)
XLA Modules:
  0.0 150.2 jit_solution(3042971091881659305)
XLA Ops:
  0.7 2.7 %shard_map.110 = (bf16[224,512]{1,0:T(8,128)(2,1)}, bf16[512,512]{1,0:T(8,128)(2,1)}, bf16[80,512]{1,0:T(8,128)(2,1)}) custom-call(bf16[2,24,24,512]{3,2,1,0:T(8,128)(2,1)} %refs_0_.2, bf16[2,24,24,512]{3,2,1,0:T(8,128)(2,1)} %refs_1_.1), custom_call_target="tpu_custom_call" | custom-call | tf_op jit(solution)/shard_map/pallas_call | solution.py:632
  3.3 3.3 %collective-permute-start.1 = (bf16[512,512]{1,0:T(8,128)(2,1)}, bf16[512,512]{1,0:T(8,128)(2,1)}, u32[]{:S(2)}, u32[]{:S(2)}) collective-permute-start(bf16[512,512]{1,0:T(8,128)(2,1)} %get-tuple-element.83), channel_id=1, source_target_pairs={{0,15},{1,0},{2,1},{3,2},{4,3},{5,4},{6,5},{7,6},{8,7},{9,8},{10,9... | collective-permute-start | bytes 1572872 | tf_op jit(solution)/shard_map/ppermute | solution.py:458
  6.6 8.7 %collective-permute-start.2 = (bf16[80,512]{1,0:T(8,128)(2,1)}, bf16[80,512]{1,0:T(8,128)(2,1)}, u32[]{:S(2)}, u32[]{:S(2)}) collective-permute-start(bf16[80,512]{1,0:T(8,128)(2,1)} %get-tuple-element.84), channel_id=1, source_target_pairs={{0,255},{1,240},{2,241},{3,242},{4,243},{5,244},{6,245},{7,246},{8... | collective-permute-start | bytes 245768 | tf_op jit(solution)/shard_map/ppermute | solution.py:458
  15.3 1.2 collective-permute-start
  16.5 6.7 %shard_map.111 = (f32[8,144,144]{2,1,0:T(8,128)S(1)}, s32[144,144]{1,0:T(8,128)S(1)}) custom-call(s32[144,144]{1,0:T(8,128)S(1)} %copy-done.5, f32[8,759]{1,0:T(8,128)S(1)} %bitcast.18), custom_call_target="tpu_custom_call" | custom-call | flops 4000000000 | bytes 1000000 | tf_op jit(solution)/shard_map/pallas_call | solution.py:649
  24.0 1.4 copy-done.2
  25.4 1.0 copy-done.3
  26.5 32.8 %shard_map.112 = (bf16[1024,512]{1,0:T(8,128)(2,1)S(1)}, bf16[1024,512]{1,0:T(8,128)(2,1)S(1)}, f32[8,144,144]{2,1,0:T(8,128)S(1)}, bf16[1152,1536]{1,0:T(8,128)...) custom-call(s32[4]{0:T(128)S(1)} %pad_add_fusion.refs_0_, ...), custom_call_target="tpu_custom_call" | custom-call | tf_op jit(solution)/shard_map/pallas_call | solution.py:669
  59.3 2.9 %shard_map.113.refs_2_ = f32[64,96]{1,0:T(8,128)S(1)} custom-call(s32[144,144]{1,0:T(8,128)S(1)} %copy-done.8, f32[8,144,144]{2,1,0:T(8,128)S(1)} %get-tuple-element.116.refs_1_), custom_call_target="tpu_custom_call" | custom-call | flops 2000000000 | bytes 1000000 | tf_op jit(solution)/shard_map/pallas_call | solution.py:707
  62.3 0.8 shard_map.114
  63.1 2.5 %collective-permute-start.5 = (bf16[128,512]{1,0:T(8,128)(2,1)S(1)}, bf16[128,512]{1,0:T(8,128)(2,1)S(1)}, u32[]{:S(2)}, u32[]{:S(2)}) collective-permute-start(bf16[128,512]{1,0:T(8,128)(2,1)S(1)} %get-tuple-element.94), channel_id=1, source_target_pairs={{0,4},{1,5},{2,6},{3,7},{4,0},{5,1},{6,2},{7,3},{8,12},{9,13},{10,... | collective-permute-start | bytes 393224 | tf_op jit(solution)/shard_map/ppermute | solution.py:479
  65.8 0.8 collective-permute-start.7
  66.6 1.8 %collective-permute-start.8 = (bf16[128,512]{1,0:T(8,128)(2,1)S(1)}, bf16[128,512]{1,0:T(8,128)(2,1)S(1)}, u32[]{:S(2)}, u32[]{:S(2)}) collective-permute-start(bf16[128,512]{1,0:T(8,128)(2,1)S(1)} %get-tuple-element.98), channel_id=1, source_target_pairs={{0,8},{1,9},{2,10},{3,11},{4,12},{5,13},{6,14},{7,15},{8,0},{9,1},... | collective-permute-start | bytes 393224 | tf_op jit(solution)/shard_map/ppermute | solution.py:479
  68.4 0.7 collective-permute-done.4.refs_2_
  69.0 3.6 %collective-permute-start.9 = (bf16[128,512]{1,0:T(8,128)(2,1)S(1)}, bf16[128,512]{1,0:T(8,128)(2,1)S(1)}, u32[]{:S(2)}, u32[]{:S(2)}) collective-permute-start(bf16[128,512]{1,0:T(8,128)(2,1)S(1)} %get-tuple-element.99), channel_id=1, source_target_pairs={{0,24},{1,25},{2,26},{3,27},{4,28},{5,29},{6,30},{7,31},{8,16},{9,... | collective-permute-start | bytes 393224 | tf_op jit(solution)/shard_map/ppermute | solution.py:479
  72.6 1.3 collective-permute-done.8.refs_7_
  74.0 1.4 collective-permute-done.9.refs_8_
  75.4 0.7 shard_map.115
  76.1 2.7 %collective-permute-start.10 = (bf16[32,512]{1,0:T(8,128)(2,1)S(1)}, bf16[32,512]{1,0:T(8,128)(2,1)S(1)}, u32[]{:S(2)}, u32[]{:S(2)}) collective-permute-start(bf16[32,512]{1,0:T(8,128)(2,1)S(1)} %get-tuple-element.109), channel_id=1, source_target_pairs={{0,16},{1,17},{2,18},{3,19},{4,20},{5,21},{6,22},{7,23},{8,24},{9,... | collective-permute-start | bytes 98312 | tf_op jit(solution)/shard_map/ppermute | solution.py:479
  78.9 0.8 collective-permute-start.11
  79.6 1.7 %collective-permute-start.12 = (bf16[32,512]{1,0:T(8,128)(2,1)S(1)}, bf16[32,512]{1,0:T(8,128)(2,1)S(1)}, u32[]{:S(2)}, u32[]{:S(2)}) collective-permute-start(bf16[32,512]{1,0:T(8,128)(2,1)S(1)} %get-tuple-element.111), channel_id=1, source_target_pairs={{0,24},{1,25},{2,26},{3,27},{4,28},{5,29},{6,30},{7,31},{8,16},{9,... | collective-permute-start | bytes 98312 | tf_op jit(solution)/shard_map/ppermute | solution.py:479
  81.4 1.4 collective-permute-start.14
  82.7 1.3 collective-permute-start.15
  84.0 3.1 %shard_map.116.refs_8_ = f32[16,512]{1,0:T(8,128)S(1)} custom-call(s32[144,144]{1,0:T(8,128)S(1)} %copy-done.8, f32[8,144,144]{2,1,0:T(8,128)S(1)} %get-tuple-element.116.refs_1_, f32[64,96]{1,0:T(8,128)S(1)} %shard_map.113.refs_2_, f32[512,128]{1,0:T(8,128)S(1)} %get-tuple-element.117.refs_3_, f32[1,512]{1,0:T(1,128)S(1)} %bitcast.15), custom_call_target="tpu_custom_call" | custom-call | flops 2000000000 | bytes 1000000 | tf_op jit(solution)/shard_map/pallas_call | solution.py:740
  87.2 1.6 %collective-permute-start.16 = (bf16[96,512]{1,0:T(8,128)(2,1)S(1)}, bf16[96,512]{1,0:T(8,128)(2,1)S(1)}, u32[]{:S(2)}, u32[]{:S(2)}) collective-permute-start(bf16[96,512]{1,0:T(8,128)(2,1)S(1)} %shard_map.117.mine_ref), channel_id=1, source_target_pairs={{0,32},{1,33},{2,34},{3,35},{4,36},{5,37},{6,38},{7,39},{8,40},{9,... | collective-permute-start | bytes 294920 | tf_op jit(solution)/shard_map/ppermute | solution.py:479
  88.8 3.1 %shard_map.120.refs_0_ = bf16[576,512]{1,0:T(8,128)(2,1)S(1)} custom-call(bf16[1152,1536]{1,0:T(8,128)(2,1)S(1)} %get-tuple-element.126.refs_0_, f32[1152,512]{1,0:T(8,128)S(1)} %get-tuple-element.122.refs_1_, f32[1152,128]{1,0:T(8,128)S(1)} %get-tuple-element.123.refs_2_, bf16[1152,512]{1,0:T(8,128)(2,1)S(1)} %get-tuple-element.124.refs_3_, ...), custom_call_target="tpu_custom_call" | custom-call | flops 3000000000 | bytes 10000000 | tf_op jit(solution)/shard_map/pallas_call | solution.py:758
  91.9 3.1 %collective-permute-start.17 = (bf16[96,512]{1,0:T(8,128)(2,1)S(1)}, bf16[96,512]{1,0:T(8,128)(2,1)S(1)}, u32[]{:S(2)}, u32[]{:S(2)}) collective-permute-start(bf16[96,512]{1,0:T(8,128)(2,1)S(1)} %shard_map.118.mine_ref), channel_id=1, source_target_pairs={{0,96},{1,97},{2,98},{3,99},{4,100},{5,101},{6,102},{7,103},{8,104... | collective-permute-start | bytes 294920 | tf_op jit(solution)/shard_map/ppermute | solution.py:479
  95.1 3.1 %shard_map.121.refs_1_ = bf16[576,512]{1,0:T(8,128)(2,1)S(1)} custom-call(bf16[1152,1536]{1,0:T(8,128)(2,1)S(1)} %get-tuple-element.126.refs_0_, f32[1152,512]{1,0:T(8,128)S(1)} %get-tuple-element.122.refs_1_, f32[1152,128]{1,0:T(8,128)S(1)} %get-tuple-element.123.refs_2_, bf16[1152,512]{1,0:T(8,128)(2,1)S(1)} %get-tuple-element.124.refs_3_, ...), custom_call_target="tpu_custom_call" | custom-call | flops 3000000000 | bytes 10000000 | tf_op jit(solution)/shard_map/pallas_call | solution.py:758
  98.5 4.7 %collective-permute-start.20 = (bf16[256,512]{1,0:T(8,128)(2,1)S(1)}, bf16[256,512]{1,0:T(8,128)(2,1)S(1)}, u32[]{:S(2)}, u32[]{:S(2)}) collective-permute-start(bf16[256,512]{1,0:T(8,128)(2,1)S(1)} %get-tuple-element.131), channel_id=1, source_target_pairs={{0,1},{1,2},{2,3},{3,4},{4,5},{5,6},{6,7},{7,8},{8,9},{9,10},{10,1... | collective-permute-start | bytes 786440 | tf_op jit(solution)/shard_map/ppermute | solution.py:458
  103.9 4.2 %collective-permute-start.18 = (bf16[96,512]{1,0:T(8,128)(2,1)S(1)}, bf16[96,512]{1,0:T(8,128)(2,1)S(1)}, u32[]{:S(2)}, u32[]{:S(2)}) collective-permute-start(bf16[96,512]{1,0:T(8,128)(2,1)S(1)} %shard_map.119.mine_ref), channel_id=1, source_target_pairs={{0,224},{1,225},{2,226},{3,227},{4,228},{5,229},{6,230},{7,231},{8... | collective-permute-start | bytes 294920 | tf_op jit(solution)/shard_map/ppermute | solution.py:479
  108.3 8.2 %collective-permute-done.21.refs_4_ = bf16[48,512]{1,0:T(8,128)(2,1)S(1)} collective-permute-done((bf16[48,512]{1,0:T(8,128)(2,1)S(1)}, bf16[48,512]{1,0:T(8,128)(2,1)S(1)}, u32[]{:S(2)}, u32[]{:S(2)}) %collective-permute-start.21) | collective-permute-done | bytes 49184 | tf_op jit(solution)/shard_map/ppermute | solution.py:458
  116.7 2.2 %collective-permute-start.27 = (bf16[64,512]{1,0:T(8,128)(2,1)S(1)}, bf16[64,512]{1,0:T(8,128)(2,1)S(1)}, u32[]{:S(2)}, u32[]{:S(2)}) collective-permute-start(bf16[64,512]{1,0:T(8,128)(2,1)S(1)} %get-tuple-element.135.refs_5_), channel_id=1, source_target_pairs={{0,6},{1,7},{2,0},{3,1},{4,2},{5,3},{6,4},{7,5},{8,14},{9,15},{10,... | collective-permute-start | bytes 196616 | tf_op jit(solution)/shard_map/ppermute | solution.py:479
  119.6 1.6 %collective-permute-start.23 = (bf16[32,512]{1,0:T(8,128)(2,1)S(1)}, bf16[32,512]{1,0:T(8,128)(2,1)S(1)}, u32[]{:S(2)}, u32[]{:S(2)}) collective-permute-start(bf16[32,512]{1,0:T(8,128)(2,1)S(1)} %get-tuple-element.134.refs_1_), channel_id=1, source_target_pairs={{0,8},{1,9},{2,10},{3,11},{4,12},{5,13},{6,14},{7,15},{8,0},{9,1},... | collective-permute-start | bytes 98312 | tf_op jit(solution)/shard_map/ppermute | solution.py:479
  121.2 0.7 collective-permute-start.22
  121.9 2.0 %collective-permute-done.23.refs_3_ = bf16[32,512]{1,0:T(8,128)(2,1)S(1)} collective-permute-done((bf16[32,512]{1,0:T(8,128)(2,1)S(1)}, bf16[32,512]{1,0:T(8,128)(2,1)S(1)}, u32[]{:S(2)}, u32[]{:S(2)}) %collective-permute-start.23) | collective-permute-done | bytes 32800 | tf_op jit(solution)/shard_map/ppermute | solution.py:479
  123.9 1.3 collective-permute-done.22.refs_2_
  125.8 1.3 collective-permute-start.30
  127.1 0.9 collective-permute-start.29
  128.0 2.3 %collective-permute-start.34 = (bf16[128,512]{1,0:T(8,128)(2,1)S(1)}, bf16[128,512]{1,0:T(8,128)(2,1)S(1)}, u32[]{:S(2)}, u32[]{:S(2)}) collective-permute-start(bf16[128,512]{1,0:T(8,128)(2,1)S(1)} %get-tuple-element.148.refs_1_), channel_id=1, source_target_pairs={{0,6},{1,7},{2,0},{3,1},{4,2},{5,3},{6,4},{7,5},{8,14},{9,15},{10,... | collective-permute-start | bytes 393224 | tf_op jit(solution)/shard_map/ppermute | solution.py:479
  130.3 1.4 collective-permute-start.33
  132.0 0.9 collective-permute-done.29.refs_3_
  132.9 1.7 %collective-permute-done.28.refs_2_ = bf16[160,512]{1,0:T(8,128)(2,1)S(1)} collective-permute-done((bf16[160,512]{1,0:T(8,128)(2,1)S(1)}, bf16[160,512]{1,0:T(8,128)(2,1)S(1)}, u32[]{:S(2)}, u32[]{:S(2)}) %collective-permute-start.28) | collective-permute-done | bytes 163872 | tf_op jit(solution)/shard_map/ppermute | solution.py:479
  135.1 5.0 %collective-permute-start.31 = (bf16[544,512]{1,0:T(8,128)(2,1)S(1)}, bf16[544,512]{1,0:T(8,128)(2,1)S(1)}, u32[]{:S(2)}, u32[]{:S(2)}) collective-permute-start(bf16[544,512]{1,0:T(8,128)(2,1)S(1)} %shard_map.126.refs_1_.mine_ref), channel_id=1, source_target_pairs={{0,1},{1,0},{2,3},{3,2},{4,5},{5,4},{6,7},{7,6},{8,9},{9,8},{10,11... | collective-permute-start | bytes 1671176 | tf_op jit(solution)/shard_map/ppermute | solution.py:479
  140.2 1.7 %shard_map.125 = bf16[1152,512]{1,0:T(8,128)(2,1)} custom-call(bf16[576,512]{1,0:T(8,128)(2,1)S(1)} %shard_map.120.refs_0_, bf16[576,512]{1,0:T(8,128)(2,1)S(1)} %shard_map.121.refs_1_, bf16[112,512]{1,0:T(8,128)(2,1)S(1)} %collective-permute-done.19.refs_2_, bf16[256,512]{1,0:T(8,128)(2,1)S(1)} %collective-permute-done.20.refs_3_, ...), custom_call_target="tpu_custom_call" | custom-call | tf_op jit(solution)/shard_map/pallas_call | solution.py:812
  143.1 1.6 %shard_map.128 = (f32[512,1536]{1,0:T(8,128)}, f32[512,512]{1,0:T(8,128)}) custom-call(s32[4]{0:T(128)S(1)} %pad_add_fusion.refs_0_, bf16[512,512]{1,0:T(8,128)(2,1)S(1)} %shard_map.127.refs_1_), custom_call_target="tpu_custom_call" | custom-call | tf_op jit(solution)/shard_map/pallas_call | solution.py:838
  144.7 1.6 %shard_map.129 = (f32[512,1536]{1,0:T(8,128)}, f32[512,512]{1,0:T(8,128)}) custom-call(s32[4]{0:T(128)S(1)} %pad_add_fusion.refs_0_, bf16[544,512]{1,0:T(8,128)(2,1)S(1)} %shard_map.126.refs_1_.mine_ref, f32[512,1536]{1,0:T(8,128)} %get-tuple-element.149.refs_2_, f32[512,512]{1,0:T(8,128)} %get-tuple-element.150.refs_3_), custom_call_target="tpu_custom_call", output_to_operand_aliasing={{0}: (2, {}), {1}: (3, {})} | custom-call | tf_op jit(solution)/shard_map/pallas_call | solution.py:838
  146.3 1.6 %shard_map.130 = (f32[512,1536]{1,0:T(8,128)}, f32[512,512]{1,0:T(8,128)}) custom-call(s32[4]{0:T(128)S(1)} %pad_add_fusion.refs_0_, bf16[512,512]{1,0:T(8,128)(2,1)S(1)} %collective-permute-done.35.refs_1_, f32[512,1536]{1,0:T(8,128)} %get-tuple-element.151.refs_2_, f32[512,512]{1,0:T(8,128)} %get-tuple-element.152.refs_3_), custom_call_target="tpu_custom_call", output_to_operand_aliasing={{0}: (2, {}), {1}: (3, {})} | custom-call | tf_op jit(solution)/shard_map/pallas_call | solution.py:838
  148.5 1.6 %shard_map.131 = (f32[512,1536]{1,0:T(8,128)}, f32[512,512]{1,0:T(8,128)}) custom-call(s32[4]{0:T(128)S(1)} %pad_add_fusion.refs_0_, bf16[544,512]{1,0:T(8,128)(2,1)S(1)} %collective-permute-done.31.refs_1_.got_ref, f32[512,1536]{1,0:T(8,128)} %get-tuple-element.153.refs_2_, ...), custom_call_target="tpu_custom_call", output_to_operand_aliasing={{0}: (2, {}), {1}: (3, {})} | custom-call | tf_op jit(solution)/shard_map/pallas_call | solution.py:838
  (66 shorter events, 6.6 us)
Async XLA Ops:
  0.6 15.8 %copy-start.5 = (s32[144,144]{1,0:T(8,128)S(1)}, s32[144,144]{1,0:T(8,128)}, u32[]{:S(2)}) copy-start(s32[144,144]{1,0:T(8,128)} %refs_0_.3) | copy-start | bytes 248836
  0.6 15.8 %copy-start.6 = (f32[759,8]{0,1:T(8,128)S(1)}, f32[759,8]{0,1:T(8,128)}, u32[]{:S(2)}) copy-start(f32[759,8]{0,1:T(8,128)} %param.11) | copy-start | bytes 72868
  3.3 20.6 %collective-permute-start.1 = (bf16[512,512]{1,0:T(8,128)(2,1)}, bf16[512,512]{1,0:T(8,128)(2,1)}, u32[]{:S(2)}, u32[]{:S(2)}) collective-permute-start(bf16[512,512]{1,0:T(8,128)(2,1)} %get-tuple-element.83), channel_id=1, source_target_pairs={{0,15},{1,0},{2,1},{3,2},{4,3},{5,4},{6,5},{7,6},{8,7},{9,8},{10,9... | collective-permute-start | bytes 1572872 | tf_op jit(solution)/shard_map/ppermute | solution.py:458
  6.6 17.3 %collective-permute-start.2 = (bf16[80,512]{1,0:T(8,128)(2,1)}, bf16[80,512]{1,0:T(8,128)(2,1)}, u32[]{:S(2)}, u32[]{:S(2)}) collective-permute-start(bf16[80,512]{1,0:T(8,128)(2,1)} %get-tuple-element.84), channel_id=1, source_target_pairs={{0,255},{1,240},{2,241},{3,242},{4,243},{5,244},{6,245},{7,246},{8... | collective-permute-start | bytes 245768 | tf_op jit(solution)/shard_map/ppermute | solution.py:458
  15.3 8.7 %collective-permute-start = (bf16[224,512]{1,0:T(8,128)(2,1)}, bf16[224,512]{1,0:T(8,128)(2,1)}, u32[]{:S(2)}, u32[]{:S(2)}) collective-permute-start(bf16[224,512]{1,0:T(8,128)(2,1)} %get-tuple-element.82), channel_id=1, source_target_pairs={{0,240},{1,241},{2,242},{3,243},{4,244},{5,245},{6,246},{7,247},{8... | collective-permute-start | bytes 688136 | tf_op jit(solution)/shard_map/ppermute | solution.py:458
  16.5 7.5 %copy-start = (bf16[2,24,24,512]{3,2,1,0:T(8,128)(2,1)S(1)}, bf16[2,24,24,512]{3,2,1,0:T(8,128)(2,1)}, u32[]{:S(2)}) copy-start(bf16[2,24,24,512]{3,2,1,0:T(8,128)(2,1)} %refs_0_.2) | copy-start | bytes 3538948
  16.5 7.5 %copy-start.1 = (bf16[2,24,24,512]{3,2,1,0:T(8,128)(2,1)S(1)}, bf16[2,24,24,512]{3,2,1,0:T(8,128)(2,1)}, u32[]{:S(2)}) copy-start(bf16[2,24,24,512]{3,2,1,0:T(8,128)(2,1)} %refs_1_.1) | copy-start | bytes 3538948
  16.5 7.5 %copy-start.4 = (f32[512]{0:T(512)S(1)}, f32[512]{0:T(512)}, u32[]{:S(2)}) copy-start(f32[512]{0:T(512)} %param.8) | copy-start | bytes 6148
  23.2 0.7 copy-start.7
  24.0 1.4 copy-start.2
  25.4 1.0 copy-start.3
  26.4 32.9 %copy-start.8 = (s32[144,144]{1,0:T(8,128)S(1)}, s32[144,144]{1,0:T(8,128)}, u32[]{:S(2)}) copy-start(s32[144,144]{1,0:T(8,128)} %copy-done.7) | copy-start | bytes 248836
  59.2 3.0 %collective-permute-start.3 = (bf16[1024,512]{1,0:T(8,128)(2,1)S(1)}, bf16[1024,512]{1,0:T(8,128)(2,1)S(1)}, u32[]{:S(2)}, u32[]{:S(2)}) collective-permute-start(bf16[1024,512]{1,0:T(8,128)(2,1)S(1)} %get-tuple-element.87), channel_id=1, source_target_pairs={{0,1},{1,0},{2,3},{3,2},{4,5},{5,4},{6,7},{7,6},{8,9},{9,8},{10,11... | collective-permute-start | bytes 3145736 | tf_op jit(solution)/shard_map/ppermute | solution.py:479
  63.0 6.0 %collective-permute-start.4 = (bf16[128,512]{1,0:T(8,128)(2,1)S(1)}, bf16[128,512]{1,0:T(8,128)(2,1)S(1)}, u32[]{:S(2)}, u32[]{:S(2)}) collective-permute-start(bf16[128,512]{1,0:T(8,128)(2,1)S(1)} %get-tuple-element.93), channel_id=1, source_target_pairs={{0,2},{1,3},{2,4},{3,5},{4,6},{5,7},{6,0},{7,1},{8,10},{9,11},{10,... | collective-permute-start | bytes 393224 | tf_op jit(solution)/shard_map/ppermute | solution.py:479
  63.1 9.5 %collective-permute-start.5 = (bf16[128,512]{1,0:T(8,128)(2,1)S(1)}, bf16[128,512]{1,0:T(8,128)(2,1)S(1)}, u32[]{:S(2)}, u32[]{:S(2)}) collective-permute-start(bf16[128,512]{1,0:T(8,128)(2,1)S(1)} %get-tuple-element.94), channel_id=1, source_target_pairs={{0,4},{1,5},{2,6},{3,7},{4,0},{5,1},{6,2},{7,3},{8,12},{9,13},{10,... | collective-permute-start | bytes 393224 | tf_op jit(solution)/shard_map/ppermute | solution.py:479
  65.7 7.0 %collective-permute-start.6 = (bf16[128,512]{1,0:T(8,128)(2,1)S(1)}, bf16[128,512]{1,0:T(8,128)(2,1)S(1)}, u32[]{:S(2)}, u32[]{:S(2)}) collective-permute-start(bf16[128,512]{1,0:T(8,128)(2,1)S(1)} %get-tuple-element.95), channel_id=1, source_target_pairs={{0,6},{1,7},{2,0},{3,1},{4,2},{5,3},{6,4},{7,5},{8,14},{9,15},{10,... | collective-permute-start | bytes 393224 | tf_op jit(solution)/shard_map/ppermute | solution.py:479
  65.8 6.8 %collective-permute-start.7 = (bf16[128,512]{1,0:T(8,128)(2,1)S(1)}, bf16[128,512]{1,0:T(8,128)(2,1)S(1)}, u32[]{:S(2)}, u32[]{:S(2)}) collective-permute-start(bf16[128,512]{1,0:T(8,128)(2,1)S(1)} %get-tuple-element.97), channel_id=1, source_target_pairs={{0,16},{1,17},{2,18},{3,19},{4,20},{5,21},{6,22},{7,23},{8,24},{9,... | collective-permute-start | bytes 393224 | tf_op jit(solution)/shard_map/ppermute | solution.py:479
  66.6 7.4 %collective-permute-start.8 = (bf16[128,512]{1,0:T(8,128)(2,1)S(1)}, bf16[128,512]{1,0:T(8,128)(2,1)S(1)}, u32[]{:S(2)}, u32[]{:S(2)}) collective-permute-start(bf16[128,512]{1,0:T(8,128)(2,1)S(1)} %get-tuple-element.98), channel_id=1, source_target_pairs={{0,8},{1,9},{2,10},{3,11},{4,12},{5,13},{6,14},{7,15},{8,0},{9,1},... | collective-permute-start | bytes 393224 | tf_op jit(solution)/shard_map/ppermute | solution.py:479
  69.0 6.4 %collective-permute-start.9 = (bf16[128,512]{1,0:T(8,128)(2,1)S(1)}, bf16[128,512]{1,0:T(8,128)(2,1)S(1)}, u32[]{:S(2)}, u32[]{:S(2)}) collective-permute-start(bf16[128,512]{1,0:T(8,128)(2,1)S(1)} %get-tuple-element.99), channel_id=1, source_target_pairs={{0,24},{1,25},{2,26},{3,27},{4,28},{5,29},{6,30},{7,31},{8,16},{9,... | collective-permute-start | bytes 393224 | tf_op jit(solution)/shard_map/ppermute | solution.py:479
  76.1 6.6 %collective-permute-start.10 = (bf16[32,512]{1,0:T(8,128)(2,1)S(1)}, bf16[32,512]{1,0:T(8,128)(2,1)S(1)}, u32[]{:S(2)}, u32[]{:S(2)}) collective-permute-start(bf16[32,512]{1,0:T(8,128)(2,1)S(1)} %get-tuple-element.109), channel_id=1, source_target_pairs={{0,16},{1,17},{2,18},{3,19},{4,20},{5,21},{6,22},{7,23},{8,24},{9,... | collective-permute-start | bytes 98312 | tf_op jit(solution)/shard_map/ppermute | solution.py:479
  78.9 8.3 %collective-permute-start.11 = (bf16[32,512]{1,0:T(8,128)(2,1)S(1)}, bf16[32,512]{1,0:T(8,128)(2,1)S(1)}, u32[]{:S(2)}, u32[]{:S(2)}) collective-permute-start(bf16[32,512]{1,0:T(8,128)(2,1)S(1)} %get-tuple-element.110), channel_id=1, source_target_pairs={{0,8},{1,9},{2,10},{3,11},{4,12},{5,13},{6,14},{7,15},{8,0},{9,1},... | collective-permute-start | bytes 98312 | tf_op jit(solution)/shard_map/ppermute | solution.py:479
  79.6 7.5 %collective-permute-start.12 = (bf16[32,512]{1,0:T(8,128)(2,1)S(1)}, bf16[32,512]{1,0:T(8,128)(2,1)S(1)}, u32[]{:S(2)}, u32[]{:S(2)}) collective-permute-start(bf16[32,512]{1,0:T(8,128)(2,1)S(1)} %get-tuple-element.111), channel_id=1, source_target_pairs={{0,24},{1,25},{2,26},{3,27},{4,28},{5,29},{6,30},{7,31},{8,16},{9,... | collective-permute-start | bytes 98312 | tf_op jit(solution)/shard_map/ppermute | solution.py:479
  81.4 5.8 %collective-permute-start.13 = (bf16[32,512]{1,0:T(8,128)(2,1)S(1)}, bf16[32,512]{1,0:T(8,128)(2,1)S(1)}, u32[]{:S(2)}, u32[]{:S(2)}) collective-permute-start(bf16[32,512]{1,0:T(8,128)(2,1)S(1)} %get-tuple-element.113), channel_id=1, source_target_pairs={{0,2},{1,3},{2,4},{3,5},{4,6},{5,7},{6,0},{7,1},{8,10},{9,11},{10,... | collective-permute-start | bytes 98312 | tf_op jit(solution)/shard_map/ppermute | solution.py:479
  81.4 5.8 %collective-permute-start.14 = (bf16[32,512]{1,0:T(8,128)(2,1)S(1)}, bf16[32,512]{1,0:T(8,128)(2,1)S(1)}, u32[]{:S(2)}, u32[]{:S(2)}) collective-permute-start(bf16[32,512]{1,0:T(8,128)(2,1)S(1)} %get-tuple-element.114), channel_id=1, source_target_pairs={{0,4},{1,5},{2,6},{3,7},{4,0},{5,1},{6,2},{7,3},{8,12},{9,13},{10,... | collective-permute-start | bytes 98312 | tf_op jit(solution)/shard_map/ppermute | solution.py:479
  82.7 4.4 %collective-permute-start.15 = (bf16[32,512]{1,0:T(8,128)(2,1)S(1)}, bf16[32,512]{1,0:T(8,128)(2,1)S(1)}, u32[]{:S(2)}, u32[]{:S(2)}) collective-permute-start(bf16[32,512]{1,0:T(8,128)(2,1)S(1)} %get-tuple-element.115), channel_id=1, source_target_pairs={{0,6},{1,7},{2,0},{3,1},{4,2},{5,3},{6,4},{7,5},{8,14},{9,15},{10,... | collective-permute-start | bytes 98312 | tf_op jit(solution)/shard_map/ppermute | solution.py:479
  87.2 4.7 %collective-permute-start.16 = (bf16[96,512]{1,0:T(8,128)(2,1)S(1)}, bf16[96,512]{1,0:T(8,128)(2,1)S(1)}, u32[]{:S(2)}, u32[]{:S(2)}) collective-permute-start(bf16[96,512]{1,0:T(8,128)(2,1)S(1)} %shard_map.117.mine_ref), channel_id=1, source_target_pairs={{0,32},{1,33},{2,34},{3,35},{4,36},{5,37},{6,38},{7,39},{8,40},{9,... | collective-permute-start | bytes 294920 | tf_op jit(solution)/shard_map/ppermute | solution.py:479
  91.9 6.2 %collective-permute-start.17 = (bf16[96,512]{1,0:T(8,128)(2,1)S(1)}, bf16[96,512]{1,0:T(8,128)(2,1)S(1)}, u32[]{:S(2)}, u32[]{:S(2)}) collective-permute-start(bf16[96,512]{1,0:T(8,128)(2,1)S(1)} %shard_map.118.mine_ref), channel_id=1, source_target_pairs={{0,96},{1,97},{2,98},{3,99},{4,100},{5,101},{6,102},{7,103},{8,104... | collective-permute-start | bytes 294920 | tf_op jit(solution)/shard_map/ppermute | solution.py:479
  98.5 18.0 %collective-permute-start.20 = (bf16[256,512]{1,0:T(8,128)(2,1)S(1)}, bf16[256,512]{1,0:T(8,128)(2,1)S(1)}, u32[]{:S(2)}, u32[]{:S(2)}) collective-permute-start(bf16[256,512]{1,0:T(8,128)(2,1)S(1)} %get-tuple-element.131), channel_id=1, source_target_pairs={{0,1},{1,2},{2,3},{3,4},{4,5},{5,6},{6,7},{7,8},{8,9},{9,10},{10,1... | collective-permute-start | bytes 786440 | tf_op jit(solution)/shard_map/ppermute | solution.py:458
  103.3 13.3 %collective-permute-start.19 = (bf16[112,512]{1,0:T(8,128)(2,1)S(1)}, bf16[112,512]{1,0:T(8,128)(2,1)S(1)}, u32[]{:S(2)}, u32[]{:S(2)}) collective-permute-start(bf16[112,512]{1,0:T(8,128)(2,1)S(1)} %get-tuple-element.130), channel_id=1, source_target_pairs={{0,16},{1,17},{2,18},{3,19},{4,20},{5,21},{6,22},{7,23},{8,24},{9,... | collective-permute-start | bytes 344072 | tf_op jit(solution)/shard_map/ppermute | solution.py:458
  103.9 12.6 %collective-permute-start.18 = (bf16[96,512]{1,0:T(8,128)(2,1)S(1)}, bf16[96,512]{1,0:T(8,128)(2,1)S(1)}, u32[]{:S(2)}, u32[]{:S(2)}) collective-permute-start(bf16[96,512]{1,0:T(8,128)(2,1)S(1)} %shard_map.119.mine_ref), channel_id=1, source_target_pairs={{0,224},{1,225},{2,226},{3,227},{4,228},{5,229},{6,230},{7,231},{8... | collective-permute-start | bytes 294920 | tf_op jit(solution)/shard_map/ppermute | solution.py:479
  108.1 8.4 %collective-permute-start.21 = (bf16[48,512]{1,0:T(8,128)(2,1)S(1)}, bf16[48,512]{1,0:T(8,128)(2,1)S(1)}, u32[]{:S(2)}, u32[]{:S(2)}) collective-permute-start(bf16[48,512]{1,0:T(8,128)(2,1)S(1)} %get-tuple-element.132), channel_id=1, source_target_pairs={{0,17},{1,18},{2,19},{3,20},{4,21},{5,22},{6,23},{7,24},{8,25},{9,... | collective-permute-start | bytes 147464 | tf_op jit(solution)/shard_map/ppermute | solution.py:458
  116.6 4.6 %collective-permute-start.24 = (bf16[32,512]{1,0:T(8,128)(2,1)S(1)}, bf16[32,512]{1,0:T(8,128)(2,1)S(1)}, u32[]{:S(2)}, u32[]{:S(2)}) collective-permute-start(bf16[32,512]{1,0:T(8,128)(2,1)S(1)} %get-tuple-element.134.refs_1_), channel_id=1, source_target_pairs={{0,24},{1,25},{2,26},{3,27},{4,28},{5,29},{6,30},{7,31},{8,16},{9,... | collective-permute-start | bytes 98312 | tf_op jit(solution)/shard_map/ppermute | solution.py:479
  116.7 8.5 %collective-permute-start.27 = (bf16[64,512]{1,0:T(8,128)(2,1)S(1)}, bf16[64,512]{1,0:T(8,128)(2,1)S(1)}, u32[]{:S(2)}, u32[]{:S(2)}) collective-permute-start(bf16[64,512]{1,0:T(8,128)(2,1)S(1)} %get-tuple-element.135.refs_5_), channel_id=1, source_target_pairs={{0,6},{1,7},{2,0},{3,1},{4,2},{5,3},{6,4},{7,5},{8,14},{9,15},{10,... | collective-permute-start | bytes 196616 | tf_op jit(solution)/shard_map/ppermute | solution.py:479
  118.9 6.4 %collective-permute-start.26 = (bf16[64,512]{1,0:T(8,128)(2,1)S(1)}, bf16[64,512]{1,0:T(8,128)(2,1)S(1)}, u32[]{:S(2)}, u32[]{:S(2)}) collective-permute-start(bf16[64,512]{1,0:T(8,128)(2,1)S(1)} %get-tuple-element.135.refs_5_), channel_id=1, source_target_pairs={{0,4},{1,5},{2,6},{3,7},{4,0},{5,1},{6,2},{7,3},{8,12},{9,13},{10,... | collective-permute-start | bytes 196616 | tf_op jit(solution)/shard_map/ppermute | solution.py:479
  119.2 6.0 %collective-permute-start.25 = (bf16[64,512]{1,0:T(8,128)(2,1)S(1)}, bf16[64,512]{1,0:T(8,128)(2,1)S(1)}, u32[]{:S(2)}, u32[]{:S(2)}) collective-permute-start(bf16[64,512]{1,0:T(8,128)(2,1)S(1)} %get-tuple-element.135.refs_5_), channel_id=1, source_target_pairs={{0,2},{1,3},{2,4},{3,5},{4,6},{5,7},{6,0},{7,1},{8,10},{9,11},{10,... | collective-permute-start | bytes 196616 | tf_op jit(solution)/shard_map/ppermute | solution.py:479
  119.6 4.3 %collective-permute-start.23 = (bf16[32,512]{1,0:T(8,128)(2,1)S(1)}, bf16[32,512]{1,0:T(8,128)(2,1)S(1)}, u32[]{:S(2)}, u32[]{:S(2)}) collective-permute-start(bf16[32,512]{1,0:T(8,128)(2,1)S(1)} %get-tuple-element.134.refs_1_), channel_id=1, source_target_pairs={{0,8},{1,9},{2,10},{3,11},{4,12},{5,13},{6,14},{7,15},{8,0},{9,1},... | collective-permute-start | bytes 98312 | tf_op jit(solution)/shard_map/ppermute | solution.py:479
  121.2 4.0 %collective-permute-start.22 = (bf16[32,512]{1,0:T(8,128)(2,1)S(1)}, bf16[32,512]{1,0:T(8,128)(2,1)S(1)}, u32[]{:S(2)}, u32[]{:S(2)}) collective-permute-start(bf16[32,512]{1,0:T(8,128)(2,1)S(1)} %get-tuple-element.134.refs_1_), channel_id=1, source_target_pairs={{0,16},{1,17},{2,18},{3,19},{4,20},{5,21},{6,22},{7,23},{8,24},{9,... | collective-permute-start | bytes 98312 | tf_op jit(solution)/shard_map/ppermute | solution.py:479
  125.8 6.0 %collective-permute-start.30 = (bf16[160,512]{1,0:T(8,128)(2,1)S(1)}, bf16[160,512]{1,0:T(8,128)(2,1)S(1)}, u32[]{:S(2)}, u32[]{:S(2)}) collective-permute-start(bf16[160,512]{1,0:T(8,128)(2,1)S(1)} %get-tuple-element.147.refs_1_), channel_id=1, source_target_pairs={{0,24},{1,25},{2,26},{3,27},{4,28},{5,29},{6,30},{7,31},{8,16},{9,... | collective-permute-start | bytes 491528 | tf_op jit(solution)/shard_map/ppermute | solution.py:479
  127.1 5.8 %collective-permute-start.29 = (bf16[160,512]{1,0:T(8,128)(2,1)S(1)}, bf16[160,512]{1,0:T(8,128)(2,1)S(1)}, u32[]{:S(2)}, u32[]{:S(2)}) collective-permute-start(bf16[160,512]{1,0:T(8,128)(2,1)S(1)} %get-tuple-element.147.refs_1_), channel_id=1, source_target_pairs={{0,8},{1,9},{2,10},{3,11},{4,12},{5,13},{6,14},{7,15},{8,0},{9,1},... | collective-permute-start | bytes 491528 | tf_op jit(solution)/shard_map/ppermute | solution.py:479
  128.0 6.5 %collective-permute-start.28 = (bf16[160,512]{1,0:T(8,128)(2,1)S(1)}, bf16[160,512]{1,0:T(8,128)(2,1)S(1)}, u32[]{:S(2)}, u32[]{:S(2)}) collective-permute-start(bf16[160,512]{1,0:T(8,128)(2,1)S(1)} %get-tuple-element.147.refs_1_), channel_id=1, source_target_pairs={{0,16},{1,17},{2,18},{3,19},{4,20},{5,21},{6,22},{7,23},{8,24},{9,... | collective-permute-start | bytes 491528 | tf_op jit(solution)/shard_map/ppermute | solution.py:479
  128.0 13.8 %collective-permute-start.34 = (bf16[128,512]{1,0:T(8,128)(2,1)S(1)}, bf16[128,512]{1,0:T(8,128)(2,1)S(1)}, u32[]{:S(2)}, u32[]{:S(2)}) collective-permute-start(bf16[128,512]{1,0:T(8,128)(2,1)S(1)} %get-tuple-element.148.refs_1_), channel_id=1, source_target_pairs={{0,6},{1,7},{2,0},{3,1},{4,2},{5,3},{6,4},{7,5},{8,14},{9,15},{10,... | collective-permute-start | bytes 393224 | tf_op jit(solution)/shard_map/ppermute | solution.py:479
  130.3 11.5 %collective-permute-start.33 = (bf16[128,512]{1,0:T(8,128)(2,1)S(1)}, bf16[128,512]{1,0:T(8,128)(2,1)S(1)}, u32[]{:S(2)}, u32[]{:S(2)}) collective-permute-start(bf16[128,512]{1,0:T(8,128)(2,1)S(1)} %get-tuple-element.148.refs_1_), channel_id=1, source_target_pairs={{0,4},{1,5},{2,6},{3,7},{4,0},{5,1},{6,2},{7,3},{8,12},{9,13},{10,... | collective-permute-start | bytes 393224 | tf_op jit(solution)/shard_map/ppermute | solution.py:479
  131.8 10.1 %collective-permute-start.32 = (bf16[128,512]{1,0:T(8,128)(2,1)S(1)}, bf16[128,512]{1,0:T(8,128)(2,1)S(1)}, u32[]{:S(2)}, u32[]{:S(2)}) collective-permute-start(bf16[128,512]{1,0:T(8,128)(2,1)S(1)} %get-tuple-element.148.refs_1_), channel_id=1, source_target_pairs={{0,2},{1,3},{2,4},{3,5},{4,6},{5,7},{6,0},{7,1},{8,10},{9,11},{10,... | collective-permute-start | bytes 393224 | tf_op jit(solution)/shard_map/ppermute | solution.py:479
  135.1 12.7 %collective-permute-start.31 = (bf16[544,512]{1,0:T(8,128)(2,1)S(1)}, bf16[544,512]{1,0:T(8,128)(2,1)S(1)}, u32[]{:S(2)}, u32[]{:S(2)}) collective-permute-start(bf16[544,512]{1,0:T(8,128)(2,1)S(1)} %shard_map.126.refs_1_.mine_ref), channel_id=1, source_target_pairs={{0,1},{1,0},{2,3},{3,2},{4,5},{5,4},{6,7},{7,6},{8,9},{9,8},{10,11... | collective-permute-start | bytes 1671176 | tf_op jit(solution)/shard_map/ppermute | solution.py:479
  142.4 3.8 %collective-permute-start.35 = (bf16[512,512]{1,0:T(8,128)(2,1)S(1)}, bf16[512,512]{1,0:T(8,128)(2,1)S(1)}, u32[]{:S(2)}, u32[]{:S(2)}) collective-permute-start(bf16[512,512]{1,0:T(8,128)(2,1)S(1)} %shard_map.127.refs_1_), channel_id=1, source_target_pairs={{0,1},{1,0},{2,3},{3,2},{4,5},{5,4},{6,7},{7,6},{8,9},{9,8},{10,11... | collective-permute-start | bytes 1572872 | tf_op jit(solution)/shard_map/ppermute | solution.py:479

commit v2 on v0

--- a/solution.py
+++ b/solution.py
@@ -88,7 +88,8 @@
         for part, (src, dst) in enumerate(
             (
                 (ref.at[:, 0:SH], top.at[which]),
-                (ref.at[:, SH : geo.rows, 0:16], left.at[which]),
+                (ref.at[0, SH : geo.rows, 0:16], left.at[which, 0]),
+                (ref.at[1, SH : geo.rows, 0:16], left.at[which, 1]),
             )
         ):
             copy = pltpu.make_async_copy(src, dst, sems.at[which, part])
@@ -160,15 +161,14 @@
     lax.fori_loop(0, win // 8, step, 0)
 
 
-def table_kernel(heads, idx_ref, sum_ref, gsum_ref, gain_ref, out_ref, acc, line):
+def table_sums(heads, first, count, idx_ref, sum_ref, acc):
     win = idx_ref.shape[0]
     rows = heads * BANDS
     iota = lax.broadcasted_iota(jnp.int32, (SPAN, win), 0)
     bands = lax.broadcasted_iota(jnp.int32, (BANDS, win), 0)
-    acc[...] = jnp.zeros_like(acc)
 
     def step(block, carry):
-        start = pl.multiple_of(block * 8, 8)
+        start = pl.multiple_of(first + block * 8, 8)
         band, place = band_of(idx_ref[pl.ds(start, 8), :])
         tops, rests = [], []
         for h in range(heads):
@@ -186,7 +186,12 @@
         acc[...] += total[:rows] + total[rows:]
         return carry
 
-    lax.fori_loop(0, win // 8, step, 0)
+    lax.fori_loop(0, count // 8, step, 0)
+
+
+def table_kernel(heads, idx_ref, sum_ref, gsum_ref, gain_ref, out_ref, acc, line):
+    acc[...] = jnp.zeros_like(acc)
+    table_sums(heads, 0, idx_ref.shape[0], idx_ref, sum_ref, acc)
     for h in range(heads):
         for b in range(BANDS):
             line[h : h + 1, b * SPAN : (b + 1) * SPAN] = acc[h * BANDS + b : h * BANDS + b + 1, :]
@@ -349,12 +354,12 @@
     send_ref[...] = grads[1 - info_ref[CORE]]
 
 
-def back_kernel(geo, first, count, dproj, unit_ref, inv, cotb, gain_ref, wqkv_ref, gtok_ref):
+def back_kernel(geo, dproj, unit_ref, inv, cotb, gain_ref, wqkv_ref, gtok_ref):
     win = geo.win
     gain = gain_ref[...]
 
     def back_step(w, carry):
-        at = pl.ds(pl.multiple_of((first + w) * win, 16), win)
+        at = pl.ds(pl.multiple_of(w * win, 16), win)
         gn = dot_nt(dproj[at, :], wqkv_ref[...]).astype(BF16).astype(F32)
         unit = unit_ref[at, :]
         hat = gn * gain
@@ -362,19 +367,16 @@
         slope = jnp.mean(hat * unit, axis=-1, keepdims=True)
         istd = inv[at, 0:1]
         cot = cotb[at, :].astype(F32)
-        to = pl.ds(pl.multiple_of(w * win, 16), win)
-        gtok_ref[to, :] = (cot + istd * (hat - centre - unit * slope)).astype(BF16)
+        gtok_ref[at, :] = (cot + istd * (hat - centre - unit * slope)).astype(BF16)
         return carry
 
-    lax.fori_loop(0, count, back_step, 0)
-
-
-def unpack_send_kernel(geo, low_ref, high_ref, rows_ref, cols_ref, corner_ref, fg, buf):
+    lax.fori_loop(0, geo.nwin, back_step, 0)
+
+
+def unpack_send_kernel(geo, gtok_ref, rows_ref, cols_ref, corner_ref, fg, buf):
     base_cols = pad16(geo.n_rows)
     base_corner = base_cols + pad16(geo.n_cols)
-    half = low_ref.shape[0]
-    fg[0:half] = low_ref[...].astype(F32)
-    fg[half:] = high_ref[...].astype(F32)
+    fg[...] = gtok_ref[...].astype(F32)
     buf[...] = jnp.zeros_like(buf)
     bases = {"rows": 0, "cols": base_cols, "corner": base_corner}
     for z in range(geo.depth):
@@ -391,10 +393,8 @@
     corner_ref[...] = buf[base_corner : base_corner + pad16(geo.n_corner)].astype(BF16)
 
 
-def assemble_kernel(geo, low_ref, high_ref, rows_ref, cols_ref, corner_ref, out_ref, fg, rr, rc, rk, grid):
-    half = low_ref.shape[0]
-    fg[0:half] = low_ref[...].astype(F32)
-    fg[half:] = high_ref[...].astype(F32)
+def assemble_kernel(geo, gtok_ref, rows_ref, cols_ref, corner_ref, out_ref, fg, rr, rc, rk, grid):
+    fg[...] = gtok_ref[...].astype(F32)
     rr[...] = rows_ref[...].astype(F32)
     rc[...] = cols_ref[...].astype(F32)
     rk[...] = corner_ref[...].astype(F32)
@@ -481,14 +481,15 @@
         return self.send(value, lambda z, x, y, c: (z ^ (2 * bit - 1), x, y, c))
 
 
-def pair_sum_kernel(ny, nx, info_ref, keep_ref, recv_ref, *outs):
-    rows = keep_ref.shape[0] // 2
-    for base, count, place, refs in ((0, ny, Y, outs[:ny]), (rows, nx, X, outs[ny:])):
-        piece = rows // count
-        for k, ref in enumerate(refs):
-            part = (info_ref[place] + k) & (count - 1)
-            at = pl.ds(pl.multiple_of(base + part * piece, 16), piece)
-            ref[...] = (keep_ref[at, :].astype(F32) + recv_ref[at, :].astype(F32)).astype(BF16)
+def part_rows(info_ref, place, step, count, rows):
+    part = (info_ref[place] + step) & (count - 1)
+    return pl.ds(pl.multiple_of(part * rows, 16), rows)
+
+
+def pair_sum_kernel(info_ref, keep_ref, recv_ref, *outs):
+    for k, ref in enumerate(outs):
+        at = part_rows(info_ref, Y, k, len(outs), ref.shape[0])
+        ref[...] = (keep_ref[at, :].astype(F32) + recv_ref[at, :].astype(F32)).astype(BF16)
 
 
 def total_of(refs):
@@ -499,16 +500,11 @@
 
 
 def cross_sum_kernel(ny, nx, info_ref, *refs):
-    ins_a, ins_b = refs[:ny], refs[ny : ny + nx]
-    outs_a, outs_b = refs[ny + nx : ny + 2 * nx], refs[ny + 2 * nx : 2 * ny + 2 * nx]
-    hold = refs[-1]
-    for ins, outs, count, place in ((ins_a, outs_a, nx, X), (ins_b, outs_b, ny, Y)):
-        hold[...] = total_of(ins)
-        piece = hold.shape[0] // count
-        for k, ref in enumerate(outs):
-            part = (info_ref[place] + k) & (count - 1)
-            at = pl.ds(pl.multiple_of(part * piece, 16), piece)
-            ref[...] = hold[at, :].astype(BF16)
+    outs, hold = refs[ny : ny + nx], refs[-1]
+    hold[...] = total_of(refs[:ny])
+    for k, ref in enumerate(outs):
+        at = part_rows(info_ref, X, k, nx, ref.shape[0])
+        ref[...] = hold[at, :].astype(BF16)
 
 
 SMALL = 16
@@ -530,71 +526,42 @@
     return total
 
 
-def join_sum_kernel(ny, nx, *refs):
+def join_sum_kernel(*refs):
     piece = refs[0].shape[0]
     small_ref, out_ref = refs[-2:]
-    out_ref[0:piece] = total_of(refs[:nx]).astype(BF16)
-    out_ref[piece : 2 * piece] = total_of(refs[nx : nx + ny]).astype(BF16)
-    put_small(out_ref, 2 * piece, small_ref[...])
-
-
-def z_sum_kernel(mine_ref, got_ref, *outs):
+    out_ref[0:piece] = total_of(refs[:-2]).astype(BF16)
+    put_small(out_ref, piece, small_ref[...])
+
+
+def z_sum_kernel(mine_ref, got_ref, out_ref):
     rows = mine_ref.shape[0] - 2 * SMALL
-    total = (mine_ref[0:rows].astype(F32) + got_ref[0:rows].astype(F32)).astype(BF16)
-    last = small_of((mine_ref, got_ref), rows)
-    if len(outs) == 1:
-        outs[0][0:rows] = total
-    else:
-        outs[0][...] = total[: rows // 2]
-        outs[1][0 : rows // 2] = total[rows // 2 :]
-    put_small(outs[-1], outs[-1].shape[0] - 2 * SMALL, last)
-
-
-def gather_kernel(ny, nx, info_ref, *refs):
-    a_ref, b_ref = refs[-2:]
-    ins_a, ins_b = refs[:nx], refs[nx : nx + ny]
-    piece = ins_a[0].shape[0]
-    for ins, out, count, place in ((ins_a, a_ref, nx, X), (ins_b, b_ref, ny, Y)):
-        for k, ref in enumerate(ins):
-            part = (info_ref[place] + (count - k)) & (count - 1)
-            out[pl.ds(pl.multiple_of(part * piece, 16), piece), :] = ref[0:piece]
-    put_small(b_ref, ny * piece, small_of(ins_b, piece))
-
-
-def merge_kernel(count, place, with_small, info_ref, *refs):
-    ins, outs = refs[:count], refs[count:]
-    out_ref = outs[0]
-    width = out_ref.shape[1]
-    piece = out_ref.shape[0] // count
+    out_ref[0:rows] = (mine_ref[0:rows].astype(F32) + got_ref[0:rows].astype(F32)).astype(BF16)
+    put_small(out_ref, rows, small_of((mine_ref, got_ref), rows))
+
+
+def gather_kernel(place, info_ref, *refs):
+    ins, out_ref = refs[:-1], refs[-1]
+    piece = ins[0].shape[0] - 2 * SMALL
     for k, ref in enumerate(ins):
-        part = (info_ref[place] + (count - k)) & (count - 1)
-        out_ref[pl.ds(pl.multiple_of(part * piece, 16), piece), :] = ref[0:piece]
-    if with_small:
-        line_ref, gain_ref = outs[1:]
-        total = small_of(ins, piece)
-        more = line_ref.shape[1] - width
-        line_ref[:, 0:width] = total[0:8]
-        line_ref[:, width:] = total[8:, 0:more]
-        gain_ref[:, 0 : width - more] = total[8:9, more:]
-        gain_ref[:, width - more :] = total[9:10, more:]
-
-
-def place_kernel(mine, info_ref, a_ref, b_ref, *refs):
-    gqkv_ref, gout_ref, hold, sems = refs[-4:]
+        at = part_rows(info_ref, place, len(ins) - k, len(ins), piece)
+        out_ref[at, :] = ref[0:piece]
+    put_small(out_ref, len(ins) * piece, small_of(ins, piece))
+
+
+def place_rows(half, value_ref, gqkv_ref, gout_ref, hold, sems):
     width = gout_ref.shape[1]
-    core = info_ref[CORE]
-    half = core if mine else 1 - core
     steps = 4
     rows = width // steps
 
     def write(targets):
         copies = []
-        for which, ref in enumerate((a_ref, b_ref)):
+        for which, target in enumerate(targets):
             for step in range(steps):
                 at = slice(step * rows, (step + 1) * rows)
-                hold[which, at] = ref[at].astype(F32)
+                src = slice(which * width + step * rows, which * width + (step + 1) * rows)
+                hold[src] = value_ref[src].astype(F32)
                 copy = pltpu.make_async_copy(
-                    hold.at[which, at], targets[which].at[at], sems.at[which, step]
+                    hold.at[src], target.at[at], sems.at[which, step]
                 )
                 copy.start()
                 copies.append(copy)
@@ -608,6 +575,23 @@
     @pl.when(half == 1)
     def _():
         write((gqkv_ref.at[:, 2 * width :], gout_ref))
+
+
+def place_own_kernel(info_ref, mine_ref, gqkv_ref, gout_ref, hold, sems):
+    place_rows(info_ref[CORE], mine_ref, gqkv_ref, gout_ref, hold, sems)
+
+
+def place_other_kernel(
+    info_ref, mine_ref, got_ref, gqkv_in, gout_in, gqkv_ref, gout_ref, line_ref, gain_ref, hold, sems
+):
+    width = gout_ref.shape[1]
+    total = small_of((mine_ref, got_ref), 2 * width)
+    more = line_ref.shape[1] - width
+    line_ref[:, 0:width] = total[0:8]
+    line_ref[:, width:] = total[8:, 0:more]
+    gain_ref[:, 0 : width - more] = total[8:9, more:]
+    gain_ref[:, width - more :] = total[9:10, more:]
+    place_rows(1 - info_ref[CORE], got_ref, gqkv_ref, gout_ref, hold, sems)
 
 
 def per_device(tokens, norm_gain, qkv_weight, out_weight, bias_table, bias_index, cotangent):
@@ -622,7 +606,7 @@
     rim = pl.pallas_call(
         lambda *refs: pack_kernel(geo, *refs),
         out_shape=[shape((n, width), BF16) for n in (n_rows, n_cols, n_corner)],
-        in_specs=[pl.BlockSpec(memory_space=pl.ANY)] * 2,
+        in_specs=[pl.BlockSpec(memory_space=pltpu.HBM)] * 2,
         out_specs=[pl.BlockSpec(memory_space=pltpu.VMEM)] * 3,
         scratch_shapes=[
             pltpu.VMEM((2, depth, SH, cols_lon, width), BF16),
@@ -630,7 +614,7 @@
             pltpu.VMEM((2, depth, SH, cols_lon, width), F32),
             pltpu.VMEM((2, depth, rows_lat - SH, 16, width), F32),
             pltpu.VMEM((n_rows + n_cols + n_corner, width), F32),
-            pltpu.SemaphoreType.DMA((2, 2)),
+            pltpu.SemaphoreType.DMA((2, 3)),
         ],
         compiler_params=pltpu.CompilerParams(vmem_limit_bytes=60 * MIB),
     )(tokens, cotangent)
@@ -655,7 +639,7 @@
     small_limit = 10 * MIB
 
     vmem, smem = pl.BlockSpec(memory_space=pltpu.VMEM), pl.BlockSpec(memory_space=pltpu.SMEM)
-    hbm = pl.BlockSpec(memory_space=pl.ANY)
+    hbm = pl.BlockSpec(memory_space=pltpu.HBM)
     send, keep, bias_sum, grad_proj, unit, inv, cot_win, gain_sum = pl.pallas_call(
         lambda *refs: main_kernel(geo, heads, *refs),
         in_specs=[smem] + [vmem] * 6 + [hbm, hbm, vmem],
@@ -693,20 +677,29 @@
     )(info, tok, cot, *rim, norm_gain.reshape(1, width), qkv_weight, out_weight, bias)
 
     got = chips.core(send)
-    piece = half_rows // 2 // ny
+    piece = half_rows // ny
     outs = call(
-        lambda *refs: pair_sum_kernel(ny, nx, *refs),
-        [shape((piece, width), BF16)] * (ny + nx),
+        pair_sum_kernel,
+        [shape((piece, width), BF16)] * ny,
         [],
         3,
         small_limit,
         smem_first=True,
     )(info, keep, got)
 
-    outs, bias_sum = lax.optimization_barrier((outs, bias_sum))
-    got_a = [outs[0]] + [chips.y(outs[k], k) for k in range(1, ny)]
-    got_b = [outs[ny]] + [chips.x(outs[ny + k], k) for k in range(1, nx)]
+    outs, grad_proj, qkv_weight, bias_sum = lax.optimization_barrier(
+        (outs, grad_proj, qkv_weight, bias_sum)
+    )
+    got = [outs[0]] + [chips.y(outs[k], k) for k in range(1, ny)]
     gain_row = norm_gain.reshape(1, width)
+    gtok = call(
+        lambda *refs: back_kernel(geo, *refs),
+        shape((cells, width), BF16),
+        [],
+        6,
+        small_limit,
+        cost=pl.CostEstimate(flops=6 * 10**9, bytes_accessed=10**7, transcendentals=0),
+    )(grad_proj, unit, inv, cot_win, gain_row, qkv_weight)
     small = call(
         lambda *refs: table_kernel(heads, *refs),
         shape((SMALL, width), F32),
@@ -715,45 +708,47 @@
         small_limit,
         cost=pl.CostEstimate(flops=3 * 10**9, bytes_accessed=10**6, transcendentals=0),
     )(index_t, bias_sum, gain_sum, gain_row)
+    got, gtok, small = lax.optimization_barrier((got, gtok, small))
+    part = piece // nx
     outs = call(
         lambda *refs: cross_sum_kernel(ny, nx, *refs),
-        [shape((piece // nx, width), BF16)] * nx + [shape((piece // ny, width), BF16)] * ny,
+        [shape((part, width), BF16)] * nx,
         [pltpu.VMEM((piece, width), F32)],
-        1 + ny + nx,
+        1 + ny,
         small_limit,
         smem_first=True,
-    )(info, *got_a, *got_b)
-
-    got_a = [outs[0]] + [chips.x(outs[k], k) for k in range(1, nx)]
-    got_b = [outs[nx]] + [chips.y(outs[nx + k], k) for k in range(1, ny)]
-    small = small + chips.core(small)
-    part = piece // nx
+    )(info, *got)
+
+    got = [outs[0]] + [chips.x(outs[k], k) for k in range(1, nx)]
     mine = call(
-        lambda *refs: join_sum_kernel(ny, nx, *refs),
-        shape((2 * part + 2 * SMALL, width), BF16),
+        join_sum_kernel,
+        shape((part + 2 * SMALL, width), BF16),
         [],
-        ny + nx + 1,
+        nx + 1,
         small_limit,
-    )(*got_a, *got_b, small)
-
-    def layer_norm_back(first, count, proj):
+    )(*got, small)
+    bit = 1
+    while bit < chips.nz:
+        mine = call(z_sum_kernel, shape(mine.shape, BF16), [], 2, small_limit)(
+            mine, chips.z(mine, bit)
+        )
+        bit *= 2
+
+    def gathered(place, count, parts):
+        rows = (parts[0].shape[0] - 2 * SMALL) * count + 2 * SMALL
         return call(
-            lambda *refs: back_kernel(geo, first, count, *refs),
-            shape((count * win, width), BF16),
+            lambda *refs: gather_kernel(place, *refs),
+            shape((rows, width), BF16),
             [],
-            6,
+            1 + count,
             small_limit,
-            cost=pl.CostEstimate(flops=3 * 10**9, bytes_accessed=10**7, transcendentals=0),
-        )(proj, unit, inv, cot_win, gain_row, qkv_weight)
-
-    half_wins = geo.nwin // 2
-    mine, grad_proj = lax.optimization_barrier((mine, grad_proj))
-    got = chips.z(mine, 1)
-    low = layer_norm_back(0, half_wins, grad_proj)
-    mine = call(z_sum_kernel, shape(mine.shape, BF16), [], 2, small_limit)(mine, got)
-    mine, grad_proj = lax.optimization_barrier((mine, grad_proj))
-    got = chips.z(mine, 2)
-    high = layer_norm_back(half_wins, geo.nwin - half_wins, grad_proj)
+            smem_first=True,
+        )(info, *parts)
+
+    mine = gathered(X, nx, [mine] + [chips.x(mine, k) for k in range(1, nx)])
+    parts = [mine] + [chips.y(mine, k) for k in range(1, ny)]
+
+    parts[-1], gtok = lax.optimization_barrier((parts[-1], gtok))
     b_rows, b_cols, b_corner = pad16(geo.n_rows), pad16(geo.n_cols), pad16(geo.n_corner)
     back = call(
         lambda *refs: unpack_send_kernel(geo, *refs),
@@ -762,34 +757,11 @@
             pltpu.VMEM((cells, width), F32),
             pltpu.VMEM((b_rows + b_cols + b_corner, width), F32),
         ],
-        2,
+        1,
         small_limit,
-    )(low, high)
-    mine = call(z_sum_kernel, shape(mine.shape, BF16), [], 2, small_limit)(mine, got)
-    mine, back = lax.optimization_barrier((mine, back))
-    got = chips.z(mine, 4)
+    )(gtok)
     back = (moved(back[0], -1, 0), moved(back[1], 0, -1), moved(back[2], -1, -1))
-    own_a, own_b = call(
-        z_sum_kernel,
-        [shape((part, width), BF16), shape((part + 2 * SMALL, width), BF16)],
-        [],
-        2,
-        small_limit,
-    )(mine, got)
-
-    got_a = [own_a] + [chips.x(own_a, k) for k in range(1, nx)]
-    got_b = [own_b] + [chips.y(own_b, k) for k in range(1, ny)]
-    own_a, own_b = call(
-        lambda *refs: gather_kernel(ny, nx, *refs),
-        [shape((piece, width), BF16), shape((piece + 2 * SMALL, width), BF16)],
-        [],
-        1 + ny + nx,
-        small_limit,
-        smem_first=True,
-    )(info, *got_a, *got_b)
-    own_a, own_b, back, low = lax.optimization_barrier((own_a, own_b, back, low))
-    got_a = [own_a] + [chips.y(own_a, k) for k in range(1, ny)]
-    got_b = [own_b] + [chips.x(own_b, k) for k in range(1, nx)]
+    parts, back = lax.optimization_barrier((parts, back))
     grad_tokens = call(
         lambda *refs: assemble_kernel(geo, *refs),
         shape((cells, width), BF16),
@@ -800,48 +772,32 @@
             pltpu.VMEM((b_corner, width), F32),
             pltpu.VMEM((cells, width), F32),
         ],
-        5,
+        4,
         small_limit,
-    )(low, high, *back)
-    mine_a = call(
-        lambda *refs: merge_kernel(ny, Y, False, *refs),
-        [shape((width, width), BF16)],
-        [],
-        1 + ny,
-        small_limit,
-        smem_first=True,
-    )(info, *got_a)[0]
-    their_a = chips.core(mine_a)
-    mine_b, line, grad_gain = call(
-        lambda *refs: merge_kernel(nx, X, True, *refs),
-        [
-            shape((width, width), BF16),
-            shape((heads, BANDS * SPAN), F32),
-            shape((1, width), F32),
-        ],
-        [],
-        1 + nx,
-        small_limit,
-        smem_first=True,
-    )(info, *got_b)
-    their_b = chips.core(mine_b)
-
-    def write(mine, a, b, written):
-        return pl.pallas_call(
-            lambda *refs: place_kernel(mine, *refs),
-            out_shape=[shape((width, 3 * width), F32), shape((width, width), F32)],
-            in_specs=[smem, vmem, vmem] + [hbm] * len(written),
-            out_specs=[hbm, hbm],
-            input_output_aliases={3 + i: i for i in range(len(written))},
-            scratch_shapes=[
-                pltpu.VMEM((2, width, width), F32),
-                pltpu.SemaphoreType.DMA((2, 4)),
-            ],
-            compiler_params=pltpu.CompilerParams(vmem_limit_bytes=small_limit),
-        )(info, a, b, *written)
-
-    written = write(True, mine_a, mine_b, ())
-    grad_qkv, grad_out = write(False, their_a, their_b, tuple(written))
+    )(gtok, *back)
+    mine = gathered(Y, ny, parts)
+    other = chips.core(mine)
+
+    outputs = [shape((width, 3 * width), F32), shape((width, width), F32)]
+    scratch = [pltpu.VMEM((half_rows, width), F32), pltpu.SemaphoreType.DMA((2, 4))]
+    params = pltpu.CompilerParams(vmem_limit_bytes=small_limit)
+    written = pl.pallas_call(
+        place_own_kernel,
+        out_shape=outputs,
+        in_specs=[smem, vmem],
+        out_specs=[hbm, hbm],
+        scratch_shapes=scratch,
+        compiler_params=params,
+    )(info, mine)
+    grad_qkv, grad_out, line, grad_gain = pl.pallas_call(
+        place_other_kernel,
+        out_shape=outputs + [shape((heads, BANDS * SPAN), F32), shape((1, width), F32)],
+        in_specs=[smem, vmem, vmem, hbm, hbm],
+        out_specs=[hbm, hbm, vmem, vmem],
+        input_output_aliases={3: 0, 4: 1},
+        scratch_shapes=scratch,
+        compiler_params=params,
+    )(info, mine, other, *written)
     grad_bias = line.T[:entries]
     return (grad_tokens.reshape(tokens.shape), grad_qkv, grad_out, grad_bias, grad_gain.reshape(width))
 

time: 153 us -> 147 us (0.961)
  starting transfers between devices: 60.4 us -> 52.2 us
  waiting for transfers between devices: 24.1 us -> 27 us
    ppermute x31 -> x17, starting transfers between devices: 38.1 us -> 28.8 us  [send(): return lax.ppermute(value, ('lat', 'lon'), pairs)]
    ppermute x6, waiting for transfers between devices: 2.14 us -> 5.57 us  [moved(): return lax.ppermute(value, ('lat', 'lon'), pairs)]
    pallas_call x13 -> x11, Pallas kernels: 14.1 us -> 13.6 us  [the longest x1 6.19 us: per_device(): call(lambda *refs: back_kernel(geo, *refs), shape((cells, width), BF16),...]
    ppermute x31 -> x17, waiting for transfers between devices: 21.9 us -> 21.4 us  [send(): return lax.ppermute(value, ('lat', 'lon'), pairs)]
  transfers between devices with their start and end apart: 37 -> 23, of which waited for: 15 -> 12; matrix products, arithmetic and copies ran while one was open for 0% -> 0% of each run, Pallas kernels for 17% -> 16%
where the time goes in v2:
time: 147 us
  Pallas kernels  63.8 us (43%)
  starting transfers between devices  52.2 us (36%)
  waiting for transfers between devices  27 us (18%)
  local copies, waits for them, and re-layouts  3.13 us (2%)
    pallas_call x1, Pallas kernels, per_device(): pl.pallas_call(lambda *refs: main_kernel(geo, heads, *refs), in_specs=[sm...  32.8 us
    ppermute x17, starting transfers between devices, send(): return lax.ppermute(value, ('lat', 'lon'), pairs)  28.8 us
    ppermute x6, starting transfers between devices, moved(): return lax.ppermute(value, ('lat', 'lon'), pairs)  23.4 us
    ppermute x17, waiting for transfers between devices, send(): return lax.ppermute(value, ('lat', 'lon'), pairs)  21.4 us
    pallas_call x1, Pallas kernels, per_device(): call(lambda *refs: lookup_kernel(heads, *refs), [shape((heads, win, win),...  6.74 us
    pallas_call x1, Pallas kernels, per_device(): call(lambda *refs: back_kernel(geo, *refs), shape((cells, width), BF16),...  6.19 us
    pallas_call x1, Pallas kernels, per_device(): call(lambda *refs: table_kernel(heads, *refs), shape((SMALL, width), F32)...  5.99 us
    ppermute x6, waiting for transfers between devices, moved(): return lax.ppermute(value, ('lat', 'lon'), pairs)  5.57 us
  transfers between devices with their start and end apart: 23, of which 12 were waited for; matrix products, arithmetic and copies ran while one was open for 0% of the time, Pallas kernels for 16%

profile of v2, /device:TPU:1, one launch (start us, length us, event | category | flops | bytes accessed | tf_op | source)
XLA Modules:
  0.0 147.1 jit_solution(4413989054154932594)
XLA Ops:
  0.7 2.7 %shard_map.110 = (bf16[224,512]{1,0:T(8,128)(2,1)}, bf16[512,512]{1,0:T(8,128)(2,1)}, bf16[80,512]{1,0:T(8,128)(2,1)}) custom-call(bf16[2,24,24,512]{3,2,1,0:T(8,128)(2,1)} %refs_0_.2, bf16[2,24,24,512]{3,2,1,0:T(8,128)(2,1)} %refs_1_.1), custom_call_target="tpu_custom_call" | custom-call | tf_op jit(solution)/shard_map/pallas_call | solution.py:606
  3.3 3.3 %collective-permute-start.1 = (bf16[512,512]{1,0:T(8,128)(2,1)}, bf16[512,512]{1,0:T(8,128)(2,1)}, u32[]{:S(2)}, u32[]{:S(2)}) collective-permute-start(bf16[512,512]{1,0:T(8,128)(2,1)} %get-tuple-element.58), channel_id=1, source_target_pairs={{0,15},{1,0},{2,1},{3,2},{4,3},{5,4},{6,5},{7,6},{8,7},{9,8},{10,9... | collective-permute-start | bytes 1572872 | tf_op jit(solution)/shard_map/ppermute | solution.py:448
  6.6 8.7 %collective-permute-start.2 = (bf16[80,512]{1,0:T(8,128)(2,1)}, bf16[80,512]{1,0:T(8,128)(2,1)}, u32[]{:S(2)}, u32[]{:S(2)}) collective-permute-start(bf16[80,512]{1,0:T(8,128)(2,1)} %get-tuple-element.59), channel_id=1, source_target_pairs={{0,255},{1,240},{2,241},{3,242},{4,243},{5,244},{6,245},{7,246},{8... | collective-permute-start | bytes 245768 | tf_op jit(solution)/shard_map/ppermute | solution.py:448
  15.3 1.2 collective-permute-start
  16.5 6.7 %shard_map.111 = (f32[8,144,144]{2,1,0:T(8,128)S(1)}, s32[144,144]{1,0:T(8,128)S(1)}) custom-call(s32[144,144]{1,0:T(8,128)S(1)} %copy-done.5, f32[8,759]{1,0:T(8,128)S(1)} %bitcast.17), custom_call_target="tpu_custom_call" | custom-call | flops 4000000000 | bytes 1000000 | tf_op jit(solution)/shard_map/pallas_call | solution.py:623
  23.2 0.7 copy-done.7
  24.0 1.4 copy-done.2
  25.4 1.0 copy-done.3
  26.5 32.8 %shard_map.112 = (bf16[1024,512]{1,0:T(8,128)(2,1)S(1)}, bf16[1024,512]{1,0:T(8,128)(2,1)S(1)}, f32[8,144,144]{2,1,0:T(8,128)S(1)}, bf16[1152,1536]{1,0:T(8,128)...) custom-call(s32[4]{0:T(128)S(1)} %pad_add_fusion.refs_0_.info_ref, ...), custom_call_target="tpu_custom_call" | custom-call | tf_op jit(solution)/shard_map/pallas_call | solution.py:643
  59.3 0.1 collective-permute-start.3
  59.4 2.6 %collective-permute-done.3.recv_ref = bf16[1024,512]{1,0:T(8,128)(2,1)S(1)} collective-permute-done((bf16[1024,512]{1,0:T(8,128)(2,1)S(1)}, bf16[1024,512]{1,0:T(8,128)(2,1)S(1)}, u32[]{:S(2)}, u32[]{:S(2)}) %collective-permute-start.3) | collective-permute-done | bytes 1048608 | tf_op jit(solution)/shard_map/ppermute | solution.py:469
  62.0 0.8 shard_map.113
  62.8 0.1 collective-permute-start.4
  62.9 2.5 %collective-permute-start.5 = (bf16[256,512]{1,0:T(8,128)(2,1)S(1)}, bf16[256,512]{1,0:T(8,128)(2,1)S(1)}, u32[]{:S(2)}, u32[]{:S(2)}) collective-permute-start(bf16[256,512]{1,0:T(8,128)(2,1)S(1)} %get-tuple-element.71), channel_id=1, source_target_pairs={{0,4},{1,5},{2,6},{3,7},{4,0},{5,1},{6,2},{7,3},{8,12},{9,13},{10,... | collective-permute-start | bytes 786440 | tf_op jit(solution)/shard_map/ppermute | solution.py:469
  65.4 0.2 collective-permute-start.6
  65.6 6.2 %shard_map.114.refs_0_ = bf16[1152,512]{1,0:T(8,128)(2,1)S(1)} custom-call(bf16[1152,1536]{1,0:T(8,128)(2,1)S(1)} %get-tuple-element.73.refs_0_, f32[1152,512]{1,0:T(8,128)S(1)} %get-tuple-element.74.refs_1_, f32[1152,128]{1,0:T(8,128)S(1)} %get-tuple-element.75.refs_2_, bf16[1152,512]{1,0:T(8,128)(2,1)S(1)} %get-tuple-element.76.refs_3_, ...), custom_call_target="tpu_custom_call" | custom-call | flops 6000000000 | bytes 10000000 | tf_op jit(solution)/shard_map/pallas_call | solution.py:695
  71.8 6.0 %shard_map.115.refs_4_ = f32[16,512]{1,0:T(8,128)S(1)} custom-call(s32[144,144]{1,0:T(8,128)S(1)} %copy-done.8, f32[8,144,144]{2,1,0:T(8,128)S(1)} %get-tuple-element.79.refs_1_, f32[512,128]{1,0:T(8,128)S(1)} %get-tuple-element.80.refs_2_, f32[1,512]{1,0:T(1,128)S(1)} %bitcast.16), custom_call_target="tpu_custom_call" | custom-call | flops 3000000000 | bytes 1000000 | tf_op jit(solution)/shard_map/pallas_call | solution.py:703
  77.8 0.8 shard_map.116
  78.6 0.5 collective-permute-start.7
  79.1 2.2 %collective-permute-start.8 = (bf16[64,512]{1,0:T(8,128)(2,1)S(1)}, bf16[64,512]{1,0:T(8,128)(2,1)S(1)}, u32[]{:S(2)}, u32[]{:S(2)}) collective-permute-start(bf16[64,512]{1,0:T(8,128)(2,1)S(1)} %get-tuple-element.87), channel_id=1, source_target_pairs={{0,8},{1,9},{2,10},{3,11},{4,12},{5,13},{6,14},{7,15},{8,0},{9,1},... | collective-permute-start | bytes 196616 | tf_op jit(solution)/shard_map/ppermute | solution.py:469
  81.3 2.0 %collective-permute-start.9 = (bf16[64,512]{1,0:T(8,128)(2,1)S(1)}, bf16[64,512]{1,0:T(8,128)(2,1)S(1)}, u32[]{:S(2)}, u32[]{:S(2)}) collective-permute-start(bf16[64,512]{1,0:T(8,128)(2,1)S(1)} %get-tuple-element.88), channel_id=1, source_target_pairs={{0,24},{1,25},{2,26},{3,27},{4,28},{5,29},{6,30},{7,31},{8,16},{9,... | collective-permute-start | bytes 196616 | tf_op jit(solution)/shard_map/ppermute | solution.py:469
  83.3 0.8 collective-permute-done.8.refs_2_
  84.1 1.1 collective-permute-done.9.refs_3_
  85.2 1.6 %collective-permute-start.10 = (bf16[96,512]{1,0:T(8,128)(2,1)S(1)}, bf16[96,512]{1,0:T(8,128)(2,1)S(1)}, u32[]{:S(2)}, u32[]{:S(2)}) collective-permute-start(bf16[96,512]{1,0:T(8,128)(2,1)S(1)} %shard_map.117.mine_ref), channel_id=1, source_target_pairs={{0,32},{1,33},{2,34},{3,35},{4,36},{5,37},{6,38},{7,39},{8,40},{9,... | collective-permute-start | bytes 294920 | tf_op jit(solution)/shard_map/ppermute | solution.py:469
  86.8 2.0 %collective-permute-done.10.got_ref = bf16[96,512]{1,0:T(8,128)(2,1)S(1)} collective-permute-done((bf16[96,512]{1,0:T(8,128)(2,1)S(1)}, bf16[96,512]{1,0:T(8,128)(2,1)S(1)}, u32[]{:S(2)}, u32[]{:S(2)}) %collective-permute-start.10) | collective-permute-done | bytes 98336 | tf_op jit(solution)/shard_map/ppermute | solution.py:469
  88.8 4.3 %collective-permute-start.11 = (bf16[96,512]{1,0:T(8,128)(2,1)S(1)}, bf16[96,512]{1,0:T(8,128)(2,1)S(1)}, u32[]{:S(2)}, u32[]{:S(2)}) collective-permute-start(bf16[96,512]{1,0:T(8,128)(2,1)S(1)} %shard_map.118.mine_ref), channel_id=1, source_target_pairs={{0,96},{1,97},{2,98},{3,99},{4,100},{5,101},{6,102},{7,103},{8,104... | collective-permute-start | bytes 294920 | tf_op jit(solution)/shard_map/ppermute | solution.py:469
  93.1 2.0 %collective-permute-done.11.got_ref = bf16[96,512]{1,0:T(8,128)(2,1)S(1)} collective-permute-done((bf16[96,512]{1,0:T(8,128)(2,1)S(1)}, bf16[96,512]{1,0:T(8,128)(2,1)S(1)}, u32[]{:S(2)}, u32[]{:S(2)}) %collective-permute-start.11) | collective-permute-done | bytes 98336 | tf_op jit(solution)/shard_map/ppermute | solution.py:469
  95.2 4.6 %collective-permute-start.12 = (bf16[96,512]{1,0:T(8,128)(2,1)S(1)}, bf16[96,512]{1,0:T(8,128)(2,1)S(1)}, u32[]{:S(2)}, u32[]{:S(2)}) collective-permute-start(bf16[96,512]{1,0:T(8,128)(2,1)S(1)} %shard_map.119.mine_ref), channel_id=1, source_target_pairs={{0,224},{1,225},{2,226},{3,227},{4,228},{5,229},{6,230},{7,231},{8... | collective-permute-start | bytes 294920 | tf_op jit(solution)/shard_map/ppermute | solution.py:469
  99.7 2.1 %collective-permute-done.12.got_ref = bf16[96,512]{1,0:T(8,128)(2,1)S(1)} collective-permute-done((bf16[96,512]{1,0:T(8,128)(2,1)S(1)}, bf16[96,512]{1,0:T(8,128)(2,1)S(1)}, u32[]{:S(2)}, u32[]{:S(2)}) %collective-permute-start.12) | collective-permute-done | bytes 98336 | tf_op jit(solution)/shard_map/ppermute | solution.py:469
  101.9 3.1 %collective-permute-start.15 = (bf16[96,512]{1,0:T(8,128)(2,1)S(1)}, bf16[96,512]{1,0:T(8,128)(2,1)S(1)}, u32[]{:S(2)}, u32[]{:S(2)}) collective-permute-start(bf16[96,512]{1,0:T(8,128)(2,1)S(1)} %shard_map.120.refs_1_), channel_id=1, source_target_pairs={{0,24},{1,25},{2,26},{3,27},{4,28},{5,29},{6,30},{7,31},{8,16},{9,... | collective-permute-start | bytes 294920 | tf_op jit(solution)/shard_map/ppermute | solution.py:469
  105.0 0.7 collective-permute-start.13
  105.7 1.9 %collective-permute-done.15.refs_4_ = bf16[96,512]{1,0:T(8,128)(2,1)S(1)} collective-permute-done((bf16[96,512]{1,0:T(8,128)(2,1)S(1)}, bf16[96,512]{1,0:T(8,128)(2,1)S(1)}, u32[]{:S(2)}, u32[]{:S(2)}) %collective-permute-start.15) | collective-permute-done | bytes 98336 | tf_op jit(solution)/shard_map/ppermute | solution.py:469
  107.6 2.5 %collective-permute-done.14.refs_3_ = bf16[96,512]{1,0:T(8,128)(2,1)S(1)} collective-permute-done((bf16[96,512]{1,0:T(8,128)(2,1)S(1)}, bf16[96,512]{1,0:T(8,128)(2,1)S(1)}, u32[]{:S(2)}, u32[]{:S(2)}) %collective-permute-start.14) | collective-permute-done | bytes 98336 | tf_op jit(solution)/shard_map/ppermute | solution.py:469
  110.1 0.7 collective-permute-done.13.refs_2_
  110.8 0.6 shard_map.121.refs_1_
  111.4 2.3 %collective-permute-start.16 = (bf16[288,512]{1,0:T(8,128)(2,1)S(1)}, bf16[288,512]{1,0:T(8,128)(2,1)S(1)}, u32[]{:S(2)}, u32[]{:S(2)}) collective-permute-start(bf16[288,512]{1,0:T(8,128)(2,1)S(1)} %shard_map.121.refs_1_), channel_id=1, source_target_pairs={{0,6},{1,7},{2,0},{3,1},{4,2},{5,3},{6,4},{7,5},{8,14},{9,15},{10,... | collective-permute-start | bytes 884744 | tf_op jit(solution)/shard_map/ppermute | solution.py:469
  113.7 1.2 collective-permute-start.18
  114.8 5.7 %collective-permute-done.16.refs_4_ = bf16[288,512]{1,0:T(8,128)(2,1)S(1)} collective-permute-done((bf16[288,512]{1,0:T(8,128)(2,1)S(1)}, bf16[288,512]{1,0:T(8,128)(2,1)S(1)}, u32[]{:S(2)}, u32[]{:S(2)}) %collective-permute-start.16) | collective-permute-done | bytes 294944 | tf_op jit(solution)/shard_map/ppermute | solution.py:469
  120.5 0.3 shard_map.122
  120.8 9.3 %collective-permute-start.20 = (bf16[256,512]{1,0:T(8,128)(2,1)S(1)}, bf16[256,512]{1,0:T(8,128)(2,1)S(1)}, u32[]{:S(2)}, u32[]{:S(2)}) collective-permute-start(bf16[256,512]{1,0:T(8,128)(2,1)S(1)} %get-tuple-element.94), channel_id=1, source_target_pairs={{0,1},{1,2},{2,3},{3,4},{4,5},{5,6},{6,7},{7,8},{8,9},{9,10},{10,1... | collective-permute-start | bytes 786440 | tf_op jit(solution)/shard_map/ppermute | solution.py:448
  130.1 1.0 collective-permute-start.21
  131.1 5.4 %collective-permute-done.21.refs_3_ = bf16[48,512]{1,0:T(8,128)(2,1)S(1)} collective-permute-done((bf16[48,512]{1,0:T(8,128)(2,1)S(1)}, bf16[48,512]{1,0:T(8,128)(2,1)S(1)}, u32[]{:S(2)}, u32[]{:S(2)}) %collective-permute-start.21) | collective-permute-done | bytes 49184 | tf_op jit(solution)/shard_map/ppermute | solution.py:448
  136.5 0.2 collective-permute-done.19.refs_1_
  136.7 0.6 shard_map.124.mine_ref
  137.3 3.5 %collective-permute-start.22 = (bf16[1056,512]{1,0:T(8,128)(2,1)S(1)}, bf16[1056,512]{1,0:T(8,128)(2,1)S(1)}, u32[]{:S(2)}, u32[]{:S(2)}) collective-permute-start(bf16[1056,512]{1,0:T(8,128)(2,1)S(1)} %shard_map.124.mine_ref), channel_id=1, source_target_pairs={{0,1},{1,0},{2,3},{3,2},{4,5},{5,4},{6,7},{7,6},{8,9},{9,8},{10,11... | collective-permute-start | bytes 3244040 | tf_op jit(solution)/shard_map/ppermute | solution.py:469
  140.8 1.9 %shard_map.125 = (f32[512,1536]{1,0:T(8,128)}, f32[512,512]{1,0:T(8,128)}) custom-call(s32[4]{0:T(128)S(1)} %pad_add_fusion.refs_0_.info_ref, bf16[1056,512]{1,0:T(8,128)(2,1)S(1)} %shard_map.124.mine_ref), custom_call_target="tpu_custom_call" | custom-call | tf_op jit(solution)/shard_map/pallas_call | solution.py:784
  142.7 1.7 %shard_map.123 = bf16[1152,512]{1,0:T(8,128)(2,1)} custom-call(bf16[1152,512]{1,0:T(8,128)(2,1)S(1)} %shard_map.114.refs_0_, bf16[112,512]{1,0:T(8,128)(2,1)S(1)} %collective-permute-done.19.refs_1_, bf16[256,512]{1,0:T(8,128)(2,1)S(1)} %collective-permute-done.20.refs_2_, bf16[48,512]{1,0:T(8,128)(2,1)S(1)} %collective-permute-done.21.refs_3_), custom_call_target="tpu_custom_call" | custom-call | tf_op jit(solution)/shard_map/pallas_call | solution.py:765
  144.4 2.5 %shard_map.126 = (f32[512,1536]{1,0:T(8,128)}, f32[512,512]{1,0:T(8,128)}, f32[8,768]{1,0:T(8,128)}, f32[1,512]{1,0:T(1,128)}) custom-call(s32[4]{0:T(128)S(1)} %pad_add_fusion.refs_0_.info_ref, bf16[1056,512]{1,0:T(8,128)(2,1)S(1)} %shard_map.124.mine_ref, ...), custom_call_target="tpu_custom_call", output_to_operand_aliasing={{0}: (3, {}), {1}: (4, {})} | custom-call | tf_op jit(solution)/shard_map/pallas_call | solution.py:792
  (34 shorter events, 0.3 us)
Async XLA Ops:
  0.6 15.8 %copy-start.5 = (s32[144,144]{1,0:T(8,128)S(1)}, s32[144,144]{1,0:T(8,128)}, u32[]{:S(2)}) copy-start(s32[144,144]{1,0:T(8,128)} %refs_0_.3) | copy-start | bytes 248836
  0.6 15.8 %copy-start.6 = (f32[759,8]{0,1:T(8,128)S(1)}, f32[759,8]{0,1:T(8,128)}, u32[]{:S(2)}) copy-start(f32[759,8]{0,1:T(8,128)} %param.11) | copy-start | bytes 72868
  3.3 20.7 %collective-permute-start.1 = (bf16[512,512]{1,0:T(8,128)(2,1)}, bf16[512,512]{1,0:T(8,128)(2,1)}, u32[]{:S(2)}, u32[]{:S(2)}) collective-permute-start(bf16[512,512]{1,0:T(8,128)(2,1)} %get-tuple-element.58), channel_id=1, source_target_pairs={{0,15},{1,0},{2,1},{3,2},{4,3},{5,4},{6,5},{7,6},{8,7},{9,8},{10,9... | collective-permute-start | bytes 1572872 | tf_op jit(solution)/shard_map/ppermute | solution.py:448
  6.6 17.3 %collective-permute-start.2 = (bf16[80,512]{1,0:T(8,128)(2,1)}, bf16[80,512]{1,0:T(8,128)(2,1)}, u32[]{:S(2)}, u32[]{:S(2)}) collective-permute-start(bf16[80,512]{1,0:T(8,128)(2,1)} %get-tuple-element.59), channel_id=1, source_target_pairs={{0,255},{1,240},{2,241},{3,242},{4,243},{5,244},{6,245},{7,246},{8... | collective-permute-start | bytes 245768 | tf_op jit(solution)/shard_map/ppermute | solution.py:448
  15.3 8.7 %collective-permute-start = (bf16[224,512]{1,0:T(8,128)(2,1)}, bf16[224,512]{1,0:T(8,128)(2,1)}, u32[]{:S(2)}, u32[]{:S(2)}) collective-permute-start(bf16[224,512]{1,0:T(8,128)(2,1)} %get-tuple-element.57), channel_id=1, source_target_pairs={{0,240},{1,241},{2,242},{3,243},{4,244},{5,245},{6,246},{7,247},{8... | collective-permute-start | bytes 688136 | tf_op jit(solution)/shard_map/ppermute | solution.py:448
  16.5 7.5 %copy-start = (bf16[2,24,24,512]{3,2,1,0:T(8,128)(2,1)S(1)}, bf16[2,24,24,512]{3,2,1,0:T(8,128)(2,1)}, u32[]{:S(2)}) copy-start(bf16[2,24,24,512]{3,2,1,0:T(8,128)(2,1)} %refs_0_.2) | copy-start | bytes 3538948
  16.5 7.5 %copy-start.1 = (bf16[2,24,24,512]{3,2,1,0:T(8,128)(2,1)S(1)}, bf16[2,24,24,512]{3,2,1,0:T(8,128)(2,1)}, u32[]{:S(2)}) copy-start(bf16[2,24,24,512]{3,2,1,0:T(8,128)(2,1)} %refs_1_.1) | copy-start | bytes 3538948
  16.5 7.5 %copy-start.4 = (f32[512]{0:T(512)S(1)}, f32[512]{0:T(512)}, u32[]{:S(2)}) copy-start(f32[512]{0:T(512)} %param.8) | copy-start | bytes 6148
  23.2 0.7 copy-start.7
  24.0 1.4 copy-start.2
  25.4 1.0 copy-start.3
  59.3 2.7 %collective-permute-start.3 = (bf16[1024,512]{1,0:T(8,128)(2,1)S(1)}, bf16[1024,512]{1,0:T(8,128)(2,1)S(1)}, u32[]{:S(2)}, u32[]{:S(2)}) collective-permute-start(bf16[1024,512]{1,0:T(8,128)(2,1)S(1)} %get-tuple-element.62), channel_id=1, source_target_pairs={{0,1},{1,0},{2,3},{3,2},{4,5},{5,4},{6,7},{7,6},{8,9},{9,8},{10,11... | collective-permute-start | bytes 3145736 | tf_op jit(solution)/shard_map/ppermute | solution.py:469
  62.8 15.0 %collective-permute-start.4 = (bf16[256,512]{1,0:T(8,128)(2,1)S(1)}, bf16[256,512]{1,0:T(8,128)(2,1)S(1)}, u32[]{:S(2)}, u32[]{:S(2)}) collective-permute-start(bf16[256,512]{1,0:T(8,128)(2,1)S(1)} %get-tuple-element.70), channel_id=1, source_target_pairs={{0,2},{1,3},{2,4},{3,5},{4,6},{5,7},{6,0},{7,1},{8,10},{9,11},{10,... | collective-permute-start | bytes 786440 | tf_op jit(solution)/shard_map/ppermute | solution.py:469
  62.9 14.9 %collective-permute-start.5 = (bf16[256,512]{1,0:T(8,128)(2,1)S(1)}, bf16[256,512]{1,0:T(8,128)(2,1)S(1)}, u32[]{:S(2)}, u32[]{:S(2)}) collective-permute-start(bf16[256,512]{1,0:T(8,128)(2,1)S(1)} %get-tuple-element.71), channel_id=1, source_target_pairs={{0,4},{1,5},{2,6},{3,7},{4,0},{5,1},{6,2},{7,3},{8,12},{9,13},{10,... | collective-permute-start | bytes 786440 | tf_op jit(solution)/shard_map/ppermute | solution.py:469
  65.4 12.4 %collective-permute-start.6 = (bf16[256,512]{1,0:T(8,128)(2,1)S(1)}, bf16[256,512]{1,0:T(8,128)(2,1)S(1)}, u32[]{:S(2)}, u32[]{:S(2)}) collective-permute-start(bf16[256,512]{1,0:T(8,128)(2,1)S(1)} %get-tuple-element.72), channel_id=1, source_target_pairs={{0,6},{1,7},{2,0},{3,1},{4,2},{5,3},{6,4},{7,5},{8,14},{9,15},{10,... | collective-permute-start | bytes 786440 | tf_op jit(solution)/shard_map/ppermute | solution.py:469
  65.6 6.2 %copy-start.8 = (s32[144,144]{1,0:T(8,128)S(1)}, s32[144,144]{1,0:T(8,128)}, u32[]{:S(2)}) copy-start(s32[144,144]{1,0:T(8,128)} %copy-done.7) | copy-start | bytes 248836
  78.6 4.7 %collective-permute-start.7 = (bf16[64,512]{1,0:T(8,128)(2,1)S(1)}, bf16[64,512]{1,0:T(8,128)(2,1)S(1)}, u32[]{:S(2)}, u32[]{:S(2)}) collective-permute-start(bf16[64,512]{1,0:T(8,128)(2,1)S(1)} %get-tuple-element.86), channel_id=1, source_target_pairs={{0,16},{1,17},{2,18},{3,19},{4,20},{5,21},{6,22},{7,23},{8,24},{9,... | collective-permute-start | bytes 196616 | tf_op jit(solution)/shard_map/ppermute | solution.py:469
  79.1 5.0 %collective-permute-start.8 = (bf16[64,512]{1,0:T(8,128)(2,1)S(1)}, bf16[64,512]{1,0:T(8,128)(2,1)S(1)}, u32[]{:S(2)}, u32[]{:S(2)}) collective-permute-start(bf16[64,512]{1,0:T(8,128)(2,1)S(1)} %get-tuple-element.87), channel_id=1, source_target_pairs={{0,8},{1,9},{2,10},{3,11},{4,12},{5,13},{6,14},{7,15},{8,0},{9,1},... | collective-permute-start | bytes 196616 | tf_op jit(solution)/shard_map/ppermute | solution.py:469
  81.3 3.9 %collective-permute-start.9 = (bf16[64,512]{1,0:T(8,128)(2,1)S(1)}, bf16[64,512]{1,0:T(8,128)(2,1)S(1)}, u32[]{:S(2)}, u32[]{:S(2)}) collective-permute-start(bf16[64,512]{1,0:T(8,128)(2,1)S(1)} %get-tuple-element.88), channel_id=1, source_target_pairs={{0,24},{1,25},{2,26},{3,27},{4,28},{5,29},{6,30},{7,31},{8,16},{9,... | collective-permute-start | bytes 196616 | tf_op jit(solution)/shard_map/ppermute | solution.py:469
  85.2 3.6 %collective-permute-start.10 = (bf16[96,512]{1,0:T(8,128)(2,1)S(1)}, bf16[96,512]{1,0:T(8,128)(2,1)S(1)}, u32[]{:S(2)}, u32[]{:S(2)}) collective-permute-start(bf16[96,512]{1,0:T(8,128)(2,1)S(1)} %shard_map.117.mine_ref), channel_id=1, source_target_pairs={{0,32},{1,33},{2,34},{3,35},{4,36},{5,37},{6,38},{7,39},{8,40},{9,... | collective-permute-start | bytes 294920 | tf_op jit(solution)/shard_map/ppermute | solution.py:469
  88.8 6.3 %collective-permute-start.11 = (bf16[96,512]{1,0:T(8,128)(2,1)S(1)}, bf16[96,512]{1,0:T(8,128)(2,1)S(1)}, u32[]{:S(2)}, u32[]{:S(2)}) collective-permute-start(bf16[96,512]{1,0:T(8,128)(2,1)S(1)} %shard_map.118.mine_ref), channel_id=1, source_target_pairs={{0,96},{1,97},{2,98},{3,99},{4,100},{5,101},{6,102},{7,103},{8,104... | collective-permute-start | bytes 294920 | tf_op jit(solution)/shard_map/ppermute | solution.py:469
  95.2 6.7 %collective-permute-start.12 = (bf16[96,512]{1,0:T(8,128)(2,1)S(1)}, bf16[96,512]{1,0:T(8,128)(2,1)S(1)}, u32[]{:S(2)}, u32[]{:S(2)}) collective-permute-start(bf16[96,512]{1,0:T(8,128)(2,1)S(1)} %shard_map.119.mine_ref), channel_id=1, source_target_pairs={{0,224},{1,225},{2,226},{3,227},{4,228},{5,229},{6,230},{7,231},{8... | collective-permute-start | bytes 294920 | tf_op jit(solution)/shard_map/ppermute | solution.py:469
  101.9 5.8 %collective-permute-start.15 = (bf16[96,512]{1,0:T(8,128)(2,1)S(1)}, bf16[96,512]{1,0:T(8,128)(2,1)S(1)}, u32[]{:S(2)}, u32[]{:S(2)}) collective-permute-start(bf16[96,512]{1,0:T(8,128)(2,1)S(1)} %shard_map.120.refs_1_), channel_id=1, source_target_pairs={{0,24},{1,25},{2,26},{3,27},{4,28},{5,29},{6,30},{7,31},{8,16},{9,... | collective-permute-start | bytes 294920 | tf_op jit(solution)/shard_map/ppermute | solution.py:469
  105.0 5.1 %collective-permute-start.14 = (bf16[96,512]{1,0:T(8,128)(2,1)S(1)}, bf16[96,512]{1,0:T(8,128)(2,1)S(1)}, u32[]{:S(2)}, u32[]{:S(2)}) collective-permute-start(bf16[96,512]{1,0:T(8,128)(2,1)S(1)} %shard_map.120.refs_1_), channel_id=1, source_target_pairs={{0,8},{1,9},{2,10},{3,11},{4,12},{5,13},{6,14},{7,15},{8,0},{9,1},... | collective-permute-start | bytes 294920 | tf_op jit(solution)/shard_map/ppermute | solution.py:469
  105.0 5.7 %collective-permute-start.13 = (bf16[96,512]{1,0:T(8,128)(2,1)S(1)}, bf16[96,512]{1,0:T(8,128)(2,1)S(1)}, u32[]{:S(2)}, u32[]{:S(2)}) collective-permute-start(bf16[96,512]{1,0:T(8,128)(2,1)S(1)} %shard_map.120.refs_1_), channel_id=1, source_target_pairs={{0,16},{1,17},{2,18},{3,19},{4,20},{5,21},{6,22},{7,23},{8,24},{9,... | collective-permute-start | bytes 294920 | tf_op jit(solution)/shard_map/ppermute | solution.py:469
  111.4 9.1 %collective-permute-start.16 = (bf16[288,512]{1,0:T(8,128)(2,1)S(1)}, bf16[288,512]{1,0:T(8,128)(2,1)S(1)}, u32[]{:S(2)}, u32[]{:S(2)}) collective-permute-start(bf16[288,512]{1,0:T(8,128)(2,1)S(1)} %shard_map.121.refs_1_), channel_id=1, source_target_pairs={{0,6},{1,7},{2,0},{3,1},{4,2},{5,3},{6,4},{7,5},{8,14},{9,15},{10,... | collective-permute-start | bytes 884744 | tf_op jit(solution)/shard_map/ppermute | solution.py:469
  113.7 17.4 %collective-permute-start.18 = (bf16[288,512]{1,0:T(8,128)(2,1)S(1)}, bf16[288,512]{1,0:T(8,128)(2,1)S(1)}, u32[]{:S(2)}, u32[]{:S(2)}) collective-permute-start(bf16[288,512]{1,0:T(8,128)(2,1)S(1)} %shard_map.121.refs_1_), channel_id=1, source_target_pairs={{0,4},{1,5},{2,6},{3,7},{4,0},{5,1},{6,2},{7,3},{8,12},{9,13},{10,... | collective-permute-start | bytes 884744 | tf_op jit(solution)/shard_map/ppermute | solution.py:469
  114.8 16.3 %collective-permute-start.17 = (bf16[288,512]{1,0:T(8,128)(2,1)S(1)}, bf16[288,512]{1,0:T(8,128)(2,1)S(1)}, u32[]{:S(2)}, u32[]{:S(2)}) collective-permute-start(bf16[288,512]{1,0:T(8,128)(2,1)S(1)} %shard_map.121.refs_1_), channel_id=1, source_target_pairs={{0,2},{1,3},{2,4},{3,5},{4,6},{5,7},{6,0},{7,1},{8,10},{9,11},{10,... | collective-permute-start | bytes 884744 | tf_op jit(solution)/shard_map/ppermute | solution.py:469
  120.8 15.9 %collective-permute-start.20 = (bf16[256,512]{1,0:T(8,128)(2,1)S(1)}, bf16[256,512]{1,0:T(8,128)(2,1)S(1)}, u32[]{:S(2)}, u32[]{:S(2)}) collective-permute-start(bf16[256,512]{1,0:T(8,128)(2,1)S(1)} %get-tuple-element.94), channel_id=1, source_target_pairs={{0,1},{1,2},{2,3},{3,4},{4,5},{5,6},{6,7},{7,8},{8,9},{9,10},{10,1... | collective-permute-start | bytes 786440 | tf_op jit(solution)/shard_map/ppermute | solution.py:448
  130.1 6.6 %collective-permute-start.19 = (bf16[112,512]{1,0:T(8,128)(2,1)S(1)}, bf16[112,512]{1,0:T(8,128)(2,1)S(1)}, u32[]{:S(2)}, u32[]{:S(2)}) collective-permute-start(bf16[112,512]{1,0:T(8,128)(2,1)S(1)} %get-tuple-element.93), channel_id=1, source_target_pairs={{0,16},{1,17},{2,18},{3,19},{4,20},{5,21},{6,22},{7,23},{8,24},{9,... | collective-permute-start | bytes 344072 | tf_op jit(solution)/shard_map/ppermute | solution.py:448
  130.1 6.4 %collective-permute-start.21 = (bf16[48,512]{1,0:T(8,128)(2,1)S(1)}, bf16[48,512]{1,0:T(8,128)(2,1)S(1)}, u32[]{:S(2)}, u32[]{:S(2)}) collective-permute-start(bf16[48,512]{1,0:T(8,128)(2,1)S(1)} %get-tuple-element.95), channel_id=1, source_target_pairs={{0,17},{1,18},{2,19},{3,20},{4,21},{5,22},{6,23},{7,24},{8,25},{9,... | collective-permute-start | bytes 147464 | tf_op jit(solution)/shard_map/ppermute | solution.py:448
  137.3 7.1 %collective-permute-start.22 = (bf16[1056,512]{1,0:T(8,128)(2,1)S(1)}, bf16[1056,512]{1,0:T(8,128)(2,1)S(1)}, u32[]{:S(2)}, u32[]{:S(2)}) collective-permute-start(bf16[1056,512]{1,0:T(8,128)(2,1)S(1)} %shard_map.124.mine_ref), channel_id=1, source_target_pairs={{0,1},{1,0},{2,3},{3,2},{4,5},{5,4},{6,7},{7,6},{8,9},{9,8},{10,11... | collective-permute-start | bytes 3244040 | tf_op jit(solution)/shard_map/ppermute | solution.py:469

commit v3 on v2

--- a/solution.py
+++ b/solution.py
@@ -354,12 +354,12 @@
     send_ref[...] = grads[1 - info_ref[CORE]]
 
 
-def back_kernel(geo, dproj, unit_ref, inv, cotb, gain_ref, wqkv_ref, gtok_ref):
+def back_kernel(geo, first, count, dproj, unit_ref, inv, cotb, gain_ref, wqkv_ref, gtok_ref):
     win = geo.win
     gain = gain_ref[...]
 
     def back_step(w, carry):
-        at = pl.ds(pl.multiple_of(w * win, 16), win)
+        at = pl.ds(pl.multiple_of((first + w) * win, 16), win)
         gn = dot_nt(dproj[at, :], wqkv_ref[...]).astype(BF16).astype(F32)
         unit = unit_ref[at, :]
         hat = gn * gain
@@ -367,16 +367,19 @@
         slope = jnp.mean(hat * unit, axis=-1, keepdims=True)
         istd = inv[at, 0:1]
         cot = cotb[at, :].astype(F32)
-        gtok_ref[at, :] = (cot + istd * (hat - centre - unit * slope)).astype(BF16)
+        to = pl.ds(pl.multiple_of(w * win, 16), win)
+        gtok_ref[to, :] = (cot + istd * (hat - centre - unit * slope)).astype(BF16)
         return carry
 
-    lax.fori_loop(0, geo.nwin, back_step, 0)
-
-
-def unpack_send_kernel(geo, gtok_ref, rows_ref, cols_ref, corner_ref, fg, buf):
+    lax.fori_loop(0, count, back_step, 0)
+
+
+def unpack_send_kernel(geo, low_ref, high_ref, rows_ref, cols_ref, corner_ref, fg, buf):
     base_cols = pad16(geo.n_rows)
     base_corner = base_cols + pad16(geo.n_cols)
-    fg[...] = gtok_ref[...].astype(F32)
+    half = low_ref.shape[0]
+    fg[0:half] = low_ref[...].astype(F32)
+    fg[half:] = high_ref[...].astype(F32)
     buf[...] = jnp.zeros_like(buf)
     bases = {"rows": 0, "cols": base_cols, "corner": base_corner}
     for z in range(geo.depth):
@@ -393,8 +396,10 @@
     corner_ref[...] = buf[base_corner : base_corner + pad16(geo.n_corner)].astype(BF16)
 
 
-def assemble_kernel(geo, gtok_ref, rows_ref, cols_ref, corner_ref, out_ref, fg, rr, rc, rk, grid):
-    fg[...] = gtok_ref[...].astype(F32)
+def assemble_kernel(geo, low_ref, high_ref, rows_ref, cols_ref, corner_ref, out_ref, fg, rr, rc, rk, grid):
+    half = low_ref.shape[0]
+    fg[0:half] = low_ref[...].astype(F32)
+    fg[half:] = high_ref[...].astype(F32)
     rr[...] = rows_ref[...].astype(F32)
     rc[...] = cols_ref[...].astype(F32)
     rk[...] = corner_ref[...].astype(F32)
@@ -687,19 +692,9 @@
         smem_first=True,
     )(info, keep, got)
 
-    outs, grad_proj, qkv_weight, bias_sum = lax.optimization_barrier(
-        (outs, grad_proj, qkv_weight, bias_sum)
-    )
+    outs, bias_sum = lax.optimization_barrier((outs, bias_sum))
     got = [outs[0]] + [chips.y(outs[k], k) for k in range(1, ny)]
     gain_row = norm_gain.reshape(1, width)
-    gtok = call(
-        lambda *refs: back_kernel(geo, *refs),
-        shape((cells, width), BF16),
-        [],
-        6,
-        small_limit,
-        cost=pl.CostEstimate(flops=6 * 10**9, bytes_accessed=10**7, transcendentals=0),
-    )(grad_proj, unit, inv, cot_win, gain_row, qkv_weight)
     small = call(
         lambda *refs: table_kernel(heads, *refs),
         shape((SMALL, width), F32),
@@ -708,7 +703,7 @@
         small_limit,
         cost=pl.CostEstimate(flops=3 * 10**9, bytes_accessed=10**6, transcendentals=0),
     )(index_t, bias_sum, gain_sum, gain_row)
-    got, gtok, small = lax.optimization_barrier((got, gtok, small))
+    got, small = lax.optimization_barrier((got, small))
     part = piece // nx
     outs = call(
         lambda *refs: cross_sum_kernel(ny, nx, *refs),
@@ -727,11 +722,26 @@
         nx + 1,
         small_limit,
     )(*got, small)
+    def layer_norm_back(first, count, proj):
+        return call(
+            lambda *refs: back_kernel(geo, first, count, *refs),
+            shape((count * win, width), BF16),
+            [],
+            6,
+            small_limit,
+            cost=pl.CostEstimate(flops=3 * 10**9, bytes_accessed=10**7, transcendentals=0),
+        )(proj, unit, inv, cot_win, gain_row, qkv_weight)
+
+    half_wins = geo.nwin // 2
+    halves = []
     bit = 1
     while bit < chips.nz:
-        mine = call(z_sum_kernel, shape(mine.shape, BF16), [], 2, small_limit)(
-            mine, chips.z(mine, bit)
-        )
+        mine, grad_proj = lax.optimization_barrier((mine, grad_proj))
+        got = chips.z(mine, bit)
+        if len(halves) < 2:
+            halves.append(layer_norm_back(len(halves) * half_wins, half_wins, grad_proj))
+            got, halves[-1] = lax.optimization_barrier((got, halves[-1]))
+        mine = call(z_sum_kernel, shape(mine.shape, BF16), [], 2, small_limit)(mine, got)
         bit *= 2
 
     def gathered(place, count, parts):
@@ -745,10 +755,7 @@
             smem_first=True,
         )(info, *parts)
 
-    mine = gathered(X, nx, [mine] + [chips.x(mine, k) for k in range(1, nx)])
-    parts = [mine] + [chips.y(mine, k) for k in range(1, ny)]
-
-    parts[-1], gtok = lax.optimization_barrier((parts[-1], gtok))
+    mine, halves = lax.optimization_barrier((mine, halves))
     b_rows, b_cols, b_corner = pad16(geo.n_rows), pad16(geo.n_cols), pad16(geo.n_corner)
     back = call(
         lambda *refs: unpack_send_kernel(geo, *refs),
@@ -757,11 +764,15 @@
             pltpu.VMEM((cells, width), F32),
             pltpu.VMEM((b_rows + b_cols + b_corner, width), F32),
         ],
-        1,
+        2,
         small_limit,
-    )(gtok)
+    )(*halves)
     back = (moved(back[0], -1, 0), moved(back[1], 0, -1), moved(back[2], -1, -1))
+    parts = [mine] + [chips.x(mine, k) for k in range(1, nx)]
     parts, back = lax.optimization_barrier((parts, back))
+    mine = gathered(X, nx, parts)
+    parts = [mine] + [chips.y(mine, k) for k in range(1, ny)]
+
     grad_tokens = call(
         lambda *refs: assemble_kernel(geo, *refs),
         shape((cells, width), BF16),
@@ -772,9 +783,10 @@
             pltpu.VMEM((b_corner, width), F32),
             pltpu.VMEM((cells, width), F32),
         ],
-        4,
+        5,
         small_limit,
-    )(gtok, *back)
+    )(*halves, *back)
+    parts, grad_tokens = lax.optimization_barrier((parts, grad_tokens))
     mine = gathered(Y, ny, parts)
     other = chips.core(mine)
 

time: 147 us -> 147 us (level)
  starting transfers between devices: 52.2 us -> 44.1 us
  waiting for transfers between devices: 27 us -> 34.9 us
    ppermute x17, waiting for transfers between devices: 21.4 us -> 32 us  [send(): return lax.ppermute(value, ('lat', 'lon'), pairs)]
    ppermute x6, starting transfers between devices: 23.4 us -> 18.5 us  [moved(): return lax.ppermute(value, ('lat', 'lon'), pairs)]
    ppermute x17, starting transfers between devices: 28.8 us -> 25.6 us  [send(): return lax.ppermute(value, ('lat', 'lon'), pairs)]
    ppermute x6, waiting for transfers between devices: 5.57 us -> 2.84 us  [moved(): return lax.ppermute(value, ('lat', 'lon'), pairs)]
    pallas_call x4 -> x5, Pallas kernels: 6.28 us -> 6.29 us  [the longest x2 6.19 us: layer_norm_back(): call(lambda *refs: back_kernel(geo, first, count, *refs), shape((count *...]
  transfers between devices with their start and end apart: 23 -> 23, of which waited for: 12 -> 13; matrix products, arithmetic and copies ran while one was open for 0% -> 0% of each run, Pallas kernels for 16% -> 15%
where the time goes in v3:
time: 147 us
  Pallas kernels  63.8 us (43%)
  starting transfers between devices  44.1 us (30%)
  waiting for transfers between devices  34.9 us (24%)
  local copies, waits for them, and re-layouts  3.13 us (2%)
    pallas_call x1, Pallas kernels, per_device(): pl.pallas_call(lambda *refs: main_kernel(geo, heads, *refs), in_specs=[sm...  32.8 us
    ppermute x17, waiting for transfers between devices, send(): return lax.ppermute(value, ('lat', 'lon'), pairs)  32 us
    ppermute x17, starting transfers between devices, send(): return lax.ppermute(value, ('lat', 'lon'), pairs)  25.6 us
    ppermute x6, starting transfers between devices, moved(): return lax.ppermute(value, ('lat', 'lon'), pairs)  18.5 us
    pallas_call x1, Pallas kernels, per_device(): call(lambda *refs: lookup_kernel(heads, *refs), [shape((heads, win, win),...  6.74 us
    pallas_call x2, Pallas kernels, layer_norm_back(): call(lambda *refs: back_kernel(geo, first, count, *refs), shape((count *...  6.19 us
    pallas_call x1, Pallas kernels, per_device(): call(lambda *refs: table_kernel(heads, *refs), shape((SMALL, width), F32)...  6.01 us
    unnamed x18, local copies, waits for them, and re-layouts  3.13 us
  transfers between devices with their start and end apart: 23, of which 13 were waited for; matrix products, arithmetic and copies ran while one was open for 0% of the time, Pallas kernels for 15%

profile of v3, /device:TPU:1, one launch (start us, length us, event | category | flops | bytes accessed | tf_op | source)
XLA Modules:
  0.0 147.0 jit_solution(758586427887663573)
XLA Ops:
  0.7 2.7 %shard_map.110 = (bf16[224,512]{1,0:T(8,128)(2,1)}, bf16[512,512]{1,0:T(8,128)(2,1)}, bf16[80,512]{1,0:T(8,128)(2,1)}) custom-call(bf16[2,24,24,512]{3,2,1,0:T(8,128)(2,1)} %refs_0_.2, bf16[2,24,24,512]{3,2,1,0:T(8,128)(2,1)} %refs_1_.1), custom_call_target="tpu_custom_call" | custom-call | tf_op jit(solution)/shard_map/pallas_call | solution.py:611
  3.3 3.3 %collective-permute-start.1 = (bf16[512,512]{1,0:T(8,128)(2,1)}, bf16[512,512]{1,0:T(8,128)(2,1)}, u32[]{:S(2)}, u32[]{:S(2)}) collective-permute-start(bf16[512,512]{1,0:T(8,128)(2,1)} %get-tuple-element.70), channel_id=1, source_target_pairs={{0,15},{1,0},{2,1},{3,2},{4,3},{5,4},{6,5},{7,6},{8,7},{9,8},{10,9... | collective-permute-start | bytes 1572872 | tf_op jit(solution)/shard_map/ppermute | solution.py:453
  6.6 8.7 %collective-permute-start.2 = (bf16[80,512]{1,0:T(8,128)(2,1)}, bf16[80,512]{1,0:T(8,128)(2,1)}, u32[]{:S(2)}, u32[]{:S(2)}) collective-permute-start(bf16[80,512]{1,0:T(8,128)(2,1)} %get-tuple-element.71), channel_id=1, source_target_pairs={{0,255},{1,240},{2,241},{3,242},{4,243},{5,244},{6,245},{7,246},{8... | collective-permute-start | bytes 245768 | tf_op jit(solution)/shard_map/ppermute | solution.py:453
  15.3 1.2 collective-permute-start
  16.5 6.7 %shard_map.111 = (f32[8,144,144]{2,1,0:T(8,128)S(1)}, s32[144,144]{1,0:T(8,128)S(1)}) custom-call(s32[144,144]{1,0:T(8,128)S(1)} %copy-done.5, f32[8,759]{1,0:T(8,128)S(1)} %bitcast.18), custom_call_target="tpu_custom_call" | custom-call | flops 4000000000 | bytes 1000000 | tf_op jit(solution)/shard_map/pallas_call | solution.py:628
  23.2 0.7 copy-done.7
  24.0 1.4 copy-done.2
  25.4 1.0 copy-done.3
  26.5 32.8 %shard_map.112 = (bf16[1024,512]{1,0:T(8,128)(2,1)S(1)}, bf16[1024,512]{1,0:T(8,128)(2,1)S(1)}, f32[8,144,144]{2,1,0:T(8,128)S(1)}, bf16[1152,1536]{1,0:T(8,128)...) custom-call(s32[4]{0:T(128)S(1)} %pad_add_fusion.refs_0_.info_ref, ...), custom_call_target="tpu_custom_call" | custom-call | tf_op jit(solution)/shard_map/pallas_call | solution.py:648
  59.4 2.6 %collective-permute-done.3.recv_ref = bf16[1024,512]{1,0:T(8,128)(2,1)S(1)} collective-permute-done((bf16[1024,512]{1,0:T(8,128)(2,1)S(1)}, bf16[1024,512]{1,0:T(8,128)(2,1)S(1)}, u32[]{:S(2)}, u32[]{:S(2)}) %collective-permute-start.3) | collective-permute-done | bytes 1048608 | tf_op jit(solution)/shard_map/ppermute | solution.py:474
  62.0 0.8 shard_map.113
  62.9 2.5 %collective-permute-start.5 = (bf16[256,512]{1,0:T(8,128)(2,1)S(1)}, bf16[256,512]{1,0:T(8,128)(2,1)S(1)}, u32[]{:S(2)}, u32[]{:S(2)}) collective-permute-start(bf16[256,512]{1,0:T(8,128)(2,1)S(1)} %get-tuple-element.82), channel_id=1, source_target_pairs={{0,4},{1,5},{2,6},{3,7},{4,0},{5,1},{6,2},{7,3},{8,12},{9,13},{10,... | collective-permute-start | bytes 786440 | tf_op jit(solution)/shard_map/ppermute | solution.py:474
  65.4 0.2 collective-permute-start.6
  65.6 6.0 %shard_map.114.refs_4_ = f32[16,512]{1,0:T(8,128)S(1)} custom-call(s32[144,144]{1,0:T(8,128)S(1)} %copy-done.8, f32[8,144,144]{2,1,0:T(8,128)S(1)} %get-tuple-element.85.refs_1_, f32[512,128]{1,0:T(8,128)S(1)} %get-tuple-element.86.refs_2_, f32[1,512]{1,0:T(1,128)S(1)} %bitcast.15), custom_call_target="tpu_custom_call" | custom-call | flops 3000000000 | bytes 1000000 | tf_op jit(solution)/shard_map/pallas_call | solution.py:698
  71.6 0.5 collective-permute-done.4.refs_2_
  72.1 5.3 %collective-permute-done.5.refs_3_ = bf16[256,512]{1,0:T(8,128)(2,1)S(1)} collective-permute-done((bf16[256,512]{1,0:T(8,128)(2,1)S(1)}, bf16[256,512]{1,0:T(8,128)(2,1)S(1)}, u32[]{:S(2)}, u32[]{:S(2)}) %collective-permute-start.5) | collective-permute-done | bytes 262176 | tf_op jit(solution)/shard_map/ppermute | solution.py:474
  77.4 0.4 collective-permute-done.6.refs_4_
  77.8 0.8 shard_map.115
  78.6 0.3 collective-permute-start.7
  78.9 2.1 %collective-permute-start.8 = (bf16[64,512]{1,0:T(8,128)(2,1)S(1)}, bf16[64,512]{1,0:T(8,128)(2,1)S(1)}, u32[]{:S(2)}, u32[]{:S(2)}) collective-permute-start(bf16[64,512]{1,0:T(8,128)(2,1)S(1)} %get-tuple-element.93), channel_id=1, source_target_pairs={{0,8},{1,9},{2,10},{3,11},{4,12},{5,13},{6,14},{7,15},{8,0},{9,1},... | collective-permute-start | bytes 196616 | tf_op jit(solution)/shard_map/ppermute | solution.py:474
  81.0 2.0 %collective-permute-start.9 = (bf16[64,512]{1,0:T(8,128)(2,1)S(1)}, bf16[64,512]{1,0:T(8,128)(2,1)S(1)}, u32[]{:S(2)}, u32[]{:S(2)}) collective-permute-start(bf16[64,512]{1,0:T(8,128)(2,1)S(1)} %get-tuple-element.94), channel_id=1, source_target_pairs={{0,24},{1,25},{2,26},{3,27},{4,28},{5,29},{6,30},{7,31},{8,16},{9,... | collective-permute-start | bytes 196616 | tf_op jit(solution)/shard_map/ppermute | solution.py:474
  83.0 0.7 collective-permute-done.7.refs_1_
  83.7 0.9 collective-permute-done.9.refs_3_
  84.6 2.0 %collective-permute-start.10 = (bf16[96,512]{1,0:T(8,128)(2,1)S(1)}, bf16[96,512]{1,0:T(8,128)(2,1)S(1)}, u32[]{:S(2)}, u32[]{:S(2)}) collective-permute-start(bf16[96,512]{1,0:T(8,128)(2,1)S(1)} %shard_map.116.mine_ref), channel_id=1, source_target_pairs={{0,32},{1,33},{2,34},{3,35},{4,36},{5,37},{6,38},{7,39},{8,40},{9,... | collective-permute-start | bytes 294920 | tf_op jit(solution)/shard_map/ppermute | solution.py:474
  86.6 3.1 %shard_map.117.refs_0_ = bf16[576,512]{1,0:T(8,128)(2,1)S(1)} custom-call(bf16[1152,1536]{1,0:T(8,128)(2,1)S(1)} %get-tuple-element.104.refs_0_, f32[1152,512]{1,0:T(8,128)S(1)} %get-tuple-element.99.refs_1_, f32[1152,128]{1,0:T(8,128)S(1)} %get-tuple-element.100.refs_2_, bf16[1152,512]{1,0:T(8,128)(2,1)S(1)} %get-tuple-element.101.refs_3_, ...), custom_call_target="tpu_custom_call" | custom-call | flops 3000000000 | bytes 10000000 | tf_op jit(solution)/shard_map/pallas_call | solution.py:726
  89.8 3.1 %collective-permute-start.11 = (bf16[96,512]{1,0:T(8,128)(2,1)S(1)}, bf16[96,512]{1,0:T(8,128)(2,1)S(1)}, u32[]{:S(2)}, u32[]{:S(2)}) collective-permute-start(bf16[96,512]{1,0:T(8,128)(2,1)S(1)} %shard_map.118.mine_ref), channel_id=1, source_target_pairs={{0,96},{1,97},{2,98},{3,99},{4,100},{5,101},{6,102},{7,103},{8,104... | collective-permute-start | bytes 294920 | tf_op jit(solution)/shard_map/ppermute | solution.py:474
  92.9 3.1 %shard_map.119.refs_1_ = bf16[576,512]{1,0:T(8,128)(2,1)S(1)} custom-call(bf16[1152,1536]{1,0:T(8,128)(2,1)S(1)} %get-tuple-element.104.refs_0_, f32[1152,512]{1,0:T(8,128)S(1)} %get-tuple-element.99.refs_1_, f32[1152,128]{1,0:T(8,128)S(1)} %get-tuple-element.100.refs_2_, bf16[1152,512]{1,0:T(8,128)(2,1)S(1)} %get-tuple-element.101.refs_3_, ...), custom_call_target="tpu_custom_call" | custom-call | flops 3000000000 | bytes 10000000 | tf_op jit(solution)/shard_map/pallas_call | solution.py:726
  96.0 3.9 %collective-permute-start.12 = (bf16[96,512]{1,0:T(8,128)(2,1)S(1)}, bf16[96,512]{1,0:T(8,128)(2,1)S(1)}, u32[]{:S(2)}, u32[]{:S(2)}) collective-permute-start(bf16[96,512]{1,0:T(8,128)(2,1)S(1)} %shard_map.120.mine_ref), channel_id=1, source_target_pairs={{0,224},{1,225},{2,226},{3,227},{4,228},{5,229},{6,230},{7,231},{8... | collective-permute-start | bytes 294920 | tf_op jit(solution)/shard_map/ppermute | solution.py:474
  99.9 2.7 %collective-permute-done.12.got_ref = bf16[96,512]{1,0:T(8,128)(2,1)S(1)} collective-permute-done((bf16[96,512]{1,0:T(8,128)(2,1)S(1)}, bf16[96,512]{1,0:T(8,128)(2,1)S(1)}, u32[]{:S(2)}, u32[]{:S(2)}) %collective-permute-start.12) | collective-permute-done | bytes 98336 | tf_op jit(solution)/shard_map/ppermute | solution.py:474
  102.7 0.3 shard_map.122
  103.0 3.9 %collective-permute-start.17 = (bf16[256,512]{1,0:T(8,128)(2,1)S(1)}, bf16[256,512]{1,0:T(8,128)(2,1)S(1)}, u32[]{:S(2)}, u32[]{:S(2)}) collective-permute-start(bf16[256,512]{1,0:T(8,128)(2,1)S(1)} %get-tuple-element.113), channel_id=1, source_target_pairs={{0,1},{1,2},{2,3},{3,4},{4,5},{5,6},{6,7},{7,8},{8,9},{9,10},{10,1... | collective-permute-start | bytes 786440 | tf_op jit(solution)/shard_map/ppermute | solution.py:453
  106.9 1.2 collective-permute-start.18
  108.1 0.2 collective-permute-start.16
  108.3 2.8 %collective-permute-start.15 = (bf16[96,512]{1,0:T(8,128)(2,1)S(1)}, bf16[96,512]{1,0:T(8,128)(2,1)S(1)}, u32[]{:S(2)}, u32[]{:S(2)}) collective-permute-start(bf16[96,512]{1,0:T(8,128)(2,1)S(1)} %shard_map.121.refs_1_), channel_id=1, source_target_pairs={{0,24},{1,25},{2,26},{3,27},{4,28},{5,29},{6,30},{7,31},{8,16},{9,... | collective-permute-start | bytes 294920 | tf_op jit(solution)/shard_map/ppermute | solution.py:474
  111.2 2.8 %collective-permute-done.18.refs_4_ = bf16[48,512]{1,0:T(8,128)(2,1)S(1)} collective-permute-done((bf16[48,512]{1,0:T(8,128)(2,1)S(1)}, bf16[48,512]{1,0:T(8,128)(2,1)S(1)}, u32[]{:S(2)}, u32[]{:S(2)}) %collective-permute-start.18) | collective-permute-done | bytes 49184 | tf_op jit(solution)/shard_map/ppermute | solution.py:453
  114.1 2.7 %collective-permute-done.14.refs_3_ = bf16[96,512]{1,0:T(8,128)(2,1)S(1)} collective-permute-done((bf16[96,512]{1,0:T(8,128)(2,1)S(1)}, bf16[96,512]{1,0:T(8,128)(2,1)S(1)}, u32[]{:S(2)}, u32[]{:S(2)}) %collective-permute-start.14) | collective-permute-done | bytes 98336 | tf_op jit(solution)/shard_map/ppermute | solution.py:474
  116.8 2.0 %collective-permute-done.13.refs_2_ = bf16[96,512]{1,0:T(8,128)(2,1)S(1)} collective-permute-done((bf16[96,512]{1,0:T(8,128)(2,1)S(1)}, bf16[96,512]{1,0:T(8,128)(2,1)S(1)}, u32[]{:S(2)}, u32[]{:S(2)}) %collective-permute-start.13) | collective-permute-done | bytes 98336 | tf_op jit(solution)/shard_map/ppermute | solution.py:474
  118.8 0.6 shard_map.123.refs_1_
  119.4 4.9 %collective-permute-start.21 = (bf16[288,512]{1,0:T(8,128)(2,1)S(1)}, bf16[288,512]{1,0:T(8,128)(2,1)S(1)}, u32[]{:S(2)}, u32[]{:S(2)}) collective-permute-start(bf16[288,512]{1,0:T(8,128)(2,1)S(1)} %shard_map.123.refs_1_), channel_id=1, source_target_pairs={{0,6},{1,7},{2,0},{3,1},{4,2},{5,3},{6,4},{7,5},{8,14},{9,15},{10,... | collective-permute-start | bytes 884744 | tf_op jit(solution)/shard_map/ppermute | solution.py:474
  124.3 0.7 collective-permute-start.19
  125.0 1.7 %shard_map.124 = bf16[1152,512]{1,0:T(8,128)(2,1)} custom-call(bf16[576,512]{1,0:T(8,128)(2,1)S(1)} %shard_map.117.refs_0_, bf16[576,512]{1,0:T(8,128)(2,1)S(1)} %shard_map.119.refs_1_, bf16[112,512]{1,0:T(8,128)(2,1)S(1)} %collective-permute-done.16.refs_2_, bf16[256,512]{1,0:T(8,128)(2,1)S(1)} %collective-permute-done.17.refs_3_, ...), custom_call_target="tpu_custom_call" | custom-call | tf_op jit(solution)/shard_map/pallas_call | solution.py:776
  126.6 10.3 %collective-permute-done.21.refs_4_ = bf16[288,512]{1,0:T(8,128)(2,1)S(1)} collective-permute-done((bf16[288,512]{1,0:T(8,128)(2,1)S(1)}, bf16[288,512]{1,0:T(8,128)(2,1)S(1)}, u32[]{:S(2)}, u32[]{:S(2)}) %collective-permute-start.21) | collective-permute-done | bytes 294944 | tf_op jit(solution)/shard_map/ppermute | solution.py:474
  136.9 3.5 %collective-permute-done.19.refs_2_ = bf16[288,512]{1,0:T(8,128)(2,1)S(1)} collective-permute-done((bf16[288,512]{1,0:T(8,128)(2,1)S(1)}, bf16[288,512]{1,0:T(8,128)(2,1)S(1)}, u32[]{:S(2)}, u32[]{:S(2)}) %collective-permute-start.19) | collective-permute-done | bytes 294944 | tf_op jit(solution)/shard_map/ppermute | solution.py:474
  140.4 0.6 shard_map.125.mine_ref
  141.0 0.9 collective-permute-start.22
  142.0 1.9 %shard_map.126 = (f32[512,1536]{1,0:T(8,128)}, f32[512,512]{1,0:T(8,128)}) custom-call(s32[4]{0:T(128)S(1)} %pad_add_fusion.refs_0_.info_ref, bf16[1056,512]{1,0:T(8,128)(2,1)S(1)} %shard_map.125.mine_ref), custom_call_target="tpu_custom_call" | custom-call | tf_op jit(solution)/shard_map/pallas_call | solution.py:796
  143.9 0.4 collective-permute-done.22.got_ref
  144.3 2.5 %shard_map.127 = (f32[512,1536]{1,0:T(8,128)}, f32[512,512]{1,0:T(8,128)}, f32[8,768]{1,0:T(8,128)}, f32[1,512]{1,0:T(1,128)}) custom-call(s32[4]{0:T(128)S(1)} %pad_add_fusion.refs_0_.info_ref, bf16[1056,512]{1,0:T(8,128)(2,1)S(1)} %shard_map.125.mine_ref, ...), custom_call_target="tpu_custom_call", output_to_operand_aliasing={{0}: (3, {}), {1}: (4, {})} | custom-call | tf_op jit(solution)/shard_map/pallas_call | solution.py:804
  (35 shorter events, 0.5 us)
Async XLA Ops:
  0.6 15.8 %copy-start.5 = (s32[144,144]{1,0:T(8,128)S(1)}, s32[144,144]{1,0:T(8,128)}, u32[]{:S(2)}) copy-start(s32[144,144]{1,0:T(8,128)} %refs_0_.3) | copy-start | bytes 248836
  0.6 15.8 %copy-start.6 = (f32[759,8]{0,1:T(8,128)S(1)}, f32[759,8]{0,1:T(8,128)}, u32[]{:S(2)}) copy-start(f32[759,8]{0,1:T(8,128)} %param.11) | copy-start | bytes 72868
  3.3 20.7 %collective-permute-start.1 = (bf16[512,512]{1,0:T(8,128)(2,1)}, bf16[512,512]{1,0:T(8,128)(2,1)}, u32[]{:S(2)}, u32[]{:S(2)}) collective-permute-start(bf16[512,512]{1,0:T(8,128)(2,1)} %get-tuple-element.70), channel_id=1, source_target_pairs={{0,15},{1,0},{2,1},{3,2},{4,3},{5,4},{6,5},{7,6},{8,7},{9,8},{10,9... | collective-permute-start | bytes 1572872 | tf_op jit(solution)/shard_map/ppermute | solution.py:453
  6.6 17.3 %collective-permute-start.2 = (bf16[80,512]{1,0:T(8,128)(2,1)}, bf16[80,512]{1,0:T(8,128)(2,1)}, u32[]{:S(2)}, u32[]{:S(2)}) collective-permute-start(bf16[80,512]{1,0:T(8,128)(2,1)} %get-tuple-element.71), channel_id=1, source_target_pairs={{0,255},{1,240},{2,241},{3,242},{4,243},{5,244},{6,245},{7,246},{8... | collective-permute-start | bytes 245768 | tf_op jit(solution)/shard_map/ppermute | solution.py:453
  15.3 8.7 %collective-permute-start = (bf16[224,512]{1,0:T(8,128)(2,1)}, bf16[224,512]{1,0:T(8,128)(2,1)}, u32[]{:S(2)}, u32[]{:S(2)}) collective-permute-start(bf16[224,512]{1,0:T(8,128)(2,1)} %get-tuple-element.69), channel_id=1, source_target_pairs={{0,240},{1,241},{2,242},{3,243},{4,244},{5,245},{6,246},{7,247},{8... | collective-permute-start | bytes 688136 | tf_op jit(solution)/shard_map/ppermute | solution.py:453
  16.5 7.5 %copy-start = (bf16[2,24,24,512]{3,2,1,0:T(8,128)(2,1)S(1)}, bf16[2,24,24,512]{3,2,1,0:T(8,128)(2,1)}, u32[]{:S(2)}) copy-start(bf16[2,24,24,512]{3,2,1,0:T(8,128)(2,1)} %refs_0_.2) | copy-start | bytes 3538948
  16.5 7.5 %copy-start.1 = (bf16[2,24,24,512]{3,2,1,0:T(8,128)(2,1)S(1)}, bf16[2,24,24,512]{3,2,1,0:T(8,128)(2,1)}, u32[]{:S(2)}) copy-start(bf16[2,24,24,512]{3,2,1,0:T(8,128)(2,1)} %refs_1_.1) | copy-start | bytes 3538948
  16.5 7.5 %copy-start.4 = (f32[512]{0:T(512)S(1)}, f32[512]{0:T(512)}, u32[]{:S(2)}) copy-start(f32[512]{0:T(512)} %param.8) | copy-start | bytes 6148
  23.2 0.7 copy-start.7
  24.0 1.4 copy-start.2
  25.4 1.0 copy-start.3
  59.3 6.3 %copy-start.8 = (s32[144,144]{1,0:T(8,128)S(1)}, s32[144,144]{1,0:T(8,128)}, u32[]{:S(2)}) copy-start(s32[144,144]{1,0:T(8,128)} %copy-done.7) | copy-start | bytes 248836
  59.3 2.7 %collective-permute-start.3 = (bf16[1024,512]{1,0:T(8,128)(2,1)S(1)}, bf16[1024,512]{1,0:T(8,128)(2,1)S(1)}, u32[]{:S(2)}, u32[]{:S(2)}) collective-permute-start(bf16[1024,512]{1,0:T(8,128)(2,1)S(1)} %get-tuple-element.74), channel_id=1, source_target_pairs={{0,1},{1,0},{2,3},{3,2},{4,5},{5,4},{6,7},{7,6},{8,9},{9,8},{10,11... | collective-permute-start | bytes 3145736 | tf_op jit(solution)/shard_map/ppermute | solution.py:474
  62.8 9.2 %collective-permute-start.4 = (bf16[256,512]{1,0:T(8,128)(2,1)S(1)}, bf16[256,512]{1,0:T(8,128)(2,1)S(1)}, u32[]{:S(2)}, u32[]{:S(2)}) collective-permute-start(bf16[256,512]{1,0:T(8,128)(2,1)S(1)} %get-tuple-element.81), channel_id=1, source_target_pairs={{0,2},{1,3},{2,4},{3,5},{4,6},{5,7},{6,0},{7,1},{8,10},{9,11},{10,... | collective-permute-start | bytes 786440 | tf_op jit(solution)/shard_map/ppermute | solution.py:474
  62.9 14.4 %collective-permute-start.5 = (bf16[256,512]{1,0:T(8,128)(2,1)S(1)}, bf16[256,512]{1,0:T(8,128)(2,1)S(1)}, u32[]{:S(2)}, u32[]{:S(2)}) collective-permute-start(bf16[256,512]{1,0:T(8,128)(2,1)S(1)} %get-tuple-element.82), channel_id=1, source_target_pairs={{0,4},{1,5},{2,6},{3,7},{4,0},{5,1},{6,2},{7,3},{8,12},{9,13},{10,... | collective-permute-start | bytes 786440 | tf_op jit(solution)/shard_map/ppermute | solution.py:474
  65.4 12.4 %collective-permute-start.6 = (bf16[256,512]{1,0:T(8,128)(2,1)S(1)}, bf16[256,512]{1,0:T(8,128)(2,1)S(1)}, u32[]{:S(2)}, u32[]{:S(2)}) collective-permute-start(bf16[256,512]{1,0:T(8,128)(2,1)S(1)} %get-tuple-element.83), channel_id=1, source_target_pairs={{0,6},{1,7},{2,0},{3,1},{4,2},{5,3},{6,4},{7,5},{8,14},{9,15},{10,... | collective-permute-start | bytes 786440 | tf_op jit(solution)/shard_map/ppermute | solution.py:474
  78.6 5.1 %collective-permute-start.7 = (bf16[64,512]{1,0:T(8,128)(2,1)S(1)}, bf16[64,512]{1,0:T(8,128)(2,1)S(1)}, u32[]{:S(2)}, u32[]{:S(2)}) collective-permute-start(bf16[64,512]{1,0:T(8,128)(2,1)S(1)} %get-tuple-element.92), channel_id=1, source_target_pairs={{0,16},{1,17},{2,18},{3,19},{4,20},{5,21},{6,22},{7,23},{8,24},{9,... | collective-permute-start | bytes 196616 | tf_op jit(solution)/shard_map/ppermute | solution.py:474
  78.9 4.8 %collective-permute-start.8 = (bf16[64,512]{1,0:T(8,128)(2,1)S(1)}, bf16[64,512]{1,0:T(8,128)(2,1)S(1)}, u32[]{:S(2)}, u32[]{:S(2)}) collective-permute-start(bf16[64,512]{1,0:T(8,128)(2,1)S(1)} %get-tuple-element.93), channel_id=1, source_target_pairs={{0,8},{1,9},{2,10},{3,11},{4,12},{5,13},{6,14},{7,15},{8,0},{9,1},... | collective-permute-start | bytes 196616 | tf_op jit(solution)/shard_map/ppermute | solution.py:474
  81.0 3.6 %collective-permute-start.9 = (bf16[64,512]{1,0:T(8,128)(2,1)S(1)}, bf16[64,512]{1,0:T(8,128)(2,1)S(1)}, u32[]{:S(2)}, u32[]{:S(2)}) collective-permute-start(bf16[64,512]{1,0:T(8,128)(2,1)S(1)} %get-tuple-element.94), channel_id=1, source_target_pairs={{0,24},{1,25},{2,26},{3,27},{4,28},{5,29},{6,30},{7,31},{8,16},{9,... | collective-permute-start | bytes 196616 | tf_op jit(solution)/shard_map/ppermute | solution.py:474
  84.6 5.1 %collective-permute-start.10 = (bf16[96,512]{1,0:T(8,128)(2,1)S(1)}, bf16[96,512]{1,0:T(8,128)(2,1)S(1)}, u32[]{:S(2)}, u32[]{:S(2)}) collective-permute-start(bf16[96,512]{1,0:T(8,128)(2,1)S(1)} %shard_map.116.mine_ref), channel_id=1, source_target_pairs={{0,32},{1,33},{2,34},{3,35},{4,36},{5,37},{6,38},{7,39},{8,40},{9,... | collective-permute-start | bytes 294920 | tf_op jit(solution)/shard_map/ppermute | solution.py:474
  89.8 6.2 %collective-permute-start.11 = (bf16[96,512]{1,0:T(8,128)(2,1)S(1)}, bf16[96,512]{1,0:T(8,128)(2,1)S(1)}, u32[]{:S(2)}, u32[]{:S(2)}) collective-permute-start(bf16[96,512]{1,0:T(8,128)(2,1)S(1)} %shard_map.118.mine_ref), channel_id=1, source_target_pairs={{0,96},{1,97},{2,98},{3,99},{4,100},{5,101},{6,102},{7,103},{8,104... | collective-permute-start | bytes 294920 | tf_op jit(solution)/shard_map/ppermute | solution.py:474
  96.0 6.6 %collective-permute-start.12 = (bf16[96,512]{1,0:T(8,128)(2,1)S(1)}, bf16[96,512]{1,0:T(8,128)(2,1)S(1)}, u32[]{:S(2)}, u32[]{:S(2)}) collective-permute-start(bf16[96,512]{1,0:T(8,128)(2,1)S(1)} %shard_map.120.mine_ref), channel_id=1, source_target_pairs={{0,224},{1,225},{2,226},{3,227},{4,228},{5,229},{6,230},{7,231},{8... | collective-permute-start | bytes 294920 | tf_op jit(solution)/shard_map/ppermute | solution.py:474
  103.0 15.8 %collective-permute-start.17 = (bf16[256,512]{1,0:T(8,128)(2,1)S(1)}, bf16[256,512]{1,0:T(8,128)(2,1)S(1)}, u32[]{:S(2)}, u32[]{:S(2)}) collective-permute-start(bf16[256,512]{1,0:T(8,128)(2,1)S(1)} %get-tuple-element.113), channel_id=1, source_target_pairs={{0,1},{1,2},{2,3},{3,4},{4,5},{5,6},{6,7},{7,8},{8,9},{9,10},{10,1... | collective-permute-start | bytes 786440 | tf_op jit(solution)/shard_map/ppermute | solution.py:453
  106.9 7.2 %collective-permute-start.18 = (bf16[48,512]{1,0:T(8,128)(2,1)S(1)}, bf16[48,512]{1,0:T(8,128)(2,1)S(1)}, u32[]{:S(2)}, u32[]{:S(2)}) collective-permute-start(bf16[48,512]{1,0:T(8,128)(2,1)S(1)} %get-tuple-element.114), channel_id=1, source_target_pairs={{0,17},{1,18},{2,19},{3,20},{4,21},{5,22},{6,23},{7,24},{8,25},{9,... | collective-permute-start | bytes 147464 | tf_op jit(solution)/shard_map/ppermute | solution.py:453
  108.1 10.7 %collective-permute-start.16 = (bf16[112,512]{1,0:T(8,128)(2,1)S(1)}, bf16[112,512]{1,0:T(8,128)(2,1)S(1)}, u32[]{:S(2)}, u32[]{:S(2)}) collective-permute-start(bf16[112,512]{1,0:T(8,128)(2,1)S(1)} %get-tuple-element.112), channel_id=1, source_target_pairs={{0,16},{1,17},{2,18},{3,19},{4,20},{5,21},{6,22},{7,23},{8,24},{9,... | collective-permute-start | bytes 344072 | tf_op jit(solution)/shard_map/ppermute | solution.py:453
  108.3 5.7 %collective-permute-start.15 = (bf16[96,512]{1,0:T(8,128)(2,1)S(1)}, bf16[96,512]{1,0:T(8,128)(2,1)S(1)}, u32[]{:S(2)}, u32[]{:S(2)}) collective-permute-start(bf16[96,512]{1,0:T(8,128)(2,1)S(1)} %shard_map.121.refs_1_), channel_id=1, source_target_pairs={{0,24},{1,25},{2,26},{3,27},{4,28},{5,29},{6,30},{7,31},{8,16},{9,... | collective-permute-start | bytes 294920 | tf_op jit(solution)/shard_map/ppermute | solution.py:474
  111.2 5.6 %collective-permute-start.14 = (bf16[96,512]{1,0:T(8,128)(2,1)S(1)}, bf16[96,512]{1,0:T(8,128)(2,1)S(1)}, u32[]{:S(2)}, u32[]{:S(2)}) collective-permute-start(bf16[96,512]{1,0:T(8,128)(2,1)S(1)} %shard_map.121.refs_1_), channel_id=1, source_target_pairs={{0,8},{1,9},{2,10},{3,11},{4,12},{5,13},{6,14},{7,15},{8,0},{9,1},... | collective-permute-start | bytes 294920 | tf_op jit(solution)/shard_map/ppermute | solution.py:474
  114.1 4.7 %collective-permute-start.13 = (bf16[96,512]{1,0:T(8,128)(2,1)S(1)}, bf16[96,512]{1,0:T(8,128)(2,1)S(1)}, u32[]{:S(2)}, u32[]{:S(2)}) collective-permute-start(bf16[96,512]{1,0:T(8,128)(2,1)S(1)} %shard_map.121.refs_1_), channel_id=1, source_target_pairs={{0,16},{1,17},{2,18},{3,19},{4,20},{5,21},{6,22},{7,23},{8,24},{9,... | collective-permute-start | bytes 294920 | tf_op jit(solution)/shard_map/ppermute | solution.py:474
  119.4 17.5 %collective-permute-start.21 = (bf16[288,512]{1,0:T(8,128)(2,1)S(1)}, bf16[288,512]{1,0:T(8,128)(2,1)S(1)}, u32[]{:S(2)}, u32[]{:S(2)}) collective-permute-start(bf16[288,512]{1,0:T(8,128)(2,1)S(1)} %shard_map.123.refs_1_), channel_id=1, source_target_pairs={{0,6},{1,7},{2,0},{3,1},{4,2},{5,3},{6,4},{7,5},{8,14},{9,15},{10,... | collective-permute-start | bytes 884744 | tf_op jit(solution)/shard_map/ppermute | solution.py:474
  124.3 12.6 %collective-permute-start.20 = (bf16[288,512]{1,0:T(8,128)(2,1)S(1)}, bf16[288,512]{1,0:T(8,128)(2,1)S(1)}, u32[]{:S(2)}, u32[]{:S(2)}) collective-permute-start(bf16[288,512]{1,0:T(8,128)(2,1)S(1)} %shard_map.123.refs_1_), channel_id=1, source_target_pairs={{0,4},{1,5},{2,6},{3,7},{4,0},{5,1},{6,2},{7,3},{8,12},{9,13},{10,... | collective-permute-start | bytes 884744 | tf_op jit(solution)/shard_map/ppermute | solution.py:474
  124.3 16.1 %collective-permute-start.19 = (bf16[288,512]{1,0:T(8,128)(2,1)S(1)}, bf16[288,512]{1,0:T(8,128)(2,1)S(1)}, u32[]{:S(2)}, u32[]{:S(2)}) collective-permute-start(bf16[288,512]{1,0:T(8,128)(2,1)S(1)} %shard_map.123.refs_1_), channel_id=1, source_target_pairs={{0,2},{1,3},{2,4},{3,5},{4,6},{5,7},{6,0},{7,1},{8,10},{9,11},{10,... | collective-permute-start | bytes 884744 | tf_op jit(solution)/shard_map/ppermute | solution.py:474
  141.0 3.3 %collective-permute-start.22 = (bf16[1056,512]{1,0:T(8,128)(2,1)S(1)}, bf16[1056,512]{1,0:T(8,128)(2,1)S(1)}, u32[]{:S(2)}, u32[]{:S(2)}) collective-permute-start(bf16[1056,512]{1,0:T(8,128)(2,1)S(1)} %shard_map.125.mine_ref), channel_id=1, source_target_pairs={{0,1},{1,0},{2,3},{3,2},{4,5},{5,4},{6,7},{7,6},{8,9},{9,8},{10,11... | collective-permute-start | bytes 3244040 | tf_op jit(solution)/shard_map/ppermute | solution.py:474

commit v4 on v3

--- a/solution.py
+++ b/solution.py
@@ -771,7 +771,10 @@
     parts = [mine] + [chips.x(mine, k) for k in range(1, nx)]
     parts, back = lax.optimization_barrier((parts, back))
     mine = gathered(X, nx, parts)
-    parts = [mine] + [chips.y(mine, k) for k in range(1, ny)]
+    ahead, behind = chips.y(mine, 1), chips.y(mine, ny - 1)
+    cut = mine.shape[0] // 2
+    far = jnp.concatenate([chips.y(ahead[:cut], 1), chips.y(behind[cut:], ny - 1)])
+    parts = [mine, ahead, far, behind]
 
     grad_tokens = call(
         lambda *refs: assemble_kernel(geo, *refs),

time: 147 us -> 148 us (level)
  starting transfers between devices: 44.1 us -> 49.4 us
  waiting for transfers between devices: 34.9 us -> 30.3 us
    ppermute x17 -> x18, starting transfers between devices: 25.6 us -> 30.9 us  [send(): return lax.ppermute(value, ('lat', 'lon'), pairs)]
    ppermute x17 -> x18, waiting for transfers between devices: 32 us -> 27.4 us  [send(): return lax.ppermute(value, ('lat', 'lon'), pairs)]
  transfers between devices with their start and end apart: 23 -> 24, of which waited for: 13 -> 14; matrix products, arithmetic and copies ran while one was open for 0% -> 0% of each run, Pallas kernels for 15% -> 15%
where the time goes in v4:
time: 148 us
  Pallas kernels  63.8 us (43%)
  starting transfers between devices  49.4 us (33%)
  waiting for transfers between devices  30.3 us (20%)
  local copies, waits for them, and re-layouts  3.15 us (2%)
    pallas_call x1, Pallas kernels, per_device(): pl.pallas_call(lambda *refs: main_kernel(geo, heads, *refs), in_specs=[sm...  32.8 us
    ppermute x18, starting transfers between devices, send(): return lax.ppermute(value, ('lat', 'lon'), pairs)  30.9 us
    ppermute x18, waiting for transfers between devices, send(): return lax.ppermute(value, ('lat', 'lon'), pairs)  27.4 us
    ppermute x6, starting transfers between devices, moved(): return lax.ppermute(value, ('lat', 'lon'), pairs)  18.5 us
    pallas_call x1, Pallas kernels, per_device(): call(lambda *refs: lookup_kernel(heads, *refs), [shape((heads, win, win),...  6.73 us
    pallas_call x2, Pallas kernels, layer_norm_back(): call(lambda *refs: back_kernel(geo, first, count, *refs), shape((count *...  6.19 us
    pallas_call x1, Pallas kernels, per_device(): call(lambda *refs: table_kernel(heads, *refs), shape((SMALL, width), F32)...  6.01 us
    unnamed x18, local copies, waits for them, and re-layouts  3.13 us
  transfers between devices with their start and end apart: 24, of which 14 were waited for; matrix products, arithmetic and copies ran while one was open for 0% of the time, Pallas kernels for 15%

profile of v4, /device:TPU:1, one launch (start us, length us, event | category | flops | bytes accessed | tf_op | source)
XLA Modules:
  0.0 147.8 jit_solution(16615622991235904579)
XLA Ops:
  0.7 2.7 %shard_map.110 = (bf16[224,512]{1,0:T(8,128)(2,1)}, bf16[512,512]{1,0:T(8,128)(2,1)}, bf16[80,512]{1,0:T(8,128)(2,1)}) custom-call(bf16[2,24,24,512]{3,2,1,0:T(8,128)(2,1)} %refs_0_.2, bf16[2,24,24,512]{3,2,1,0:T(8,128)(2,1)} %refs_1_.1), custom_call_target="tpu_custom_call" | custom-call | tf_op jit(solution)/shard_map/pallas_call | solution.py:611
  3.3 3.3 %collective-permute-start.1 = (bf16[512,512]{1,0:T(8,128)(2,1)}, bf16[512,512]{1,0:T(8,128)(2,1)}, u32[]{:S(2)}, u32[]{:S(2)}) collective-permute-start(bf16[512,512]{1,0:T(8,128)(2,1)} %get-tuple-element.70), channel_id=1, source_target_pairs={{0,15},{1,0},{2,1},{3,2},{4,3},{5,4},{6,5},{7,6},{8,7},{9,8},{10,9... | collective-permute-start | bytes 1572872 | tf_op jit(solution)/shard_map/ppermute | solution.py:453
  6.6 8.7 %collective-permute-start.2 = (bf16[80,512]{1,0:T(8,128)(2,1)}, bf16[80,512]{1,0:T(8,128)(2,1)}, u32[]{:S(2)}, u32[]{:S(2)}) collective-permute-start(bf16[80,512]{1,0:T(8,128)(2,1)} %get-tuple-element.71), channel_id=1, source_target_pairs={{0,255},{1,240},{2,241},{3,242},{4,243},{5,244},{6,245},{7,246},{8... | collective-permute-start | bytes 245768 | tf_op jit(solution)/shard_map/ppermute | solution.py:453
  15.3 1.2 collective-permute-start
  16.5 6.7 %shard_map.111 = (f32[8,144,144]{2,1,0:T(8,128)S(1)}, s32[144,144]{1,0:T(8,128)S(1)}) custom-call(s32[144,144]{1,0:T(8,128)S(1)} %copy-done.5, f32[8,759]{1,0:T(8,128)S(1)} %bitcast.18), custom_call_target="tpu_custom_call" | custom-call | flops 4000000000 | bytes 1000000 | tf_op jit(solution)/shard_map/pallas_call | solution.py:628
  23.2 0.7 copy-done.7
  24.0 1.4 copy-done.2
  25.4 1.0 copy-done.3
  26.4 32.8 %shard_map.112 = (bf16[1024,512]{1,0:T(8,128)(2,1)S(1)}, bf16[1024,512]{1,0:T(8,128)(2,1)S(1)}, f32[8,144,144]{2,1,0:T(8,128)S(1)}, bf16[1152,1536]{1,0:T(8,128)...) custom-call(s32[4]{0:T(128)S(1)} %pad_add_fusion.refs_0_.info_ref, ...), custom_call_target="tpu_custom_call" | custom-call | tf_op jit(solution)/shard_map/pallas_call | solution.py:648
  59.4 2.6 %collective-permute-done.3.recv_ref = bf16[1024,512]{1,0:T(8,128)(2,1)S(1)} collective-permute-done((bf16[1024,512]{1,0:T(8,128)(2,1)S(1)}, bf16[1024,512]{1,0:T(8,128)(2,1)S(1)}, u32[]{:S(2)}, u32[]{:S(2)}) %collective-permute-start.3) | collective-permute-done | bytes 1048608 | tf_op jit(solution)/shard_map/ppermute | solution.py:474
  62.0 0.8 shard_map.113
  62.9 2.5 %collective-permute-start.5 = (bf16[256,512]{1,0:T(8,128)(2,1)S(1)}, bf16[256,512]{1,0:T(8,128)(2,1)S(1)}, u32[]{:S(2)}, u32[]{:S(2)}) collective-permute-start(bf16[256,512]{1,0:T(8,128)(2,1)S(1)} %get-tuple-element.82), channel_id=1, source_target_pairs={{0,4},{1,5},{2,6},{3,7},{4,0},{5,1},{6,2},{7,3},{8,12},{9,13},{10,... | collective-permute-start | bytes 786440 | tf_op jit(solution)/shard_map/ppermute | solution.py:474
  65.6 6.0 %shard_map.114.refs_4_ = f32[16,512]{1,0:T(8,128)S(1)} custom-call(s32[144,144]{1,0:T(8,128)S(1)} %copy-done.8, f32[8,144,144]{2,1,0:T(8,128)S(1)} %get-tuple-element.85.refs_1_, f32[512,128]{1,0:T(8,128)S(1)} %get-tuple-element.86.refs_2_, f32[1,512]{1,0:T(1,128)S(1)} %bitcast.15), custom_call_target="tpu_custom_call" | custom-call | flops 3000000000 | bytes 1000000 | tf_op jit(solution)/shard_map/pallas_call | solution.py:698
  71.6 0.4 collective-permute-done.4.refs_2_
  72.0 5.3 %collective-permute-done.5.refs_3_ = bf16[256,512]{1,0:T(8,128)(2,1)S(1)} collective-permute-done((bf16[256,512]{1,0:T(8,128)(2,1)S(1)}, bf16[256,512]{1,0:T(8,128)(2,1)S(1)}, u32[]{:S(2)}, u32[]{:S(2)}) %collective-permute-start.5) | collective-permute-done | bytes 262176 | tf_op jit(solution)/shard_map/ppermute | solution.py:474
  77.4 0.4 collective-permute-done.6.refs_4_
  77.8 0.8 shard_map.115
  78.5 0.3 collective-permute-start.7
  78.8 2.1 %collective-permute-start.8 = (bf16[64,512]{1,0:T(8,128)(2,1)S(1)}, bf16[64,512]{1,0:T(8,128)(2,1)S(1)}, u32[]{:S(2)}, u32[]{:S(2)}) collective-permute-start(bf16[64,512]{1,0:T(8,128)(2,1)S(1)} %get-tuple-element.93), channel_id=1, source_target_pairs={{0,8},{1,9},{2,10},{3,11},{4,12},{5,13},{6,14},{7,15},{8,0},{9,1},... | collective-permute-start | bytes 196616 | tf_op jit(solution)/shard_map/ppermute | solution.py:474
  81.0 2.0 %collective-permute-start.9 = (bf16[64,512]{1,0:T(8,128)(2,1)S(1)}, bf16[64,512]{1,0:T(8,128)(2,1)S(1)}, u32[]{:S(2)}, u32[]{:S(2)}) collective-permute-start(bf16[64,512]{1,0:T(8,128)(2,1)S(1)} %get-tuple-element.94), channel_id=1, source_target_pairs={{0,24},{1,25},{2,26},{3,27},{4,28},{5,29},{6,30},{7,31},{8,16},{9,... | collective-permute-start | bytes 196616 | tf_op jit(solution)/shard_map/ppermute | solution.py:474
  82.9 0.7 collective-permute-done.7.refs_1_
  83.7 0.9 collective-permute-done.9.refs_3_
  84.6 2.0 %collective-permute-start.10 = (bf16[96,512]{1,0:T(8,128)(2,1)S(1)}, bf16[96,512]{1,0:T(8,128)(2,1)S(1)}, u32[]{:S(2)}, u32[]{:S(2)}) collective-permute-start(bf16[96,512]{1,0:T(8,128)(2,1)S(1)} %shard_map.116.mine_ref), channel_id=1, source_target_pairs={{0,32},{1,33},{2,34},{3,35},{4,36},{5,37},{6,38},{7,39},{8,40},{9,... | collective-permute-start | bytes 294920 | tf_op jit(solution)/shard_map/ppermute | solution.py:474
  86.6 3.1 %shard_map.117.refs_0_ = bf16[576,512]{1,0:T(8,128)(2,1)S(1)} custom-call(bf16[1152,1536]{1,0:T(8,128)(2,1)S(1)} %get-tuple-element.104.refs_0_, f32[1152,512]{1,0:T(8,128)S(1)} %get-tuple-element.99.refs_1_, f32[1152,128]{1,0:T(8,128)S(1)} %get-tuple-element.100.refs_2_, bf16[1152,512]{1,0:T(8,128)(2,1)S(1)} %get-tuple-element.101.refs_3_, ...), custom_call_target="tpu_custom_call" | custom-call | flops 3000000000 | bytes 10000000 | tf_op jit(solution)/shard_map/pallas_call | solution.py:726
  89.7 3.1 %collective-permute-start.11 = (bf16[96,512]{1,0:T(8,128)(2,1)S(1)}, bf16[96,512]{1,0:T(8,128)(2,1)S(1)}, u32[]{:S(2)}, u32[]{:S(2)}) collective-permute-start(bf16[96,512]{1,0:T(8,128)(2,1)S(1)} %shard_map.118.mine_ref), channel_id=1, source_target_pairs={{0,96},{1,97},{2,98},{3,99},{4,100},{5,101},{6,102},{7,103},{8,104... | collective-permute-start | bytes 294920 | tf_op jit(solution)/shard_map/ppermute | solution.py:474
  92.9 3.1 %shard_map.119.refs_1_ = bf16[576,512]{1,0:T(8,128)(2,1)S(1)} custom-call(bf16[1152,1536]{1,0:T(8,128)(2,1)S(1)} %get-tuple-element.104.refs_0_, f32[1152,512]{1,0:T(8,128)S(1)} %get-tuple-element.99.refs_1_, f32[1152,128]{1,0:T(8,128)S(1)} %get-tuple-element.100.refs_2_, bf16[1152,512]{1,0:T(8,128)(2,1)S(1)} %get-tuple-element.101.refs_3_, ...), custom_call_target="tpu_custom_call" | custom-call | flops 3000000000 | bytes 10000000 | tf_op jit(solution)/shard_map/pallas_call | solution.py:726
  96.0 3.8 %collective-permute-start.12 = (bf16[96,512]{1,0:T(8,128)(2,1)S(1)}, bf16[96,512]{1,0:T(8,128)(2,1)S(1)}, u32[]{:S(2)}, u32[]{:S(2)}) collective-permute-start(bf16[96,512]{1,0:T(8,128)(2,1)S(1)} %shard_map.120.mine_ref), channel_id=1, source_target_pairs={{0,224},{1,225},{2,226},{3,227},{4,228},{5,229},{6,230},{7,231},{8... | collective-permute-start | bytes 294920 | tf_op jit(solution)/shard_map/ppermute | solution.py:474
  99.9 2.7 %collective-permute-done.12.got_ref = bf16[96,512]{1,0:T(8,128)(2,1)S(1)} collective-permute-done((bf16[96,512]{1,0:T(8,128)(2,1)S(1)}, bf16[96,512]{1,0:T(8,128)(2,1)S(1)}, u32[]{:S(2)}, u32[]{:S(2)}) %collective-permute-start.12) | collective-permute-done | bytes 98336 | tf_op jit(solution)/shard_map/ppermute | solution.py:474
  102.6 0.3 shard_map.122
  103.0 3.9 %collective-permute-start.17 = (bf16[256,512]{1,0:T(8,128)(2,1)S(1)}, bf16[256,512]{1,0:T(8,128)(2,1)S(1)}, u32[]{:S(2)}, u32[]{:S(2)}) collective-permute-start(bf16[256,512]{1,0:T(8,128)(2,1)S(1)} %get-tuple-element.113), channel_id=1, source_target_pairs={{0,1},{1,2},{2,3},{3,4},{4,5},{5,6},{6,7},{7,8},{8,9},{9,10},{10,1... | collective-permute-start | bytes 786440 | tf_op jit(solution)/shard_map/ppermute | solution.py:453
  106.9 1.2 collective-permute-start.18
  108.1 0.2 collective-permute-start.16
  108.3 2.8 %collective-permute-start.15 = (bf16[96,512]{1,0:T(8,128)(2,1)S(1)}, bf16[96,512]{1,0:T(8,128)(2,1)S(1)}, u32[]{:S(2)}, u32[]{:S(2)}) collective-permute-start(bf16[96,512]{1,0:T(8,128)(2,1)S(1)} %shard_map.121.refs_1_), channel_id=1, source_target_pairs={{0,24},{1,25},{2,26},{3,27},{4,28},{5,29},{6,30},{7,31},{8,16},{9,... | collective-permute-start | bytes 294920 | tf_op jit(solution)/shard_map/ppermute | solution.py:474
  111.2 2.8 %collective-permute-done.18.refs_4_ = bf16[48,512]{1,0:T(8,128)(2,1)S(1)} collective-permute-done((bf16[48,512]{1,0:T(8,128)(2,1)S(1)}, bf16[48,512]{1,0:T(8,128)(2,1)S(1)}, u32[]{:S(2)}, u32[]{:S(2)}) %collective-permute-start.18) | collective-permute-done | bytes 49184 | tf_op jit(solution)/shard_map/ppermute | solution.py:453
  114.0 2.8 %collective-permute-done.14.refs_3_ = bf16[96,512]{1,0:T(8,128)(2,1)S(1)} collective-permute-done((bf16[96,512]{1,0:T(8,128)(2,1)S(1)}, bf16[96,512]{1,0:T(8,128)(2,1)S(1)}, u32[]{:S(2)}, u32[]{:S(2)}) %collective-permute-start.14) | collective-permute-done | bytes 98336 | tf_op jit(solution)/shard_map/ppermute | solution.py:474
  116.8 2.0 %collective-permute-done.13.refs_2_ = bf16[96,512]{1,0:T(8,128)(2,1)S(1)} collective-permute-done((bf16[96,512]{1,0:T(8,128)(2,1)S(1)}, bf16[96,512]{1,0:T(8,128)(2,1)S(1)}, u32[]{:S(2)}, u32[]{:S(2)}) %collective-permute-start.13) | collective-permute-done | bytes 98336 | tf_op jit(solution)/shard_map/ppermute | solution.py:474
  118.8 0.6 shard_map.123.refs_1_
  119.4 4.9 %collective-permute-start.21 = (bf16[288,512]{1,0:T(8,128)(2,1)S(1)}, bf16[288,512]{1,0:T(8,128)(2,1)S(1)}, u32[]{:S(2)}, u32[]{:S(2)}) collective-permute-start(bf16[288,512]{1,0:T(8,128)(2,1)S(1)} %shard_map.123.refs_1_), channel_id=1, source_target_pairs={{0,6},{1,7},{2,0},{3,1},{4,2},{5,3},{6,4},{7,5},{8,14},{9,15},{10,... | collective-permute-start | bytes 884744 | tf_op jit(solution)/shard_map/ppermute | solution.py:474
  124.3 5.6 %collective-permute-done.21.refs_4_ = bf16[288,512]{1,0:T(8,128)(2,1)S(1)} collective-permute-done((bf16[288,512]{1,0:T(8,128)(2,1)S(1)}, bf16[288,512]{1,0:T(8,128)(2,1)S(1)}, u32[]{:S(2)}, u32[]{:S(2)}) %collective-permute-start.21) | collective-permute-done | bytes 294944 | tf_op jit(solution)/shard_map/ppermute | solution.py:474
  129.9 3.7 %collective-permute-start.22 = (bf16[144,512]{1,0:T(8,128)(2,1)S(1)}, bf16[144,512]{1,0:T(8,128)(2,1)S(1)}, u32[]{:S(2)}, u32[]{:S(2)}) collective-permute-start(bf16[144,512]{1,0:T(8,128)(2,1)S(1)} %slice.13), channel_id=1, source_target_pairs={{0,6},{1,7},{2,0},{3,1},{4,2},{5,3},{6,4},{7,5},{8,14},{9,15},{10,... | collective-permute-start | bytes 442376 | tf_op jit(solution)/shard_map/ppermute | solution.py:474
  133.7 1.7 %shard_map.124 = bf16[1152,512]{1,0:T(8,128)(2,1)} custom-call(bf16[576,512]{1,0:T(8,128)(2,1)S(1)} %shard_map.117.refs_0_, bf16[576,512]{1,0:T(8,128)(2,1)S(1)} %shard_map.119.refs_1_, bf16[112,512]{1,0:T(8,128)(2,1)S(1)} %collective-permute-done.16.refs_2_, bf16[256,512]{1,0:T(8,128)(2,1)S(1)} %collective-permute-done.17.refs_3_, ...), custom_call_target="tpu_custom_call" | custom-call | tf_op jit(solution)/shard_map/pallas_call | solution.py:779
  135.4 0.3 collective-permute-done.22
  135.7 3.2 %collective-permute-done.20 = bf16[144,512]{1,0:T(8,128)(2,1)S(1)} collective-permute-done((bf16[144,512]{1,0:T(8,128)(2,1)S(1)}, bf16[144,512]{1,0:T(8,128)(2,1)S(1)}, u32[]{:S(2)}, u32[]{:S(2)}) %collective-permute-start.20) | collective-permute-done | bytes 147488 | tf_op jit(solution)/shard_map/ppermute | solution.py:474
  138.9 0.6 shard_map.125.mine_ref
  139.6 3.1 %collective-permute-start.23 = (bf16[1056,512]{1,0:T(8,128)(2,1)S(1)}, bf16[1056,512]{1,0:T(8,128)(2,1)S(1)}, u32[]{:S(2)}, u32[]{:S(2)}) collective-permute-start(bf16[1056,512]{1,0:T(8,128)(2,1)S(1)} %shard_map.125.mine_ref), channel_id=1, source_target_pairs={{0,1},{1,0},{2,3},{3,2},{4,5},{5,4},{6,7},{7,6},{8,9},{9,8},{10,11... | collective-permute-start | bytes 3244040 | tf_op jit(solution)/shard_map/ppermute | solution.py:474
  142.7 1.9 %shard_map.126 = (f32[512,1536]{1,0:T(8,128)}, f32[512,512]{1,0:T(8,128)}) custom-call(s32[4]{0:T(128)S(1)} %pad_add_fusion.refs_0_.info_ref, bf16[1056,512]{1,0:T(8,128)(2,1)S(1)} %shard_map.125.mine_ref), custom_call_target="tpu_custom_call" | custom-call | tf_op jit(solution)/shard_map/pallas_call | solution.py:799
  144.6 0.4 collective-permute-done.23.got_ref
  145.0 2.5 %shard_map.127 = (f32[512,1536]{1,0:T(8,128)}, f32[512,512]{1,0:T(8,128)}, f32[8,768]{1,0:T(8,128)}, f32[1,512]{1,0:T(1,128)}) custom-call(s32[4]{0:T(128)S(1)} %pad_add_fusion.refs_0_.info_ref, bf16[1056,512]{1,0:T(8,128)(2,1)S(1)} %shard_map.125.mine_ref, ...), custom_call_target="tpu_custom_call", output_to_operand_aliasing={{0}: (3, {}), {1}: (4, {})} | custom-call | tf_op jit(solution)/shard_map/pallas_call | solution.py:807
  (40 shorter events, 0.8 us)
Async XLA Ops:
  0.6 15.8 %copy-start.5 = (s32[144,144]{1,0:T(8,128)S(1)}, s32[144,144]{1,0:T(8,128)}, u32[]{:S(2)}) copy-start(s32[144,144]{1,0:T(8,128)} %refs_0_.3) | copy-start | bytes 248836
  0.6 15.8 %copy-start.6 = (f32[759,8]{0,1:T(8,128)S(1)}, f32[759,8]{0,1:T(8,128)}, u32[]{:S(2)}) copy-start(f32[759,8]{0,1:T(8,128)} %param.11) | copy-start | bytes 72868
  3.3 20.7 %collective-permute-start.1 = (bf16[512,512]{1,0:T(8,128)(2,1)}, bf16[512,512]{1,0:T(8,128)(2,1)}, u32[]{:S(2)}, u32[]{:S(2)}) collective-permute-start(bf16[512,512]{1,0:T(8,128)(2,1)} %get-tuple-element.70), channel_id=1, source_target_pairs={{0,15},{1,0},{2,1},{3,2},{4,3},{5,4},{6,5},{7,6},{8,7},{9,8},{10,9... | collective-permute-start | bytes 1572872 | tf_op jit(solution)/shard_map/ppermute | solution.py:453
  6.6 17.3 %collective-permute-start.2 = (bf16[80,512]{1,0:T(8,128)(2,1)}, bf16[80,512]{1,0:T(8,128)(2,1)}, u32[]{:S(2)}, u32[]{:S(2)}) collective-permute-start(bf16[80,512]{1,0:T(8,128)(2,1)} %get-tuple-element.71), channel_id=1, source_target_pairs={{0,255},{1,240},{2,241},{3,242},{4,243},{5,244},{6,245},{7,246},{8... | collective-permute-start | bytes 245768 | tf_op jit(solution)/shard_map/ppermute | solution.py:453
  15.3 8.7 %collective-permute-start = (bf16[224,512]{1,0:T(8,128)(2,1)}, bf16[224,512]{1,0:T(8,128)(2,1)}, u32[]{:S(2)}, u32[]{:S(2)}) collective-permute-start(bf16[224,512]{1,0:T(8,128)(2,1)} %get-tuple-element.69), channel_id=1, source_target_pairs={{0,240},{1,241},{2,242},{3,243},{4,244},{5,245},{6,246},{7,247},{8... | collective-permute-start | bytes 688136 | tf_op jit(solution)/shard_map/ppermute | solution.py:453
  16.5 7.5 %copy-start = (bf16[2,24,24,512]{3,2,1,0:T(8,128)(2,1)S(1)}, bf16[2,24,24,512]{3,2,1,0:T(8,128)(2,1)}, u32[]{:S(2)}) copy-start(bf16[2,24,24,512]{3,2,1,0:T(8,128)(2,1)} %refs_0_.2) | copy-start | bytes 3538948
  16.5 7.5 %copy-start.1 = (bf16[2,24,24,512]{3,2,1,0:T(8,128)(2,1)S(1)}, bf16[2,24,24,512]{3,2,1,0:T(8,128)(2,1)}, u32[]{:S(2)}) copy-start(bf16[2,24,24,512]{3,2,1,0:T(8,128)(2,1)} %refs_1_.1) | copy-start | bytes 3538948
  16.5 7.5 %copy-start.4 = (f32[512]{0:T(512)S(1)}, f32[512]{0:T(512)}, u32[]{:S(2)}) copy-start(f32[512]{0:T(512)} %param.8) | copy-start | bytes 6148
  23.2 0.7 copy-start.7
  24.0 1.4 copy-start.2
  25.4 1.0 copy-start.3
  59.3 6.3 %copy-start.8 = (s32[144,144]{1,0:T(8,128)S(1)}, s32[144,144]{1,0:T(8,128)}, u32[]{:S(2)}) copy-start(s32[144,144]{1,0:T(8,128)} %copy-done.7) | copy-start | bytes 248836
  59.3 2.7 %collective-permute-start.3 = (bf16[1024,512]{1,0:T(8,128)(2,1)S(1)}, bf16[1024,512]{1,0:T(8,128)(2,1)S(1)}, u32[]{:S(2)}, u32[]{:S(2)}) collective-permute-start(bf16[1024,512]{1,0:T(8,128)(2,1)S(1)} %get-tuple-element.74), channel_id=1, source_target_pairs={{0,1},{1,0},{2,3},{3,2},{4,5},{5,4},{6,7},{7,6},{8,9},{9,8},{10,11... | collective-permute-start | bytes 3145736 | tf_op jit(solution)/shard_map/ppermute | solution.py:474
  62.8 9.2 %collective-permute-start.4 = (bf16[256,512]{1,0:T(8,128)(2,1)S(1)}, bf16[256,512]{1,0:T(8,128)(2,1)S(1)}, u32[]{:S(2)}, u32[]{:S(2)}) collective-permute-start(bf16[256,512]{1,0:T(8,128)(2,1)S(1)} %get-tuple-element.81), channel_id=1, source_target_pairs={{0,2},{1,3},{2,4},{3,5},{4,6},{5,7},{6,0},{7,1},{8,10},{9,11},{10,... | collective-permute-start | bytes 786440 | tf_op jit(solution)/shard_map/ppermute | solution.py:474
  62.9 14.5 %collective-permute-start.5 = (bf16[256,512]{1,0:T(8,128)(2,1)S(1)}, bf16[256,512]{1,0:T(8,128)(2,1)S(1)}, u32[]{:S(2)}, u32[]{:S(2)}) collective-permute-start(bf16[256,512]{1,0:T(8,128)(2,1)S(1)} %get-tuple-element.82), channel_id=1, source_target_pairs={{0,4},{1,5},{2,6},{3,7},{4,0},{5,1},{6,2},{7,3},{8,12},{9,13},{10,... | collective-permute-start | bytes 786440 | tf_op jit(solution)/shard_map/ppermute | solution.py:474
  65.4 12.4 %collective-permute-start.6 = (bf16[256,512]{1,0:T(8,128)(2,1)S(1)}, bf16[256,512]{1,0:T(8,128)(2,1)S(1)}, u32[]{:S(2)}, u32[]{:S(2)}) collective-permute-start(bf16[256,512]{1,0:T(8,128)(2,1)S(1)} %get-tuple-element.83), channel_id=1, source_target_pairs={{0,6},{1,7},{2,0},{3,1},{4,2},{5,3},{6,4},{7,5},{8,14},{9,15},{10,... | collective-permute-start | bytes 786440 | tf_op jit(solution)/shard_map/ppermute | solution.py:474
  78.5 5.1 %collective-permute-start.7 = (bf16[64,512]{1,0:T(8,128)(2,1)S(1)}, bf16[64,512]{1,0:T(8,128)(2,1)S(1)}, u32[]{:S(2)}, u32[]{:S(2)}) collective-permute-start(bf16[64,512]{1,0:T(8,128)(2,1)S(1)} %get-tuple-element.92), channel_id=1, source_target_pairs={{0,16},{1,17},{2,18},{3,19},{4,20},{5,21},{6,22},{7,23},{8,24},{9,... | collective-permute-start | bytes 196616 | tf_op jit(solution)/shard_map/ppermute | solution.py:474
  78.8 4.8 %collective-permute-start.8 = (bf16[64,512]{1,0:T(8,128)(2,1)S(1)}, bf16[64,512]{1,0:T(8,128)(2,1)S(1)}, u32[]{:S(2)}, u32[]{:S(2)}) collective-permute-start(bf16[64,512]{1,0:T(8,128)(2,1)S(1)} %get-tuple-element.93), channel_id=1, source_target_pairs={{0,8},{1,9},{2,10},{3,11},{4,12},{5,13},{6,14},{7,15},{8,0},{9,1},... | collective-permute-start | bytes 196616 | tf_op jit(solution)/shard_map/ppermute | solution.py:474
  81.0 3.6 %collective-permute-start.9 = (bf16[64,512]{1,0:T(8,128)(2,1)S(1)}, bf16[64,512]{1,0:T(8,128)(2,1)S(1)}, u32[]{:S(2)}, u32[]{:S(2)}) collective-permute-start(bf16[64,512]{1,0:T(8,128)(2,1)S(1)} %get-tuple-element.94), channel_id=1, source_target_pairs={{0,24},{1,25},{2,26},{3,27},{4,28},{5,29},{6,30},{7,31},{8,16},{9,... | collective-permute-start | bytes 196616 | tf_op jit(solution)/shard_map/ppermute | solution.py:474
  84.6 5.1 %collective-permute-start.10 = (bf16[96,512]{1,0:T(8,128)(2,1)S(1)}, bf16[96,512]{1,0:T(8,128)(2,1)S(1)}, u32[]{:S(2)}, u32[]{:S(2)}) collective-permute-start(bf16[96,512]{1,0:T(8,128)(2,1)S(1)} %shard_map.116.mine_ref), channel_id=1, source_target_pairs={{0,32},{1,33},{2,34},{3,35},{4,36},{5,37},{6,38},{7,39},{8,40},{9,... | collective-permute-start | bytes 294920 | tf_op jit(solution)/shard_map/ppermute | solution.py:474
  89.7 6.3 %collective-permute-start.11 = (bf16[96,512]{1,0:T(8,128)(2,1)S(1)}, bf16[96,512]{1,0:T(8,128)(2,1)S(1)}, u32[]{:S(2)}, u32[]{:S(2)}) collective-permute-start(bf16[96,512]{1,0:T(8,128)(2,1)S(1)} %shard_map.118.mine_ref), channel_id=1, source_target_pairs={{0,96},{1,97},{2,98},{3,99},{4,100},{5,101},{6,102},{7,103},{8,104... | collective-permute-start | bytes 294920 | tf_op jit(solution)/shard_map/ppermute | solution.py:474
  96.0 6.6 %collective-permute-start.12 = (bf16[96,512]{1,0:T(8,128)(2,1)S(1)}, bf16[96,512]{1,0:T(8,128)(2,1)S(1)}, u32[]{:S(2)}, u32[]{:S(2)}) collective-permute-start(bf16[96,512]{1,0:T(8,128)(2,1)S(1)} %shard_map.120.mine_ref), channel_id=1, source_target_pairs={{0,224},{1,225},{2,226},{3,227},{4,228},{5,229},{6,230},{7,231},{8... | collective-permute-start | bytes 294920 | tf_op jit(solution)/shard_map/ppermute | solution.py:474
  103.0 15.8 %collective-permute-start.17 = (bf16[256,512]{1,0:T(8,128)(2,1)S(1)}, bf16[256,512]{1,0:T(8,128)(2,1)S(1)}, u32[]{:S(2)}, u32[]{:S(2)}) collective-permute-start(bf16[256,512]{1,0:T(8,128)(2,1)S(1)} %get-tuple-element.113), channel_id=1, source_target_pairs={{0,1},{1,2},{2,3},{3,4},{4,5},{5,6},{6,7},{7,8},{8,9},{9,10},{10,1... | collective-permute-start | bytes 786440 | tf_op jit(solution)/shard_map/ppermute | solution.py:453
  106.9 7.1 %collective-permute-start.18 = (bf16[48,512]{1,0:T(8,128)(2,1)S(1)}, bf16[48,512]{1,0:T(8,128)(2,1)S(1)}, u32[]{:S(2)}, u32[]{:S(2)}) collective-permute-start(bf16[48,512]{1,0:T(8,128)(2,1)S(1)} %get-tuple-element.114), channel_id=1, source_target_pairs={{0,17},{1,18},{2,19},{3,20},{4,21},{5,22},{6,23},{7,24},{8,25},{9,... | collective-permute-start | bytes 147464 | tf_op jit(solution)/shard_map/ppermute | solution.py:453
  108.1 10.7 %collective-permute-start.16 = (bf16[112,512]{1,0:T(8,128)(2,1)S(1)}, bf16[112,512]{1,0:T(8,128)(2,1)S(1)}, u32[]{:S(2)}, u32[]{:S(2)}) collective-permute-start(bf16[112,512]{1,0:T(8,128)(2,1)S(1)} %get-tuple-element.112), channel_id=1, source_target_pairs={{0,16},{1,17},{2,18},{3,19},{4,20},{5,21},{6,22},{7,23},{8,24},{9,... | collective-permute-start | bytes 344072 | tf_op jit(solution)/shard_map/ppermute | solution.py:453
  108.3 5.7 %collective-permute-start.15 = (bf16[96,512]{1,0:T(8,128)(2,1)S(1)}, bf16[96,512]{1,0:T(8,128)(2,1)S(1)}, u32[]{:S(2)}, u32[]{:S(2)}) collective-permute-start(bf16[96,512]{1,0:T(8,128)(2,1)S(1)} %shard_map.121.refs_1_), channel_id=1, source_target_pairs={{0,24},{1,25},{2,26},{3,27},{4,28},{5,29},{6,30},{7,31},{8,16},{9,... | collective-permute-start | bytes 294920 | tf_op jit(solution)/shard_map/ppermute | solution.py:474
  111.2 5.6 %collective-permute-start.14 = (bf16[96,512]{1,0:T(8,128)(2,1)S(1)}, bf16[96,512]{1,0:T(8,128)(2,1)S(1)}, u32[]{:S(2)}, u32[]{:S(2)}) collective-permute-start(bf16[96,512]{1,0:T(8,128)(2,1)S(1)} %shard_map.121.refs_1_), channel_id=1, source_target_pairs={{0,8},{1,9},{2,10},{3,11},{4,12},{5,13},{6,14},{7,15},{8,0},{9,1},... | collective-permute-start | bytes 294920 | tf_op jit(solution)/shard_map/ppermute | solution.py:474
  114.0 4.7 %collective-permute-start.13 = (bf16[96,512]{1,0:T(8,128)(2,1)S(1)}, bf16[96,512]{1,0:T(8,128)(2,1)S(1)}, u32[]{:S(2)}, u32[]{:S(2)}) collective-permute-start(bf16[96,512]{1,0:T(8,128)(2,1)S(1)} %shard_map.121.refs_1_), channel_id=1, source_target_pairs={{0,16},{1,17},{2,18},{3,19},{4,20},{5,21},{6,22},{7,23},{8,24},{9,... | collective-permute-start | bytes 294920 | tf_op jit(solution)/shard_map/ppermute | solution.py:474
  119.4 10.5 %collective-permute-start.21 = (bf16[288,512]{1,0:T(8,128)(2,1)S(1)}, bf16[288,512]{1,0:T(8,128)(2,1)S(1)}, u32[]{:S(2)}, u32[]{:S(2)}) collective-permute-start(bf16[288,512]{1,0:T(8,128)(2,1)S(1)} %shard_map.123.refs_1_), channel_id=1, source_target_pairs={{0,6},{1,7},{2,0},{3,1},{4,2},{5,3},{6,4},{7,5},{8,14},{9,15},{10,... | collective-permute-start | bytes 884744 | tf_op jit(solution)/shard_map/ppermute | solution.py:474
  124.3 9.3 %collective-permute-start.19 = (bf16[288,512]{1,0:T(8,128)(2,1)S(1)}, bf16[288,512]{1,0:T(8,128)(2,1)S(1)}, u32[]{:S(2)}, u32[]{:S(2)}) collective-permute-start(bf16[288,512]{1,0:T(8,128)(2,1)S(1)} %shard_map.123.refs_1_), channel_id=1, source_target_pairs={{0,2},{1,3},{2,4},{3,5},{4,6},{5,7},{6,0},{7,1},{8,10},{9,11},{10,... | collective-permute-start | bytes 884744 | tf_op jit(solution)/shard_map/ppermute | solution.py:474
  129.9 5.8 %collective-permute-start.22 = (bf16[144,512]{1,0:T(8,128)(2,1)S(1)}, bf16[144,512]{1,0:T(8,128)(2,1)S(1)}, u32[]{:S(2)}, u32[]{:S(2)}) collective-permute-start(bf16[144,512]{1,0:T(8,128)(2,1)S(1)} %slice.13), channel_id=1, source_target_pairs={{0,6},{1,7},{2,0},{3,1},{4,2},{5,3},{6,4},{7,5},{8,14},{9,15},{10,... | collective-permute-start | bytes 442376 | tf_op jit(solution)/shard_map/ppermute | solution.py:474
  133.6 5.3 %collective-permute-start.20 = (bf16[144,512]{1,0:T(8,128)(2,1)S(1)}, bf16[144,512]{1,0:T(8,128)(2,1)S(1)}, u32[]{:S(2)}, u32[]{:S(2)}) collective-permute-start(bf16[144,512]{1,0:T(8,128)(2,1)S(1)} %slice.12), channel_id=1, source_target_pairs={{0,2},{1,3},{2,4},{3,5},{4,6},{5,7},{6,0},{7,1},{8,10},{9,11},{10,... | collective-permute-start | bytes 442376 | tf_op jit(solution)/shard_map/ppermute | solution.py:474
  139.6 5.5 %collective-permute-start.23 = (bf16[1056,512]{1,0:T(8,128)(2,1)S(1)}, bf16[1056,512]{1,0:T(8,128)(2,1)S(1)}, u32[]{:S(2)}, u32[]{:S(2)}) collective-permute-start(bf16[1056,512]{1,0:T(8,128)(2,1)S(1)} %shard_map.125.mine_ref), channel_id=1, source_target_pairs={{0,1},{1,0},{2,3},{3,2},{4,5},{5,4},{6,7},{7,6},{8,9},{9,8},{10,11... | collective-permute-start | bytes 3244040 | tf_op jit(solution)/shard_map/ppermute | solution.py:474
